TPU v7x, 32 devices: a whole 2x2x4 slice. The times are simulated.
32 devices in a mesh: lon: 16 (over z, y, core), lat: 2 (over x).
Axes of the slice: x: 2, y: 2, z: 4, core: 2. Of those that a mesh axis runs over, the one named last changes fastest.
Arguments:
- features: bfloat16 [20, 224, 768], P('lat', 'lon'), may hold values from -6 to 6
- cotangent: bfloat16 [20, 224, 768], P('lat', 'lon'), may hold values from -6 to 6
- weight_in: float32 [2, 8, 96, 96], replicated, may hold values from -0.4375 to 0.4375
- bias_in: float32 [2, 8, 96], replicated, may hold values from -4 to 4
- weight_out: float32 [2, 8, 96, 96], replicated, may hold values from -0.4375 to 0.4375
Outputs:
- grad_features: bfloat16 [20, 224, 768], P('lat', 'lon')
- grad_weight_in: float32 [2, 8, 96, 96], replicated
- grad_bias_in: float32 [2, 8, 96], replicated
- grad_weight_out: float32 [2, 8, 96, 96], replicated
All inputs are finite; a program needn't handle non-finite values.
Results may differ from a plain program's by a relative error of at most 0.001.
Values may be sent and summed in bfloat16 or wider, within the bound.
No kernel may reach another device: no remote copies, remote signals or barrier semaphores. Data moves between devices by JAX's collectives and lax.ppermute only.
A program may use at most 128 MiB of HBM per device.

v0:
```python
import functools
import math

import jax
import jax.numpy as jnp
import ml_dtypes
import numpy as np
from jax import lax
from jax.experimental import pallas as pl
from jax.experimental.pallas import tpu as pltpu
from jax.sharding import PartitionSpec as P

MODE_DEV = 4
PAD = 16
HALF = PAD // 2
POWER = 13.0
TOP = 2.0**9
VMEM = 40 * 2**20

root_half = math.sqrt(0.5)
density_norm = 1.0 / math.sqrt(2.0 * math.pi)


def halves(table):
    table = table.astype(np.float32)
    high = table.astype(ml_dtypes.bfloat16)
    low = (table - high.astype(np.float32)).astype(ml_dtypes.bfloat16)
    return high, low


def lon_table(columns, mode_count):
    product = np.arange(columns)[:, None] * np.arange(mode_count)[None, :] % columns
    angle = product * (2.0 * math.pi / columns)
    stacked = np.stack([np.cos(angle), -np.sin(angle)], axis=2) * columns**-0.5
    return stacked.reshape(columns, 2 * mode_count)


def lon_tables(blocks, inner, cols):
    modes = MODE_DEV * blocks
    table = lon_table(blocks * inner * cols, modes * inner)
    table = table.reshape(blocks, inner, cols, inner, 2 * modes)
    table = np.pad(table, ((0, 0), (0, 0), (0, PAD - cols), (0, 0), (0, 0)))
    forward = table.transpose(3, 1, 4, 0, 2).reshape(inner, inner, 2 * modes, blocks * PAD)
    split = table.reshape(blocks, inner, 2, HALF, inner, 2 * modes)
    synth = split.transpose(1, 4, 2, 0, 3, 5).reshape(inner, inner, 2 * blocks * HALF, 2 * modes)
    high, low = halves(forward)
    return np.concatenate([high, low], axis=2), *halves(synth)


def lat_table(rows, lat_count, group):
    total = rows * lat_count
    product = np.arange(total)[:, None] * np.arange(total)[None, :] % total
    angle = product * (2.0 * math.pi / total)
    c, s = np.cos(angle), np.sin(angle)
    basis = np.stack([np.stack([c, s], -1), np.stack([-s, c], -1)], axis=0) * total**-0.5
    basis = basis.reshape(2, total, lat_count, rows // 2, 2, 2).transpose(0, 1, 2, 4, 3, 5)
    size = 2 * total * group
    return np.einsum("akxhqb,mn->akmxhqnb", basis, np.eye(group)).reshape(size, size)


def split(values):
    high = values.astype(jnp.bfloat16)
    return high, (values - high.astype(jnp.float32)).astype(jnp.bfloat16)


def dot(left, right, dims=((1,), (0,))):
    return lax.dot_general(left, right, (dims, ((), ())), preferred_element_type=jnp.float32)


def dot3(left, right, dims=((1,), (0,))):
    return dot(left[0], right[0], dims) + (dot(left[0], right[1], dims) + dot(left[1], right[0], dims))


def scaled(values, top):
    level = jnp.maximum(top, 1e-30).astype(jnp.bfloat16).astype(jnp.float32)
    return values * (TOP / level), level


def encode(values):
    square = values * values
    fourth = square * square
    return (values * fourth * (fourth * fourth)).astype(jnp.bfloat16)


def decode(coded):
    coded = coded.astype(jnp.float32)
    size = jnp.abs(coded)
    root = jnp.exp(jnp.log(jnp.maximum(size, 1e-37)) * (1.0 / POWER))
    root = jnp.where(size > 0.0, root, 0.0)
    return jnp.where(coded < 0.0, -root, root)


def call(kernel, scalars, inputs, outputs, specs=None, scratch=(), flops=0):
    def full(shape):
        return pl.BlockSpec(shape, lambda i, s: (0,) * len(shape))

    specs = specs or {}
    in_specs = [specs.get(n, full(x.shape)) for n, x in enumerate(inputs)]
    out_specs = [full(o.shape) for o in outputs]
    moved = sum(math.prod(x.shape) * x.dtype.itemsize for x in (*inputs, *outputs))
    return pl.pallas_call(
        kernel,
        grid_spec=pltpu.PrefetchScalarGridSpec(
            num_scalar_prefetch=1,
            grid=(1,),
            in_specs=in_specs,
            out_specs=out_specs,
            scratch_shapes=list(scratch),
        ),
        out_shape=list(outputs),
        compiler_params=pltpu.CompilerParams(vmem_limit_bytes=VMEM),
        cost_estimate=pl.CostEstimate(flops=flops, bytes_accessed=moved, transcendentals=0),
    )(scalars, *inputs)


def pack_kernel(width, place_ref, x_ref, g_ref, out_ref):
    rows, cols, channels = x_ref.shape
    blocks = channels // width
    for q in range(rows // 2):
        lanes = [ref[2 * q + h].astype(jnp.float32) for h in range(2) for ref in (x_ref, g_ref)]
        lanes = [jnp.pad(x, ((0, PAD - cols), (0, 0))) for x in lanes]
        for b in range(blocks):
            pieces = [x[:, b * width : (b + 1) * width] for x in lanes]
            out_ref[b, q * PAD : (q + 1) * PAD, :] = jnp.concatenate(pieces, axis=1).astype(jnp.bfloat16)


def lon_kernel(inner, place_ref, table_ref, *refs):
    fields, (coded_ref, spec_ref) = refs[:inner], refs[inner:]
    member = place_ref[1]
    pairs, modes, lanes = spec_ref.shape
    blocks = fields[0].shape[0]
    tops = []
    for q in range(pairs):
        total = None
        for s, field in enumerate(fields):
            source = lax.rem(member - s + inner, inner)
            data = field[:, q * PAD : (q + 1) * PAD, :].reshape(blocks * PAD, lanes)
            term = dot(table_ref[0, source], data)
            total = term if total is None else total + term
        spec = total[:modes] + total[modes:]
        spec_ref[q] = spec
        tops.append(jnp.max(jnp.abs(spec), axis=0, keepdims=True))
    values, level = scaled(spec_ref[...], functools.reduce(jnp.maximum, tops))
    coded_ref[: pairs * modes, :] = encode(values).reshape(pairs * modes, lanes)
    coded_ref[pairs * modes :, :] = jnp.broadcast_to(level, (PAD, lanes)).astype(jnp.bfloat16)


def mlp_kernel(lat, inner, pairs, scaling, place_ref, *refs):
    spec_refs = refs[:lat]
    l_high, l_low, t_high, t_low, win_ref, bin_ref, wout_ref = refs[lat : lat + 7]
    back_ref, keep_ref, *rest = refs[lat + 7 :]
    send_refs, (z_ref, w_ref) = rest[: inner - 1], rest[inner - 1 :]
    place, member, x = place_ref[0], place_ref[1], place_ref[2]
    modes = (spec_refs[0].shape[0] - PAD) // pairs
    width = win_ref.shape[2]
    wide = 2 * width
    band = modes // lat
    group = band // 2
    size = l_high.shape[0]
    points = size // 2
    part = size // lat

    for s, ref in enumerate(spec_refs):
        source = lax.rem(x - s + lat, lat)
        start = pl.multiple_of(source * part, part)
        level = ref[pairs * modes :, :].astype(jnp.float32)[:1] * (1.0 / TOP)
        for q in range(pairs):
            values = decode(ref[q * modes : (q + 1) * modes, :]) * level
            for n in range(lat):
                for h in range(2):
                    row = start + (h * pairs + q) * band
                    piece = values[n * band : (n + 1) * band, h * wide : (h + 1) * wide]
                    z_ref[n, pl.ds(pl.multiple_of(row, 8), band), :] = piece

    def real_form(ref):
        re, im = ref[0, 0], ref[1, 0]
        return split(
            jnp.concatenate([jnp.concatenate([re, im], axis=1), jnp.concatenate([-im, re], axis=1)], axis=0)
        )

    m_in, m_out = real_form(win_ref), real_form(wout_ref)
    bias = jnp.concatenate([bin_ref[0, pl.ds(place, 1), :], bin_ref[1, pl.ds(place, 1), :]], axis=1)
    table = (l_high[...], l_low[...])
    inverse = (t_high[0], t_low[0])
    local = lax.broadcasted_iota(jnp.int32, (points, 1), 0) & (group - 1)
    sums = [None, None, None]
    for n in range(lat):
        spectra = dot3(table, split(z_ref[n]))
        spec_x = jnp.concatenate([spectra[:points, :width], spectra[points:, :width]], axis=1)
        spec_g = jnp.concatenate([spectra[:points, width:], spectra[points:, width:]], axis=1)
        first = (local + (member * (modes // 2) + n * group)) == 0
        grad_out = spec_g * jnp.where(first, 1.0, 2.0)
        x_parts, g_parts = split(spec_x), split(grad_out)
        pre = dot3(x_parts, m_in) + bias
        cdf = 0.5 * (1.0 + lax.erf(pre * root_half))
        hidden = pre * cdf
        slopes = cdf + pre * jnp.exp(-0.5 * pre * pre) * density_norm
        grad_pre = dot3(g_parts, m_out, ((1,), (1,))) * slopes
        p_parts = split(grad_pre)
        grad_spec = dot3(p_parts, m_in, ((1,), (1,)))
        stacked = jnp.concatenate([grad_spec[:, :width], grad_spec[:, width:]], axis=0)
        back = dot3(inverse, split(stacked))
        for q in range(pairs):
            pieces = [back[(h * pairs + q) * band : (h * pairs + q + 1) * band] for h in range(2)]
            back_ref[q, n * band : (n + 1) * band, :] = jnp.concatenate(pieces, axis=1)
        terms = (
            dot3(x_parts, p_parts, ((0,), (0,))),
            dot3(split(hidden), g_parts, ((0,), (0,))),
            jnp.sum(grad_pre, axis=0, keepdims=True),
        )
        sums = [t if a is None else a + t for a, t in zip(sums, terms)]

    pieces = []
    for total in sums[:2]:
        pieces.append(total[:width, :width] + total[width:, width:])
        pieces.append(total[:width, width:] - total[width:, :width])
    weights = jnp.concatenate(pieces, axis=1) * scaling
    share = width // inner
    w_ref[...] = jnp.zeros_like(w_ref)
    for n in range(inner):
        w_ref[n, :share, :] = weights[n * share : (n + 1) * share]
    w_ref[0, share : share + 1, :wide] = sums[2] * scaling
    keep_ref[...] = w_ref[member]
    for s in range(1, inner):
        send_refs[s - 1][...] = w_ref[lax.rem(member + s, inner)]


def synth_kernel(inner, place_ref, high_ref, low_ref, *refs):
    backs, sums, (out_ref, wide_ref) = refs[:inner], refs[inner : 2 * inner], refs[2 * inner :]
    member = place_ref[1]
    pairs, modes, lanes = backs[0].shape
    blocks, total_rows, wide = out_ref.shape
    data_rows = pairs * HALF
    for q in range(pairs):
        total = None
        for s, back in enumerate(backs):
            source = lax.rem(member - s + inner, inner)
            term = dot3((high_ref[0, source], low_ref[0, source]), split(back[q]))
            total = term if total is None else total + term
        part = blocks * HALF
        columns = jnp.concatenate([total[:part], total[part:]], axis=1)
        wide_ref[:, q * HALF : (q + 1) * HALF, :] = columns.reshape(blocks, HALF, wide)
    weights = sums[0][...]
    for ref in sums[1:]:
        weights = weights + ref[...]

    top_w = jnp.max(jnp.abs(weights), axis=0, keepdims=True)
    weights, level_w = scaled(weights, top_w)
    columns = wide_ref[:, :data_rows, :]
    top = jnp.max(jnp.max(jnp.abs(columns), axis=0), axis=0, keepdims=True)
    columns, level = scaled(columns, top)
    sum_rows = weights.shape[0]
    place_row = lax.broadcasted_iota(jnp.int32, (sum_rows, 1), 0)
    tail = jnp.where(place_row == sum_rows - 2, level_w, encode(weights).astype(jnp.float32))
    tail = jnp.where(place_row == sum_rows - 1, level, tail)
    coded = encode(columns).astype(jnp.float32)
    for b in range(blocks):
        out_ref[b] = jnp.concatenate([coded[b], tail], axis=0).astype(jnp.bfloat16)


def columns_kernel(place_ref, data_ref, cot_ref, out_ref):
    rows, cols, _ = cot_ref.shape
    blocks, total_rows, wide = data_ref.shape
    width = wide // 4
    pairs = rows // 2
    top = -(-pairs * HALF // 16) * 16
    values = []
    for b in range(blocks):
        level = data_ref[b, total_rows - 16 :, :].astype(jnp.float32)[15:16]
        values.append(decode(data_ref[b, :top, :]) * (level * (1.0 / TOP)))
    for q in range(pairs):
        for h in range(2):
            parts = []
            for half in range(2):
                start = (2 * half + h) * width
                pieces = [v[q * HALF : (q + 1) * HALF, start : start + width] for v in values]
                parts.append(jnp.concatenate(pieces, axis=1))
            column = jnp.concatenate(parts, axis=0)[:cols]
            row = 2 * q + h
            out_ref[row] = (cot_ref[row].astype(jnp.float32) + column).astype(jnp.bfloat16)


def weights_kernel(inner, data_rows, place_ref, *refs):
    pieces, (win_ref, bin_ref, wout_ref) = refs[:inner], refs[inner:]
    member = place_ref[1]
    blocks, total_rows, wide = pieces[0].shape
    width = wide // 4
    share = width // inner
    base = data_rows // 16 * 16
    skip = data_rows - base
    for b in range(blocks):
        held = []
        for ref in pieces:
            raw = ref[b, base:, :]
            level = raw.astype(jnp.float32)[total_rows - base - 2 : total_rows - base - 1]
            held.append(decode(raw)[skip:] * (level * (1.0 / TOP)))
        for n in range(inner):
            part = held[0]
            for s in range(1, inner):
                part = jnp.where(lax.rem(member - s + inner, inner) == n, held[s], part)
            for i, (ref, k) in enumerate(((win_ref, 0), (win_ref, 1), (wout_ref, 0), (wout_ref, 1))):
                ref[k, b, n * share : (n + 1) * share, :] = part[:share, i * width : (i + 1) * width]
            if n == 0:
                for k in range(2):
                    bin_ref[k, b : b + 1, :] = part[share : share + 1, k * width : (k + 1) * width]


def body(features, cotangent, weight_in, bias_in, weight_out):
    lon_count, lat_count = lax.axis_size("lon"), lax.axis_size("lat")
    blocks, width = weight_in.shape[1:3]
    rows, cols, _ = features.shape
    inner = lon_count // blocks
    pairs = rows // 2
    wide = 4 * width
    modes = 2 * MODE_DEV * blocks
    group = modes // 2 // lat_count
    size = 2 * rows * lat_count * group
    lon_place = lax.axis_index("lon")
    lat_place = lax.axis_index("lat")
    scalars = jnp.stack([lon_place // inner, lon_place % inner, lat_place]).astype(jnp.int32)
    scaling = (rows * lat_count * modes // 2 * inner) ** -0.5
    forward, synth_high, synth_low = lon_tables(blocks, inner, cols)
    table = lat_table(rows, lat_count, group)
    l_high, l_low = halves(table)
    t_high, t_low = halves(table.T.reshape(lat_count, size // lat_count, size))
    share = width // inner
    total_rows = -(-(pairs * HALF + share + 1 + 2) // 16) * 16
    sum_rows = total_rows - pairs * HALF
    f32, bf16 = jnp.float32, jnp.bfloat16
    shape = jax.ShapeDtypeStruct

    places = [[g * inner + i for g in range(blocks)] for i in range(inner)]

    def exchange(values):
        return lax.all_to_all(
            values, "lon", split_axis=0, concat_axis=0, tiled=True, axis_index_groups=places
        )

    def to_member(values, step):
        turn = [(i, i // inner * inner + (i + step) % inner) for i in range(lon_count)]
        return lax.ppermute(values, "lon", turn)

    def to_lat(values, step):
        return lax.ppermute(values, "lat", [(i, (i + step) % lat_count) for i in range(lat_count)])

    def member_block(array):
        rest = array.shape[1:]
        return pl.BlockSpec((1, *rest), lambda i, s: (s[1],) + (0,) * len(rest))

    (packed,) = call(
        functools.partial(pack_kernel, width),
        scalars,
        (features, cotangent),
        (shape((blocks, pairs * PAD, wide), bf16),),
    )
    arrived = exchange(packed)
    fields = [arrived] + [to_member(arrived, s) for s in range(1, inner)]
    (coded,) = call(
        functools.partial(lon_kernel, inner),
        scalars,
        (forward, *fields),
        (shape((pairs * modes + PAD, wide), bf16),),
        specs={0: member_block(forward)},
        scratch=(pltpu.VMEM((pairs, modes, wide), f32),),
    )
    spectra = [coded] + [to_lat(coded, s) for s in range(1, lat_count)]
    n = lat_count
    lat_block = pl.BlockSpec((1, *t_high.shape[1:]), lambda i, s: (s[2], 0, 0))
    block_spec = pl.BlockSpec((2, 1, width, width), lambda i, s: (0, s[0], 0, 0))
    back, keep, *send = call(
        functools.partial(mlp_kernel, lat_count, inner, pairs, scaling),
        scalars,
        (*spectra, l_high, l_low, t_high, t_low, weight_in, bias_in, weight_out),
        (shape((pairs, modes, 2 * width), f32), *[shape((sum_rows, wide), f32)] * inner),
        specs={n + 2: lat_block, n + 3: lat_block, n + 4: block_spec, n + 6: block_spec},
        scratch=(
            pltpu.VMEM((lat_count, size, 2 * width), f32),
            pltpu.VMEM((inner, sum_rows, wide), f32),
        ),
    )
    backs = [back] + [to_member(back, s) for s in range(1, inner)]
    sums = [keep] + [to_member(send[s - 1], s) for s in range(1, inner)]
    (payload,) = call(
        functools.partial(synth_kernel, inner),
        scalars,
        (synth_high, synth_low, *backs, *sums),
        (shape((blocks, total_rows, wide), bf16),),
        specs={0: member_block(synth_high), 1: member_block(synth_low)},
        scratch=(pltpu.VMEM((blocks, pairs * HALF, wide), f32),),
    )
    returned = exchange(payload)
    gathered = [returned] + [to_member(returned, s) for s in range(1, inner)]
    (grad_features,) = call(
        columns_kernel, scalars, (returned, cotangent), (shape(features.shape, bf16),)
    )
    grad_w_in, grad_b_in, grad_w_out = call(
        functools.partial(weights_kernel, inner, pairs * HALF),
        scalars,
        gathered,
        (shape(weight_in.shape, f32), shape(bias_in.shape, f32), shape(weight_out.shape, f32)),
    )
    return grad_features, grad_w_in, grad_b_in, grad_w_out


def solution(mesh):
    placed = (P("lat", "lon", None), P("lat", "lon", None), P(), P(), P())
    return jax.shard_map(
        body,
        mesh=mesh,
        in_specs=placed,
        out_specs=(P("lat", "lon", None), P(), P(), P()),
        check_vma=False,
    )
```

profile of v0, /device:TPU:0, one launch (start us, length us, event | category | flops | bytes accessed | tf_op | source)
XLA Modules:
  0.0 75.3 jit_solution(15694543248943512852)
XLA Ops:
  0.6 0.1 pad_add_fusion.place_ref
  0.7 0.9 %copy-done = bf16[10,14,768]{2,1,0:T(8,128)(2,1)S(1)} copy-done((bf16[10,14,768]{2,1,0:T(8,128)(2,1)S(1)}, bf16[10,14,768]{2,1,0:T(8,128)(2,1)}, u32[]{:S(2)}) %copy-start) | copy-done | bytes 215064
  1.7 0.9 %copy-done.8 = bf16[10,14,768]{2,1,0:T(8,128)(2,1)S(1)} copy-done((bf16[10,14,768]{2,1,0:T(8,128)(2,1)S(1)}, bf16[10,14,768]{2,1,0:T(8,128)(2,1)}, u32[]{:S(2)}) %copy-start.8) | copy-done | bytes 215064
  2.6 0.8 %shard_map.147 = bf16[8,80,384]{2,1,0:T(8,128)(2,1)S(1)} custom-call(s32[3]{0:T(128)S(1)} %pad_add_fusion.place_ref, bf16[10,14,768]{2,1,0:T(8,128)(2,1)S(1)} %copy-done.8, bf16[10,14,768]{2,1,0:T(8,128)(2,1)S(1)} %copy-done), custom_call_target="tpu_custom_call" | custom-call | bytes 921600 | tf_op jit(solution)/shard_map/pallas_call | solution.py:101
  3.4 0.0 copy-start.3
  3.4 21.0 %all_to_all.10.refs_0_ = bf16[8,80,384]{2,1,0:T(8,128)(2,1)S(1)} all-to-all(bf16[8,80,384]{2,1,0:T(8,128)(2,1)S(1)} %shard_map.147), channel_id=1, replica_groups={{0,4,8,12,16,20,24,28},{2,6,10,14,18,22,26,30},{1,5,9,13,17,21,25,29},{..., dimensions={0} | all-to-all | bytes 983040 | tf_op jit(solution)/shard_map/all_to_all | solution.py:335
  24.5 0.0 collective-permute-start
  24.5 1.9 %collective-permute-done.refs_1_ = bf16[8,80,384]{2,1,0:T(8,128)(2,1)S(1)} collective-permute-done((bf16[8,80,384]{2,1,0:T(8,128)(2,1)S(1)}, bf16[8,80,384]{2,1,0:T(8,128)(2,1)S(1)}, u32[]{:S(2)}, u32[]{:S(2)}) %collective-permute-start) | collective-permute-done | bytes 491552 | tf_op jit(solution)/shard_map/ppermute | solution.py:341
  26.4 0.9 %copy-done.11 = bf16[2,2,128,128]{3,2,1,0:T(8,128)(2,1)S(1)} copy-done((bf16[2,2,128,128]{3,2,1,0:T(8,128)(2,1)S(1)}, bf16[2,2,128,128]{3,2,1,0:T(8,128)(2,1)}, u32[]{:S(2)}) %copy-start.11) | copy-done | bytes 131096
  27.3 1.1 %shard_map.148.refs_0_ = bf16[336,384]{1,0:T(8,128)(2,1)S(1)} custom-call(s32[3]{0:T(128)S(1)} %pad_add_fusion.place_ref, bf16[2,2,128,128]{3,2,1,0:T(8,128)(2,1)S(1)} %copy-done.11, bf16[8,80,384]{2,1,0:T(8,128)(2,1)S(1)} %all_to_all.10.refs_0_, bf16[8,80,384]{2,1,0:T(8,128)(2,1)S(1)} %collective-permute-done.refs_1_), custom_call_target="tpu_custom_call" | custom-call | bytes 1372160 | tf_op jit(solution)/shard_map/pallas_call | solution.py:101
  28.4 1.6 %collective-permute-start.1 = (bf16[336,384]{1,0:T(8,128)(2,1)S(1)}, bf16[336,384]{1,0:T(8,128)(2,1)S(1)}, u32[]{:S(2)}, u32[]{:S(2)}) collective-permute-start(bf16[336,384]{1,0:T(8,128)(2,1)S(1)} %shard_map.148.refs_0_), channel_id=1, source_target_pairs={{0,1},{1,0},{2,3},{3,2},{4,5},{5,4},{6,7},{7,6},{8,9},{9,8},{10,11... | collective-permute-start | bytes 774152 | tf_op jit(solution)/shard_map/ppermute | solution.py:344
  29.9 6.8 %collective-permute-done.1.refs_1_ = bf16[336,384]{1,0:T(8,128)(2,1)S(1)} collective-permute-done((bf16[336,384]{1,0:T(8,128)(2,1)S(1)}, bf16[336,384]{1,0:T(8,128)(2,1)S(1)}, u32[]{:S(2)}, u32[]{:S(2)}) %collective-permute-start.1) | collective-permute-done | bytes 258080 | tf_op jit(solution)/shard_map/ppermute | solution.py:344
  36.7 0.0 copy-done.4
  36.7 0.0 copy-done.5
  36.7 0.0 copy-done.3
  36.7 0.0 copy-done.2
  36.7 0.0 copy-done.12
  36.7 0.0 copy-start.6
  36.7 1.1 %copy-done.6 = f32[2,8,96,96]{3,2,1,0:T(8,128)S(1)} copy-done((f32[2,8,96,96]{3,2,1,0:T(8,128)S(1)}, f32[2,8,96,96]{3,2,1,0:T(8,128)}, u32[]{:S(2)}) %copy-start.6) | copy-done | bytes 589848
  37.9 1.1 %copy-done.7 = f32[2,8,96,96]{3,2,1,0:T(8,128)S(1)} copy-done((f32[2,8,96,96]{3,2,1,0:T(8,128)S(1)}, f32[2,8,96,96]{3,2,1,0:T(8,128)}, u32[]{:S(2)}) %copy-start.7) | copy-done | bytes 589848
  39.0 8.2 %shard_map.149 = (f32[5,64,192]{2,1,0:T(8,128)S(1)}, f32[56,384]{1,0:T(8,128)S(1)}, f32[56,384]{1,0:T(8,128)S(1)}) custom-call(s32[3]{0:T(128)S(1)} %pad_add_fusion.place_ref, bf16[336,384]{1,0:T(8,128)(2,1)S(1)} %shard_map.148.refs_0_, bf16[336,384]{1,0:T(8,128)(2,1)S(1)} %collective-permute-done.1.refs_1_, bf16[640,640]{1,0:T(8,128)(2,1)S(1)} %copy-done.2, ...), custom_call_target="tpu_custom_call" | custom-call | bytes 5396480 | tf_op jit(solution)/shard_map/pallas_call | solution.py:101
  47.2 0.1 collective-permute-start.2
  47.3 0.5 collective-permute-start.3
  47.8 1.2 %collective-permute-done.3.refs_3_ = f32[56,384]{1,0:T(8,128)S(1)} collective-permute-done((f32[56,384]{1,0:T(8,128)S(1)}, f32[56,384]{1,0:T(8,128)S(1)}, u32[]{:S(2)}, u32[]{:S(2)}) %collective-permute-start.3) | collective-permute-done | bytes 86048 | tf_op jit(solution)/shard_map/ppermute | solution.py:341
  49.1 0.0 collective-permute-done.2.refs_1_
  49.1 1.4 %shard_map.150 = bf16[8,96,384]{2,1,0:T(8,128)(2,1)S(1)} custom-call(s32[3]{0:T(128)S(1)} %pad_add_fusion.place_ref, bf16[2,2,128,64]{3,2,1,0:T(8,128)(2,1)S(1)} %copy-done.9, bf16[2,2,128,64]{3,2,1,0:T(8,128)(2,1)S(1)} %copy-done.10, f32[5,64,192]{2,1,0:T(8,128)S(1)} %get-tuple-element.10.refs_0_, f32[5,64,192]{2,1,0:T(8,128)S(1)} %collective-permute-done.2.refs_1_, ...), custom_call_target="tpu_custom_call" | custom-call | bytes 1384448 | tf_op jit(solution)/shard_map/pallas_call | solution.py:101
  50.5 0.0 copy-start.1
  50.5 20.4 %all_to_all.11.data_ref.refs_0_ = bf16[8,96,384]{2,1,0:T(8,128)(2,1)S(1)} all-to-all(bf16[8,96,384]{2,1,0:T(8,128)(2,1)S(1)} %shard_map.150), channel_id=1, replica_groups={{0,4,8,12,16,20,24,28},{2,6,10,14,18,22,26,30},{1,5,9,13,17,21,25,29},{..., dimensions={0} | all-to-all | bytes 1179648 | tf_op jit(solution)/shard_map/all_to_all | solution.py:335
  70.9 0.0 collective-permute-start.4
  70.9 1.6 %shard_map.151 = bf16[10,14,768]{2,1,0:T(8,128)(2,1)} custom-call(s32[3]{0:T(128)S(1)} %pad_add_fusion.place_ref, bf16[8,96,384]{2,1,0:T(8,128)(2,1)S(1)} %all_to_all.11.data_ref.refs_0_, bf16[10,14,768]{2,1,0:T(8,128)(2,1)S(1)} %copy-done.1), custom_call_target="tpu_custom_call" | custom-call | bytes 1019904 | tf_op jit(solution)/shard_map/pallas_call | solution.py:101
  72.5 0.4 collective-permute-done.4.refs_1_
  72.9 2.5 %shard_map.152 = (f32[2,8,96,96]{3,2,1,0:T(8,128)}, f32[2,8,96]{2,1,0:T(8,128)}, f32[2,8,96,96]{3,2,1,0:T(8,128)}) custom-call(s32[3]{0:T(128)S(1)} %pad_add_fusion.place_ref, bf16[8,96,384]{2,1,0:T(8,128)(2,1)S(1)} %all_to_all.11.data_ref.refs_0_, bf16[8,96,384]{2,1,0:T(8,128)(2,1)S(1)} %collective-permute-done.4.refs_1_), custom_call_target="tpu_custom_call" | custom-call | bytes 2365440 | tf_op jit(solution)/shard_map/pallas_call | solution.py:101
  (13 shorter events, 0.0 us)
Async XLA Ops:
  0.7 0.9 %copy-start = (bf16[10,14,768]{2,1,0:T(8,128)(2,1)S(1)}, bf16[10,14,768]{2,1,0:T(8,128)(2,1)}, u32[]{:S(2)}) copy-start(bf16[10,14,768]{2,1,0:T(8,128)(2,1)} %cot_ref.1) | copy-start | bytes 645124
  1.7 0.9 %copy-start.8 = (bf16[10,14,768]{2,1,0:T(8,128)(2,1)S(1)}, bf16[10,14,768]{2,1,0:T(8,128)(2,1)}, u32[]{:S(2)}) copy-start(bf16[10,14,768]{2,1,0:T(8,128)(2,1)} %x_ref.1) | copy-start | bytes 645124
  2.6 34.1 %copy-start.4 = (bf16[2,320,640]{2,1,0:T(8,128)(2,1)S(1)}, bf16[2,320,640]{2,1,0:T(8,128)(2,1)}, u32[]{:S(2)}) copy-start(bf16[2,320,640]{2,1,0:T(8,128)(2,1)} %constant.49.clone.refs_4_) | copy-start | bytes 2457604
  2.6 34.1 %copy-start.5 = (bf16[2,320,640]{2,1,0:T(8,128)(2,1)S(1)}, bf16[2,320,640]{2,1,0:T(8,128)(2,1)}, u32[]{:S(2)}) copy-start(bf16[2,320,640]{2,1,0:T(8,128)(2,1)} %constant.50.clone.refs_5_) | copy-start | bytes 2457604
  3.4 33.3 %copy-start.3 = (bf16[640,640]{1,0:T(8,128)(2,1)S(1)}, bf16[640,640]{1,0:T(8,128)(2,1)}, u32[]{:S(2)}) copy-start(bf16[640,640]{1,0:T(8,128)(2,1)} %constant.48.clone.refs_3_) | copy-start | bytes 2457604
  24.5 12.2 %copy-start.2 = (bf16[640,640]{1,0:T(8,128)(2,1)S(1)}, bf16[640,640]{1,0:T(8,128)(2,1)}, u32[]{:S(2)}) copy-start(bf16[640,640]{1,0:T(8,128)(2,1)} %constant.47.clone.refs_2_) | copy-start | bytes 2457604
  24.5 1.9 %collective-permute-start = (bf16[8,80,384]{2,1,0:T(8,128)(2,1)S(1)}, bf16[8,80,384]{2,1,0:T(8,128)(2,1)S(1)}, u32[]{:S(2)}, u32[]{:S(2)}) collective-permute-start(bf16[8,80,384]{2,1,0:T(8,128)(2,1)S(1)} %all_to_all.10.refs_0_), channel_id=1, source_target_pairs={{0,2},{2,0},{4,6},{6,4},{8,10},{10,8},{12,14},{14,12},{16,18},{18,... | collective-permute-start | bytes 1474568 | tf_op jit(solution)/shard_map/ppermute | solution.py:341
  26.4 0.9 %copy-start.11 = (bf16[2,2,128,128]{3,2,1,0:T(8,128)(2,1)S(1)}, bf16[2,2,128,128]{3,2,1,0:T(8,128)(2,1)}, u32[]{:S(2)}) copy-start(bf16[2,2,128,128]{3,2,1,0:T(8,128)(2,1)} %constant.46.clone.table_ref) | copy-start | bytes 393220
  27.3 9.5 %copy-start.12 = (f32[2,8,96]{2,1,0:T(8,128)S(1)}, f32[2,8,96]{2,1,0:T(8,128)}, u32[]{:S(2)}) copy-start(f32[2,8,96]{2,1,0:T(8,128)} %refs_7_.1) | copy-start | bytes 18436
  28.4 8.3 %collective-permute-start.1 = (bf16[336,384]{1,0:T(8,128)(2,1)S(1)}, bf16[336,384]{1,0:T(8,128)(2,1)S(1)}, u32[]{:S(2)}, u32[]{:S(2)}) collective-permute-start(bf16[336,384]{1,0:T(8,128)(2,1)S(1)} %shard_map.148.refs_0_), channel_id=1, source_target_pairs={{0,1},{1,0},{2,3},{3,2},{4,5},{5,4},{6,7},{7,6},{8,9},{9,8},{10,11... | collective-permute-start | bytes 774152 | tf_op jit(solution)/shard_map/ppermute | solution.py:344
  36.7 1.1 %copy-start.6 = (f32[2,8,96,96]{3,2,1,0:T(8,128)S(1)}, f32[2,8,96,96]{3,2,1,0:T(8,128)}, u32[]{:S(2)}) copy-start(f32[2,8,96,96]{3,2,1,0:T(8,128)} %refs_6_.1) | copy-start | bytes 1769476
  37.9 1.1 %copy-start.7 = (f32[2,8,96,96]{3,2,1,0:T(8,128)S(1)}, f32[2,8,96,96]{3,2,1,0:T(8,128)}, u32[]{:S(2)}) copy-start(f32[2,8,96,96]{3,2,1,0:T(8,128)} %refs_8_.1) | copy-start | bytes 1769476
  39.0 10.1 %copy-start.9 = (bf16[2,2,128,64]{3,2,1,0:T(8,128)(2,1)S(1)}, bf16[2,2,128,64]{3,2,1,0:T(8,128)(2,1)}, u32[]{:S(2)}) copy-start(bf16[2,2,128,64]{3,2,1,0:T(8,128)(2,1)} %constant.51.clone.high_ref) | copy-start | bytes 196612
  39.0 10.1 %copy-start.10 = (bf16[2,2,128,64]{3,2,1,0:T(8,128)(2,1)S(1)}, bf16[2,2,128,64]{3,2,1,0:T(8,128)(2,1)}, u32[]{:S(2)}) copy-start(bf16[2,2,128,64]{3,2,1,0:T(8,128)(2,1)} %constant.52.clone.low_ref) | copy-start | bytes 196612
  47.2 1.8 %collective-permute-start.2 = (f32[5,64,192]{2,1,0:T(8,128)S(1)}, f32[5,64,192]{2,1,0:T(8,128)S(1)}, u32[]{:S(2)}, u32[]{:S(2)}) collective-permute-start(f32[5,64,192]{2,1,0:T(8,128)S(1)} %get-tuple-element.10.refs_0_), channel_id=1, source_target_pairs={{0,2},{2,0},{4,6},{6,4},{8,10},{10,8},{12,14},{14,12},{16,18},{18,... | collective-permute-start | bytes 737288 | tf_op jit(solution)/shard_map/ppermute | solution.py:341
  47.3 1.7 %collective-permute-start.3 = (f32[56,384]{1,0:T(8,128)S(1)}, f32[56,384]{1,0:T(8,128)S(1)}, u32[]{:S(2)}, u32[]{:S(2)}) collective-permute-start(f32[56,384]{1,0:T(8,128)S(1)} %get-tuple-element.12), channel_id=1, source_target_pairs={{0,2},{2,0},{4,6},{6,4},{8,10},{10,8},{12,14},{14,12},{16,18},{18,... | collective-permute-start | bytes 258056 | tf_op jit(solution)/shard_map/ppermute | solution.py:341
  50.5 20.4 %copy-start.1 = (bf16[10,14,768]{2,1,0:T(8,128)(2,1)S(1)}, bf16[10,14,768]{2,1,0:T(8,128)(2,1)}, u32[]{:S(2)}) copy-start(bf16[10,14,768]{2,1,0:T(8,128)(2,1)} %cot_ref.1) | copy-start | bytes 645124
  70.9 2.0 %collective-permute-start.4 = (bf16[8,96,384]{2,1,0:T(8,128)(2,1)S(1)}, bf16[8,96,384]{2,1,0:T(8,128)(2,1)S(1)}, u32[]{:S(2)}, u32[]{:S(2)}) collective-permute-start(bf16[8,96,384]{2,1,0:T(8,128)(2,1)S(1)} %all_to_all.11.data_ref.refs_0_), channel_id=1, source_target_pairs={{0,2},{2,0},{4,6},{6,4},{8,10},{10,8},{12,14},{14,12},{16,18},{18,... | collective-permute-start | bytes 1769480 | tf_op jit(solution)/shard_map/ppermute | solution.py:341
where the time goes:
time: 75.7 us; the launch traced here: 75.3 us
  blocking collectives  41.4 us (55%)
  Pallas kernels  15.6 us (21%)
  waiting for transfers between devices  10.3 us (14%)
  local copies, waits for them, and re-layouts  5.09 us (7%)
  starting transfers between devices  2.13 us (3%)
    all_to_all x2, blocking collectives, exchange(): lax.all_to_all(values, 'lon', split_axis=0, concat_axis=0, tiled=True, ax...  41.4 us
    pallas_call x6, Pallas kernels, call(): pl.pallas_call(kernel, grid_spec=pltpu.PrefetchScalarGridSpec(num_scalar_...  15.6 us
    ppermute x1, waiting for transfers between devices, to_lat(): lax.ppermute(values, 'lat', [(i, (i + step) % lat_count) for i in range(l...  6.76 us
    unnamed x26, local copies, waits for them, and re-layouts  5.09 us
    ppermute x4, waiting for transfers between devices, to_member(): return lax.ppermute(values, 'lon', turn)  3.49 us
    ppermute x1, starting transfers between devices, to_lat(): lax.ppermute(values, 'lat', [(i, (i + step) % lat_count) for i in range(l...  1.56 us
  transfers between devices with their start and end apart: 5, of which 4 were waited for; matrix products, arithmetic and copies ran while one was open for 0% of the time, Pallas kernels for 2%

commit v1 on v0

--- a/solution.py
+++ b/solution.py
@@ -13,6 +13,7 @@
 MODE_DEV = 4
 PAD = 16
 HALF = PAD // 2
+SUB = 4
 POWER = 13.0
 TOP = 2.0**9
 VMEM = 40 * 2**20
@@ -113,15 +114,30 @@
     )(scalars, *inputs)
 
 
-def pack_kernel(width, place_ref, x_ref, g_ref, out_ref):
+def pack_kernel(width, place_ref, x_hbm, g_hbm, table_hbm, out_ref, table_ref, x_ref, g_ref, sems, table_sem):
     rows, cols, channels = x_ref.shape
     blocks = channels // width
-    for q in range(rows // 2):
+    pairs = rows // 2
+
+    def fetch(q, n):
+        source, target = ((x_hbm, x_ref), (g_hbm, g_ref))[n]
+        part = pl.ds(2 * q, 2)
+        return pltpu.make_async_copy(source.at[part], target.at[part], sems.at[n, q])
+
+    for q in range(pairs):
+        for n in range(2):
+            fetch(q, n).start()
+    table = pltpu.make_async_copy(table_hbm.at[place_ref[1]], table_ref, table_sem)
+    table.start()
+    for q in range(pairs):
+        for n in range(2):
+            fetch(q, n).wait()
         lanes = [ref[2 * q + h].astype(jnp.float32) for h in range(2) for ref in (x_ref, g_ref)]
         lanes = [jnp.pad(x, ((0, PAD - cols), (0, 0))) for x in lanes]
         for b in range(blocks):
             pieces = [x[:, b * width : (b + 1) * width] for x in lanes]
             out_ref[b, q * PAD : (q + 1) * PAD, :] = jnp.concatenate(pieces, axis=1).astype(jnp.bfloat16)
+    table.wait()
 
 
 def lon_kernel(inner, place_ref, table_ref, *refs):
@@ -135,7 +151,7 @@
         for s, field in enumerate(fields):
             source = lax.rem(member - s + inner, inner)
             data = field[:, q * PAD : (q + 1) * PAD, :].reshape(blocks * PAD, lanes)
-            term = dot(table_ref[0, source], data)
+            term = dot(table_ref[source], data)
             total = term if total is None else total + term
         spec = total[:modes] + total[modes:]
         spec_ref[q] = spec
@@ -145,73 +161,87 @@
     coded_ref[pairs * modes :, :] = jnp.broadcast_to(level, (PAD, lanes)).astype(jnp.bfloat16)
 
 
+def lat_rows(ref, pairs):
+    modes = (ref.shape[0] - PAD) // pairs
+    wide = ref.shape[1] // 2
+    tile = 2 * SUB
+    level = ref[pairs * modes :, :].astype(jnp.float32)[:1] * (1.0 / TOP)
+    values = [decode(ref[q * modes : (q + 1) * modes, :]) * level for q in range(pairs)]
+    rows = []
+    for h in range(2):
+        for q in range(pairs):
+            parts = [
+                values[q][n * tile : (n + 1) * tile, h * wide : (h + 1) * wide] for n in range(modes // tile)
+            ]
+            rows.append(jnp.concatenate(parts, axis=1))
+    return jnp.concatenate(rows, axis=0)
+
+
+def ready_kernel(pairs, place_ref, spec_ref, l_high, l_low, win_ref, bin_ref, wout_ref, *outs):
+    part_ref, form_ref, bias_ref = outs
+    place, x = place_ref[0], place_ref[2]
+    for n, ref in enumerate((win_ref, wout_ref)):
+        re, im = ref[0, 0], ref[1, 0]
+        form = jnp.concatenate([jnp.concatenate([re, im], axis=1), jnp.concatenate([-im, re], axis=1)], axis=0)
+        form_ref[2 * n], form_ref[2 * n + 1] = split(form)
+    bias = jnp.concatenate([bin_ref[0, pl.ds(place, 1), :], bin_ref[1, pl.ds(place, 1), :]], axis=1)
+    bias_ref[...] = jnp.broadcast_to(bias, bias_ref.shape)
+    part_ref[...] = dot3((l_high[x], l_low[x]), split(lat_rows(spec_ref, pairs)))
+
+
 def mlp_kernel(lat, inner, pairs, scaling, place_ref, *refs):
-    spec_refs = refs[:lat]
-    l_high, l_low, t_high, t_low, win_ref, bin_ref, wout_ref = refs[lat : lat + 7]
-    back_ref, keep_ref, *rest = refs[lat + 7 :]
-    send_refs, (z_ref, w_ref) = rest[: inner - 1], rest[inner - 1 :]
-    place, member, x = place_ref[0], place_ref[1], place_ref[2]
-    modes = (spec_refs[0].shape[0] - PAD) // pairs
-    width = win_ref.shape[2]
-    wide = 2 * width
-    band = modes // lat
-    group = band // 2
-    size = l_high.shape[0]
-    points = size // 2
-    part = size // lat
-
-    for s, ref in enumerate(spec_refs):
-        source = lax.rem(x - s + lat, lat)
-        start = pl.multiple_of(source * part, part)
-        level = ref[pairs * modes :, :].astype(jnp.float32)[:1] * (1.0 / TOP)
-        for q in range(pairs):
-            values = decode(ref[q * modes : (q + 1) * modes, :]) * level
-            for n in range(lat):
-                for h in range(2):
-                    row = start + (h * pairs + q) * band
-                    piece = values[n * band : (n + 1) * band, h * wide : (h + 1) * wide]
-                    z_ref[n, pl.ds(pl.multiple_of(row, 8), band), :] = piece
-
-    def real_form(ref):
-        re, im = ref[0, 0], ref[1, 0]
-        return split(
-            jnp.concatenate([jnp.concatenate([re, im], axis=1), jnp.concatenate([-im, re], axis=1)], axis=0)
-        )
-
-    m_in, m_out = real_form(win_ref), real_form(wout_ref)
-    bias = jnp.concatenate([bin_ref[0, pl.ds(place, 1), :], bin_ref[1, pl.ds(place, 1), :]], axis=1)
-    table = (l_high[...], l_low[...])
-    inverse = (t_high[0], t_low[0])
-    local = lax.broadcasted_iota(jnp.int32, (points, 1), 0) & (group - 1)
-    sums = [None, None, None]
-    for n in range(lat):
-        spectra = dot3(table, split(z_ref[n]))
-        spec_x = jnp.concatenate([spectra[:points, :width], spectra[points:, :width]], axis=1)
-        spec_g = jnp.concatenate([spectra[:points, width:], spectra[points:, width:]], axis=1)
-        first = (local + (member * (modes // 2) + n * group)) == 0
-        grad_out = spec_g * jnp.where(first, 1.0, 2.0)
-        x_parts, g_parts = split(spec_x), split(grad_out)
-        pre = dot3(x_parts, m_in) + bias
-        cdf = 0.5 * (1.0 + lax.erf(pre * root_half))
-        hidden = pre * cdf
-        slopes = cdf + pre * jnp.exp(-0.5 * pre * pre) * density_norm
-        grad_pre = dot3(g_parts, m_out, ((1,), (1,))) * slopes
-        p_parts = split(grad_pre)
-        grad_spec = dot3(p_parts, m_in, ((1,), (1,)))
-        stacked = jnp.concatenate([grad_spec[:, :width], grad_spec[:, width:]], axis=0)
-        back = dot3(inverse, split(stacked))
-        for q in range(pairs):
-            pieces = [back[(h * pairs + q) * band : (h * pairs + q + 1) * band] for h in range(2)]
-            back_ref[q, n * band : (n + 1) * band, :] = jnp.concatenate(pieces, axis=1)
-        terms = (
-            dot3(x_parts, p_parts, ((0,), (0,))),
-            dot3(split(hidden), g_parts, ((0,), (0,))),
-            jnp.sum(grad_pre, axis=0, keepdims=True),
-        )
-        sums = [t if a is None else a + t for a, t in zip(sums, terms)]
+    others = refs[: lat - 1]
+    part_ref, form_ref, bias_ref, l_high, l_low, t_high, t_low = refs[lat - 1 : lat + 6]
+    back_ref, keep_ref, *rest = refs[lat + 6 :]
+    send_refs, (w_ref,) = rest[: inner - 1], rest[inner - 1 :]
+    member, x = place_ref[1], place_ref[2]
+    wide = form_ref.shape[1]
+    width = wide // 2
+    tile = 2 * SUB
+    points = l_high.shape[1] // 2
+    subs = part_ref.shape[1] // wide
+
+    spectra = part_ref[...]
+    for s, ref in enumerate(others):
+        source = lax.rem(x - s - 1 + lat, lat)
+        spectra = spectra + dot3((l_high[source], l_low[source]), split(lat_rows(ref, pairs)))
+
+    def of_points(start):
+        rows = []
+        for n in range(subs):
+            lanes = slice(n * wide + start, n * wide + start + width)
+            rows.append(jnp.concatenate([spectra[:points, lanes], spectra[points:, lanes]], axis=1))
+        return jnp.concatenate(rows, axis=0)
+
+    spec_x, spec_g = of_points(0), of_points(width)
+    m_in, m_out = (form_ref[0], form_ref[1]), (form_ref[2], form_ref[3])
+    point = lax.broadcasted_iota(jnp.int32, (subs * points, 1), 0)
+    first = ((point & (SUB - 1)) + jnp.where(point < points, 0, SUB) + member * SUB) == 0
+    grad_out = spec_g * jnp.where(first, 1.0, 2.0)
+    x_parts, g_parts = split(spec_x), split(grad_out)
+    pre = dot3(x_parts, m_in) + bias_ref[:1]
+    cdf = 0.5 * (1.0 + lax.erf(pre * root_half))
+    hidden = pre * cdf
+    slopes = cdf + pre * jnp.exp(-0.5 * pre * pre) * density_norm
+    grad_pre = dot3(g_parts, m_out, ((1,), (1,))) * slopes
+    p_parts = split(grad_pre)
+    grad_spec = dot3(p_parts, m_in, ((1,), (1,)))
+    lanes = []
+    for n in range(subs):
+        piece = grad_spec[n * points : (n + 1) * points]
+        lanes.append(jnp.concatenate([piece[:, :width], piece[:, width:]], axis=0))
+    back = dot3((t_high[0], t_low[0]), split(jnp.concatenate(lanes, axis=1)))
+    for q in range(pairs):
+        for n in range(subs):
+            pieces = [
+                back[(h * pairs + q) * tile : (h * pairs + q + 1) * tile, n * width : (n + 1) * width]
+                for h in range(2)
+            ]
+            back_ref[q, n * tile : (n + 1) * tile, :] = jnp.concatenate(pieces, axis=1)
 
     pieces = []
-    for total in sums[:2]:
+    for left, right in ((x_parts, p_parts), (split(hidden), g_parts)):
+        total = dot3(left, right, ((0,), (0,)))
         pieces.append(total[:width, :width] + total[width:, width:])
         pieces.append(total[:width, width:] - total[width:, :width])
     weights = jnp.concatenate(pieces, axis=1) * scaling
@@ -219,7 +249,7 @@
     w_ref[...] = jnp.zeros_like(w_ref)
     for n in range(inner):
         w_ref[n, :share, :] = weights[n * share : (n + 1) * share]
-    w_ref[0, share : share + 1, :wide] = sums[2] * scaling
+    w_ref[0, share : share + 1, :wide] = jnp.sum(grad_pre, axis=0, keepdims=True) * scaling
     keep_ref[...] = w_ref[member]
     for s in range(1, inner):
         send_refs[s - 1][...] = w_ref[lax.rem(member + s, inner)]
@@ -313,15 +343,15 @@
     pairs = rows // 2
     wide = 4 * width
     modes = 2 * MODE_DEV * blocks
-    group = modes // 2 // lat_count
-    size = 2 * rows * lat_count * group
+    size = 2 * rows * lat_count * SUB
+    subs = modes // (2 * SUB)
     lon_place = lax.axis_index("lon")
     lat_place = lax.axis_index("lat")
     scalars = jnp.stack([lon_place // inner, lon_place % inner, lat_place]).astype(jnp.int32)
     scaling = (rows * lat_count * modes // 2 * inner) ** -0.5
     forward, synth_high, synth_low = lon_tables(blocks, inner, cols)
-    table = lat_table(rows, lat_count, group)
-    l_high, l_low = halves(table)
+    table = lat_table(rows, lat_count, SUB)
+    l_high, l_low = halves(table.reshape(size, lat_count, -1).transpose(1, 0, 2))
     t_high, t_low = halves(table.T.reshape(lat_count, size // lat_count, size))
     share = width // inner
     total_rows = -(-(pairs * HALF + share + 1 + 2) // 16) * 16
@@ -347,36 +377,48 @@
         rest = array.shape[1:]
         return pl.BlockSpec((1, *rest), lambda i, s: (s[1],) + (0,) * len(rest))
 
-    (packed,) = call(
+    in_hbm = pl.BlockSpec(memory_space=pltpu.HBM)
+    field = pltpu.VMEM(features.shape, bf16)
+    packed, lon_part = call(
         functools.partial(pack_kernel, width),
         scalars,
-        (features, cotangent),
-        (shape((blocks, pairs * PAD, wide), bf16),),
+        (features, cotangent, forward),
+        (shape((blocks, pairs * PAD, wide), bf16), shape(forward.shape[1:], bf16)),
+        specs={0: in_hbm, 1: in_hbm, 2: in_hbm},
+        scratch=(field, field, pltpu.SemaphoreType.DMA((2, pairs)), pltpu.SemaphoreType.DMA(())),
     )
     arrived = exchange(packed)
     fields = [arrived] + [to_member(arrived, s) for s in range(1, inner)]
     (coded,) = call(
         functools.partial(lon_kernel, inner),
         scalars,
-        (forward, *fields),
+        (lon_part, *fields),
         (shape((pairs * modes + PAD, wide), bf16),),
-        specs={0: member_block(forward)},
         scratch=(pltpu.VMEM((pairs, modes, wide), f32),),
     )
-    spectra = [coded] + [to_lat(coded, s) for s in range(1, lat_count)]
-    n = lat_count
+    others = [to_lat(coded, s) for s in range(1, lat_count)]
+    block_spec = pl.BlockSpec((2, 1, width, width), lambda i, s: (0, s[0], 0, 0))
+    part, forms, bias = call(
+        functools.partial(ready_kernel, pairs),
+        scalars,
+        (coded, l_high, l_low, weight_in, bias_in, weight_out),
+        (
+            shape((size, 2 * subs * width), f32),
+            shape((4, 2 * width, 2 * width), bf16),
+            shape((8, 2 * width), f32),
+        ),
+        specs={3: block_spec, 5: block_spec},
+        flops=6 * size * size // lat_count * 2 * subs * width,
+    )
+    n = lat_count - 1
     lat_block = pl.BlockSpec((1, *t_high.shape[1:]), lambda i, s: (s[2], 0, 0))
-    block_spec = pl.BlockSpec((2, 1, width, width), lambda i, s: (0, s[0], 0, 0))
     back, keep, *send = call(
         functools.partial(mlp_kernel, lat_count, inner, pairs, scaling),
         scalars,
-        (*spectra, l_high, l_low, t_high, t_low, weight_in, bias_in, weight_out),
+        (*others, part, forms, bias, l_high, l_low, t_high, t_low),
         (shape((pairs, modes, 2 * width), f32), *[shape((sum_rows, wide), f32)] * inner),
-        specs={n + 2: lat_block, n + 3: lat_block, n + 4: block_spec, n + 6: block_spec},
-        scratch=(
-            pltpu.VMEM((lat_count, size, 2 * width), f32),
-            pltpu.VMEM((inner, sum_rows, wide), f32),
-        ),
+        specs={n + 5: lat_block, n + 6: lat_block},
+        scratch=(pltpu.VMEM((inner, sum_rows, wide), f32),),
     )
     backs = [back] + [to_member(back, s) for s in range(1, inner)]
     sums = [keep] + [to_member(send[s - 1], s) for s in range(1, inner)]

time: 75.7 us -> 70.1 us (0.926)
  local copies, waits for them, and re-layouts: 5.09 us -> 2.84 us
  Pallas kernels: 15.6 us -> 13.7 us
  waiting for transfers between devices: 10.3 us -> 8.96 us
    unnamed x26, local copies, waits for them, and re-layouts: 5.09 us -> 2.84 us
    pallas_call x6 -> x7, Pallas kernels: 15.6 us -> 13.7 us  [call(): pl.pallas_call(kernel, grid_spec=pltpu.PrefetchScalarGridSpec(num_scalar_...]
    ppermute x1, waiting for transfers between devices: 6.76 us -> 5.46 us  [to_lat(): lax.ppermute(values, 'lat', [(i, (i + step) % lat_count) for i in range(l...]
  transfers between devices with their start and end apart: 5 -> 5, of which waited for: 4 -> 4; matrix products, arithmetic and copies ran while one was open for 0% -> 0% of each run, Pallas kernels for 2% -> 4%
where the time goes in v1:
time: 70.1 us; the launch traced here: 69.9 us
  blocking collectives  41.4 us (59%)
  Pallas kernels  13.7 us (20%)
  waiting for transfers between devices  8.96 us (13%)
  local copies, waits for them, and re-layouts  2.84 us (4%)
  starting transfers between devices  2.13 us (3%)
  between operations  0.76 us (1%)
    all_to_all x2, blocking collectives, exchange(): lax.all_to_all(values, 'lon', split_axis=0, concat_axis=0, tiled=True, ax...  41.4 us
    pallas_call x7, Pallas kernels, call(): pl.pallas_call(kernel, grid_spec=pltpu.PrefetchScalarGridSpec(num_scalar_...  13.7 us
    ppermute x1, waiting for transfers between devices, to_lat(): lax.ppermute(values, 'lat', [(i, (i + step) % lat_count) for i in range(l...  5.46 us
    ppermute x4, waiting for transfers between devices, to_member(): return lax.ppermute(values, 'lon', turn)  3.49 us
    unnamed x26, local copies, waits for them, and re-layouts  2.84 us
    ppermute x1, starting transfers between devices, to_lat(): lax.ppermute(values, 'lat', [(i, (i + step) % lat_count) for i in range(l...  1.56 us
  transfers between devices with their start and end apart: 5, of which 4 were waited for; matrix products, arithmetic and copies ran while one was open for 0% of the time, Pallas kernels for 4%

profile of v1, /device:TPU:0, one launch (start us, length us, event | category | flops | bytes accessed | tf_op | source)
XLA Modules:
  0.0 69.9 jit_solution(17479969092724030654)
XLA Ops:
  0.6 0.1 pad_add_fusion.place_ref
  0.7 0.9 %copy-done = bf16[10,14,768]{2,1,0:T(8,128)(2,1)S(1)} copy-done((bf16[10,14,768]{2,1,0:T(8,128)(2,1)S(1)}, bf16[10,14,768]{2,1,0:T(8,128)(2,1)}, u32[]{:S(2)}) %copy-start) | copy-done | bytes 215064
  1.7 0.9 %copy-done.6 = bf16[10,14,768]{2,1,0:T(8,128)(2,1)S(1)} copy-done((bf16[10,14,768]{2,1,0:T(8,128)(2,1)S(1)}, bf16[10,14,768]{2,1,0:T(8,128)(2,1)}, u32[]{:S(2)}) %copy-start.6) | copy-done | bytes 215064
  2.6 0.9 %copy-done.9 = bf16[2,2,128,128]{3,2,1,0:T(8,128)(2,1)S(1)} copy-done((bf16[2,2,128,128]{3,2,1,0:T(8,128)(2,1)S(1)}, bf16[2,2,128,128]{3,2,1,0:T(8,128)(2,1)}, u32[]{:S(2)}) %copy-start.9) | copy-done | bytes 131096
  3.5 1.9 %shard_map.147 = (bf16[8,80,384]{2,1,0:T(8,128)(2,1)S(1)}, bf16[2,128,128]{2,1,0:T(8,128)(2,1)S(1)}) custom-call(s32[3]{0:T(128)S(1)} %pad_add_fusion.place_ref, bf16[10,14,768]{2,1,0:T(8,128)(2,1)S(1)} %copy-done.6, bf16[10,14,768]{2,1,0:T(8,128)(2,1)S(1)} %copy-done, bf16[2,2,128,128]{3,2,1,0:T(8,128)(2,1)S(1)} %copy-done.9), custom_call_target="tpu_custom_call" | custom-call | bytes 1118208 | tf_op jit(solution)/shard_map/pallas_call | solution.py:102
  5.5 0.0 copy-start.3
  5.5 21.0 %all_to_all.10.refs_0_ = bf16[8,80,384]{2,1,0:T(8,128)(2,1)S(1)} all-to-all(bf16[8,80,384]{2,1,0:T(8,128)(2,1)S(1)} %get-tuple-element.16), channel_id=1, replica_groups={{0,4,8,12,16,20,24,28},{2,6,10,14,18,22,26,30},{1,5,9,13,17,21,25,29},{..., dimensions={0} | all-to-all | bytes 983040 | tf_op jit(solution)/shard_map/all_to_all | solution.py:365
  26.5 0.0 collective-permute-start
  26.5 1.9 %collective-permute-done.refs_1_ = bf16[8,80,384]{2,1,0:T(8,128)(2,1)S(1)} collective-permute-done((bf16[8,80,384]{2,1,0:T(8,128)(2,1)S(1)}, bf16[8,80,384]{2,1,0:T(8,128)(2,1)S(1)}, u32[]{:S(2)}, u32[]{:S(2)}) %collective-permute-start) | collective-permute-done | bytes 491552 | tf_op jit(solution)/shard_map/ppermute | solution.py:371
  28.4 1.1 %shard_map.148.spec_ref = bf16[336,384]{1,0:T(8,128)(2,1)S(1)} custom-call(s32[3]{0:T(128)S(1)} %pad_add_fusion.place_ref, bf16[2,128,128]{2,1,0:T(8,128)(2,1)S(1)} %get-tuple-element.15.table_ref, bf16[8,80,384]{2,1,0:T(8,128)(2,1)S(1)} %all_to_all.10.refs_0_, bf16[8,80,384]{2,1,0:T(8,128)(2,1)S(1)} %collective-permute-done.refs_1_), custom_call_target="tpu_custom_call" | custom-call | bytes 1306624 | tf_op jit(solution)/shard_map/pallas_call | solution.py:102
  29.5 0.0 copy-start.10
  29.5 0.0 copy-start.11
  29.5 1.6 %collective-permute-start.1 = (bf16[336,384]{1,0:T(8,128)(2,1)S(1)}, bf16[336,384]{1,0:T(8,128)(2,1)S(1)}, u32[]{:S(2)}, u32[]{:S(2)}) collective-permute-start(bf16[336,384]{1,0:T(8,128)(2,1)S(1)} %shard_map.148.spec_ref), channel_id=1, source_target_pairs={{0,1},{1,0},{2,3},{3,2},{4,5},{5,4},{6,7},{7,6},{8,9},{9,8},{10,11... | collective-permute-start | bytes 774152 | tf_op jit(solution)/shard_map/ppermute | solution.py:374
  31.1 0.0 copy-done.3
  31.1 0.0 copy-done.2
  31.1 0.0 copy-done.4
  31.1 1.3 %shard_map.149 = (f32[160,1536]{1,0:T(8,128)S(1)}, bf16[4,192,192]{2,1,0:T(8,128)(2,1)S(1)}, f32[8,192]{1,0:T(8,128)S(1)}) custom-call(s32[3]{0:T(128)S(1)} %pad_add_fusion.place_ref, bf16[336,384]{1,0:T(8,128)(2,1)S(1)} %shard_map.148.spec_ref, bf16[2,160,80]{2,1,0:T(8,128)(2,1)S(1)} %copy-done.4, bf16[2,160,80]{2,1,0:T(8,128)(2,1)S(1)} %copy-done.5, ...), custom_call_target="tpu_custom_call" | custom-call | flops 117964800 | bytes 2830336 | tf_op jit(solution)/shard_map/pallas_call | solution.py:102
  32.4 5.5 %collective-permute-done.1.refs_0_ = bf16[336,384]{1,0:T(8,128)(2,1)S(1)} collective-permute-done((bf16[336,384]{1,0:T(8,128)(2,1)S(1)}, bf16[336,384]{1,0:T(8,128)(2,1)S(1)}, u32[]{:S(2)}, u32[]{:S(2)}) %collective-permute-start.1) | collective-permute-done | bytes 258080 | tf_op jit(solution)/shard_map/ppermute | solution.py:374
  37.9 0.0 copy-done.10
  37.9 3.9 %shard_map.150 = (f32[5,64,192]{2,1,0:T(8,128)S(1)}, f32[56,384]{1,0:T(8,128)S(1)}, f32[56,384]{1,0:T(8,128)S(1)}) custom-call(s32[3]{0:T(128)S(1)} %pad_add_fusion.place_ref, bf16[336,384]{1,0:T(8,128)(2,1)S(1)} %collective-permute-done.1.refs_0_, f32[160,1536]{1,0:T(8,128)S(1)} %get-tuple-element.17.refs_1_, ...), custom_call_target="tpu_custom_call" | custom-call | bytes 2164736 | tf_op jit(solution)/shard_map/pallas_call | solution.py:102
  41.8 0.1 collective-permute-start.2
  41.9 0.5 collective-permute-start.3
  42.4 1.2 %collective-permute-done.3.refs_3_ = f32[56,384]{1,0:T(8,128)S(1)} collective-permute-done((f32[56,384]{1,0:T(8,128)S(1)}, f32[56,384]{1,0:T(8,128)S(1)}, u32[]{:S(2)}, u32[]{:S(2)}) %collective-permute-start.3) | collective-permute-done | bytes 86048 | tf_op jit(solution)/shard_map/ppermute | solution.py:371
  43.6 0.0 collective-permute-done.2.refs_1_
  43.6 0.0 copy-done.7
  43.6 1.4 %shard_map.151 = bf16[8,96,384]{2,1,0:T(8,128)(2,1)S(1)} custom-call(s32[3]{0:T(128)S(1)} %pad_add_fusion.place_ref, bf16[2,2,128,64]{3,2,1,0:T(8,128)(2,1)S(1)} %copy-done.7, bf16[2,2,128,64]{3,2,1,0:T(8,128)(2,1)S(1)} %copy-done.8, f32[5,64,192]{2,1,0:T(8,128)S(1)} %get-tuple-element.20.refs_0_, f32[5,64,192]{2,1,0:T(8,128)S(1)} %collective-permute-done.2.refs_1_, ...), custom_call_target="tpu_custom_call" | custom-call | bytes 1384448 | tf_op jit(solution)/shard_map/pallas_call | solution.py:102
  45.0 0.0 copy-start.1
  45.0 20.3 %all_to_all.11.data_ref.refs_0_ = bf16[8,96,384]{2,1,0:T(8,128)(2,1)S(1)} all-to-all(bf16[8,96,384]{2,1,0:T(8,128)(2,1)S(1)} %shard_map.151), channel_id=1, replica_groups={{0,4,8,12,16,20,24,28},{2,6,10,14,18,22,26,30},{1,5,9,13,17,21,25,29},{..., dimensions={0} | all-to-all | bytes 1179648 | tf_op jit(solution)/shard_map/all_to_all | solution.py:365
  65.4 0.0 collective-permute-start.4
  65.4 1.6 %shard_map.152 = bf16[10,14,768]{2,1,0:T(8,128)(2,1)} custom-call(s32[3]{0:T(128)S(1)} %pad_add_fusion.place_ref, bf16[8,96,384]{2,1,0:T(8,128)(2,1)S(1)} %all_to_all.11.data_ref.refs_0_, bf16[10,14,768]{2,1,0:T(8,128)(2,1)S(1)} %copy-done.1), custom_call_target="tpu_custom_call" | custom-call | bytes 1019904 | tf_op jit(solution)/shard_map/pallas_call | solution.py:102
  67.0 0.4 collective-permute-done.4.refs_1_
  67.4 2.5 %shard_map.153 = (f32[2,8,96,96]{3,2,1,0:T(8,128)}, f32[2,8,96]{2,1,0:T(8,128)}, f32[2,8,96,96]{3,2,1,0:T(8,128)}) custom-call(s32[3]{0:T(128)S(1)} %pad_add_fusion.place_ref, bf16[8,96,384]{2,1,0:T(8,128)(2,1)S(1)} %all_to_all.11.data_ref.refs_0_, bf16[8,96,384]{2,1,0:T(8,128)(2,1)S(1)} %collective-permute-done.4.refs_1_), custom_call_target="tpu_custom_call" | custom-call | bytes 2365440 | tf_op jit(solution)/shard_map/pallas_call | solution.py:102
  (14 shorter events, 0.0 us)
Async XLA Ops:
  0.7 0.9 %copy-start = (bf16[10,14,768]{2,1,0:T(8,128)(2,1)S(1)}, bf16[10,14,768]{2,1,0:T(8,128)(2,1)}, u32[]{:S(2)}) copy-start(bf16[10,14,768]{2,1,0:T(8,128)(2,1)} %cot_ref.1) | copy-start | bytes 645124
  1.7 0.9 %copy-start.6 = (bf16[10,14,768]{2,1,0:T(8,128)(2,1)S(1)}, bf16[10,14,768]{2,1,0:T(8,128)(2,1)}, u32[]{:S(2)}) copy-start(bf16[10,14,768]{2,1,0:T(8,128)(2,1)} %x_hbm.1) | copy-start | bytes 645124
  2.6 0.9 %copy-start.9 = (bf16[2,2,128,128]{3,2,1,0:T(8,128)(2,1)S(1)}, bf16[2,2,128,128]{3,2,1,0:T(8,128)(2,1)}, u32[]{:S(2)}) copy-start(bf16[2,2,128,128]{3,2,1,0:T(8,128)(2,1)} %constant.46.clone.table_hbm) | copy-start | bytes 393220
  5.5 25.6 %copy-start.3 = (f32[2,8,96,96]{3,2,1,0:T(8,128)S(1)}, f32[2,8,96,96]{3,2,1,0:T(8,128)}, u32[]{:S(2)}) copy-start(f32[2,8,96,96]{3,2,1,0:T(8,128)} %wout_ref.1) | copy-start | bytes 1769476
  26.5 4.6 %copy-start.2 = (f32[2,8,96,96]{3,2,1,0:T(8,128)S(1)}, f32[2,8,96,96]{3,2,1,0:T(8,128)}, u32[]{:S(2)}) copy-start(f32[2,8,96,96]{3,2,1,0:T(8,128)} %win_ref.1) | copy-start | bytes 1769476
  26.5 1.9 %collective-permute-start = (bf16[8,80,384]{2,1,0:T(8,128)(2,1)S(1)}, bf16[8,80,384]{2,1,0:T(8,128)(2,1)S(1)}, u32[]{:S(2)}, u32[]{:S(2)}) collective-permute-start(bf16[8,80,384]{2,1,0:T(8,128)(2,1)S(1)} %all_to_all.10.refs_0_), channel_id=1, source_target_pairs={{0,2},{2,0},{4,6},{6,4},{8,10},{10,8},{12,14},{14,12},{16,18},{18,... | collective-permute-start | bytes 1474568 | tf_op jit(solution)/shard_map/ppermute | solution.py:371
  28.4 2.7 %copy-start.4 = (bf16[2,160,80]{2,1,0:T(8,128)(2,1)S(1)}, bf16[2,160,80]{2,1,0:T(8,128)(2,1)}, u32[]{:S(2)}) copy-start(bf16[2,160,80]{2,1,0:T(8,128)(2,1)} %constant.47.clone.l_high.refs_4_) | copy-start | bytes 153604
  28.4 2.7 %copy-start.5 = (bf16[2,160,80]{2,1,0:T(8,128)(2,1)S(1)}, bf16[2,160,80]{2,1,0:T(8,128)(2,1)}, u32[]{:S(2)}) copy-start(bf16[2,160,80]{2,1,0:T(8,128)(2,1)} %constant.48.clone.l_low.refs_5_) | copy-start | bytes 153604
  28.4 2.7 %copy-start.12 = (f32[2,8,96]{2,1,0:T(8,128)S(1)}, f32[2,8,96]{2,1,0:T(8,128)}, u32[]{:S(2)}) copy-start(f32[2,8,96]{2,1,0:T(8,128)} %bin_ref.1) | copy-start | bytes 18436
  29.5 8.4 %copy-start.10 = (bf16[2,80,160]{2,1,0:T(8,128)(2,1)S(1)}, bf16[2,80,160]{2,1,0:T(8,128)(2,1)}, u32[]{:S(2)}) copy-start(bf16[2,80,160]{2,1,0:T(8,128)(2,1)} %constant.49.clone.refs_6_) | copy-start | bytes 153604
  29.5 8.3 %copy-start.11 = (bf16[2,80,160]{2,1,0:T(8,128)(2,1)S(1)}, bf16[2,80,160]{2,1,0:T(8,128)(2,1)}, u32[]{:S(2)}) copy-start(bf16[2,80,160]{2,1,0:T(8,128)(2,1)} %constant.50.clone.refs_7_) | copy-start | bytes 153604
  29.5 8.3 %collective-permute-start.1 = (bf16[336,384]{1,0:T(8,128)(2,1)S(1)}, bf16[336,384]{1,0:T(8,128)(2,1)S(1)}, u32[]{:S(2)}, u32[]{:S(2)}) collective-permute-start(bf16[336,384]{1,0:T(8,128)(2,1)S(1)} %shard_map.148.spec_ref), channel_id=1, source_target_pairs={{0,1},{1,0},{2,3},{3,2},{4,5},{5,4},{6,7},{7,6},{8,9},{9,8},{10,11... | collective-permute-start | bytes 774152 | tf_op jit(solution)/shard_map/ppermute | solution.py:374
  37.9 5.8 %copy-start.7 = (bf16[2,2,128,64]{3,2,1,0:T(8,128)(2,1)S(1)}, bf16[2,2,128,64]{3,2,1,0:T(8,128)(2,1)}, u32[]{:S(2)}) copy-start(bf16[2,2,128,64]{3,2,1,0:T(8,128)(2,1)} %constant.51.clone.high_ref) | copy-start | bytes 196612
  37.9 5.8 %copy-start.8 = (bf16[2,2,128,64]{3,2,1,0:T(8,128)(2,1)S(1)}, bf16[2,2,128,64]{3,2,1,0:T(8,128)(2,1)}, u32[]{:S(2)}) copy-start(bf16[2,2,128,64]{3,2,1,0:T(8,128)(2,1)} %constant.52.clone.low_ref) | copy-start | bytes 196612
  41.8 1.8 %collective-permute-start.2 = (f32[5,64,192]{2,1,0:T(8,128)S(1)}, f32[5,64,192]{2,1,0:T(8,128)S(1)}, u32[]{:S(2)}, u32[]{:S(2)}) collective-permute-start(f32[5,64,192]{2,1,0:T(8,128)S(1)} %get-tuple-element.20.refs_0_), channel_id=1, source_target_pairs={{0,2},{2,0},{4,6},{6,4},{8,10},{10,8},{12,14},{14,12},{16,18},{18,... | collective-permute-start | bytes 737288 | tf_op jit(solution)/shard_map/ppermute | solution.py:371
  41.9 1.7 %collective-permute-start.3 = (f32[56,384]{1,0:T(8,128)S(1)}, f32[56,384]{1,0:T(8,128)S(1)}, u32[]{:S(2)}, u32[]{:S(2)}) collective-permute-start(f32[56,384]{1,0:T(8,128)S(1)} %get-tuple-element.22), channel_id=1, source_target_pairs={{0,2},{2,0},{4,6},{6,4},{8,10},{10,8},{12,14},{14,12},{16,18},{18,... | collective-permute-start | bytes 258056 | tf_op jit(solution)/shard_map/ppermute | solution.py:371
  45.0 20.4 %copy-start.1 = (bf16[10,14,768]{2,1,0:T(8,128)(2,1)S(1)}, bf16[10,14,768]{2,1,0:T(8,128)(2,1)}, u32[]{:S(2)}) copy-start(bf16[10,14,768]{2,1,0:T(8,128)(2,1)} %cot_ref.1) | copy-start | bytes 645124
  65.4 2.0 %collective-permute-start.4 = (bf16[8,96,384]{2,1,0:T(8,128)(2,1)S(1)}, bf16[8,96,384]{2,1,0:T(8,128)(2,1)S(1)}, u32[]{:S(2)}, u32[]{:S(2)}) collective-permute-start(bf16[8,96,384]{2,1,0:T(8,128)(2,1)S(1)} %all_to_all.11.data_ref.refs_0_), channel_id=1, source_target_pairs={{0,2},{2,0},{4,6},{6,4},{8,10},{10,8},{12,14},{14,12},{16,18},{18,... | collective-permute-start | bytes 1769480 | tf_op jit(solution)/shard_map/ppermute | solution.py:371

commit v2 on v1

--- a/solution.py
+++ b/solution.py
@@ -14,6 +14,7 @@
 PAD = 16
 HALF = PAD // 2
 SUB = 4
+SPARE = 6
 POWER = 13.0
 TOP = 2.0**9
 VMEM = 40 * 2**20
@@ -44,8 +45,8 @@
     forward = table.transpose(3, 1, 4, 0, 2).reshape(inner, inner, 2 * modes, blocks * PAD)
     split = table.reshape(blocks, inner, 2, HALF, inner, 2 * modes)
     synth = split.transpose(1, 4, 2, 0, 3, 5).reshape(inner, inner, 2 * blocks * HALF, 2 * modes)
-    high, low = halves(forward)
-    return np.concatenate([high, low], axis=2), *halves(synth)
+    forward, synth = np.concatenate(halves(forward), axis=2), np.concatenate(halves(synth), axis=3)
+    return forward.reshape(-1, blocks * PAD), synth.reshape(-1, 4 * modes)
 
 
 def lat_table(rows, lat_count, group):
@@ -59,6 +60,18 @@
     return np.einsum("akxhqb,mn->akmxhqnb", basis, np.eye(group)).reshape(size, size)
 
 
+def all_tables(blocks, inner, cols, rows, lat_count):
+    forward, synth = lon_tables(blocks, inner, cols)
+    table = lat_table(rows, lat_count, SUB)
+    size = table.shape[0]
+    lat = np.concatenate(halves(table.reshape(size, lat_count, -1).transpose(1, 0, 2)), axis=1)
+    parts = [forward, lat.reshape(2 * lat_count * size, -1), synth]
+    lanes = max(p.shape[1] for p in parts)
+    parts = [np.pad(p, ((0, 0), (0, lanes - p.shape[1]))) for p in parts]
+    starts = np.cumsum([0] + [len(p) for p in parts])
+    return np.concatenate(parts), [int(n) for n in starts]
+
+
 def split(values):
     high = values.astype(jnp.bfloat16)
     return high, (values - high.astype(jnp.float32)).astype(jnp.bfloat16)
@@ -75,6 +88,15 @@
 def scaled(values, top):
     level = jnp.maximum(top, 1e-30).astype(jnp.bfloat16).astype(jnp.float32)
     return values * (TOP / level), level
+
+
+def table_rows(ref, start, count, place):
+    return ref[pl.ds(pl.multiple_of(start + place * count, PAD), count), :]
+
+
+def lat_part(ref, start, size, part, x):
+    rows = table_rows(ref, start, 2 * size, x)[:, :part]
+    return rows[:size], rows[size:]
 
 
 def encode(values):
@@ -92,12 +114,10 @@
 
 
 def call(kernel, scalars, inputs, outputs, specs=None, scratch=(), flops=0):
-    def full(shape):
-        return pl.BlockSpec(shape, lambda i, s: (0,) * len(shape))
-
+    whole = pl.BlockSpec(memory_space=pltpu.VMEM)
     specs = specs or {}
-    in_specs = [specs.get(n, full(x.shape)) for n, x in enumerate(inputs)]
-    out_specs = [full(o.shape) for o in outputs]
+    in_specs = [specs.get(n, whole) for n in range(len(inputs))]
+    out_specs = [whole] * len(outputs)
     moved = sum(math.prod(x.shape) * x.dtype.itemsize for x in (*inputs, *outputs))
     return pl.pallas_call(
         kernel,
@@ -114,30 +134,16 @@
     )(scalars, *inputs)
 
 
-def pack_kernel(width, place_ref, x_hbm, g_hbm, table_hbm, out_ref, table_ref, x_ref, g_ref, sems, table_sem):
+def pack_kernel(width, place_ref, x_ref, g_ref, out_ref):
     rows, cols, channels = x_ref.shape
     blocks = channels // width
     pairs = rows // 2
-
-    def fetch(q, n):
-        source, target = ((x_hbm, x_ref), (g_hbm, g_ref))[n]
-        part = pl.ds(2 * q, 2)
-        return pltpu.make_async_copy(source.at[part], target.at[part], sems.at[n, q])
-
     for q in range(pairs):
-        for n in range(2):
-            fetch(q, n).start()
-    table = pltpu.make_async_copy(table_hbm.at[place_ref[1]], table_ref, table_sem)
-    table.start()
-    for q in range(pairs):
-        for n in range(2):
-            fetch(q, n).wait()
         lanes = [ref[2 * q + h].astype(jnp.float32) for h in range(2) for ref in (x_ref, g_ref)]
         lanes = [jnp.pad(x, ((0, PAD - cols), (0, 0))) for x in lanes]
         for b in range(blocks):
             pieces = [x[:, b * width : (b + 1) * width] for x in lanes]
             out_ref[b, q * PAD : (q + 1) * PAD, :] = jnp.concatenate(pieces, axis=1).astype(jnp.bfloat16)
-    table.wait()
 
 
 def lon_kernel(inner, place_ref, table_ref, *refs):
@@ -151,7 +157,7 @@
         for s, field in enumerate(fields):
             source = lax.rem(member - s + inner, inner)
             data = field[:, q * PAD : (q + 1) * PAD, :].reshape(blocks * PAD, lanes)
-            term = dot(table_ref[source], data)
+            term = dot(table_rows(table_ref, 0, 2 * modes, member * inner + source), data)
             total = term if total is None else total + term
         spec = total[:modes] + total[modes:]
         spec_ref[q] = spec
@@ -177,7 +183,7 @@
     return jnp.concatenate(rows, axis=0)
 
 
-def ready_kernel(pairs, place_ref, spec_ref, l_high, l_low, win_ref, bin_ref, wout_ref, *outs):
+def ready_kernel(pairs, start, place_ref, table_ref, spec_ref, win_ref, bin_ref, wout_ref, *outs):
     part_ref, form_ref, bias_ref = outs
     place, x = place_ref[0], place_ref[2]
     for n, ref in enumerate((win_ref, wout_ref)):
@@ -186,25 +192,29 @@
         form_ref[2 * n], form_ref[2 * n + 1] = split(form)
     bias = jnp.concatenate([bin_ref[0, pl.ds(place, 1), :], bin_ref[1, pl.ds(place, 1), :]], axis=1)
     bias_ref[...] = jnp.broadcast_to(bias, bias_ref.shape)
-    part_ref[...] = dot3((l_high[x], l_low[x]), split(lat_rows(spec_ref, pairs)))
-
-
-def mlp_kernel(lat, inner, pairs, scaling, place_ref, *refs):
+    rows = split(lat_rows(spec_ref, pairs))
+    part_ref[...] = dot3(lat_part(table_ref, start, part_ref.shape[0], rows[0].shape[0], x), rows)
+
+
+def mlp_kernel(lat, inner, pairs, start, scaling, place_ref, table_ref, *refs):
     others = refs[: lat - 1]
-    part_ref, form_ref, bias_ref, l_high, l_low, t_high, t_low = refs[lat - 1 : lat + 6]
-    back_ref, keep_ref, *rest = refs[lat + 6 :]
+    part_ref, form_ref, bias_ref = refs[lat - 1 : lat + 2]
+    back_ref, keep_ref, *rest = refs[lat + 2 :]
     send_refs, (w_ref,) = rest[: inner - 1], rest[inner - 1 :]
     member, x = place_ref[1], place_ref[2]
     wide = form_ref.shape[1]
     width = wide // 2
     tile = 2 * SUB
-    points = l_high.shape[1] // 2
+    size = part_ref.shape[0]
+    points = size // 2
+    part = size // lat
     subs = part_ref.shape[1] // wide
 
     spectra = part_ref[...]
     for s, ref in enumerate(others):
         source = lax.rem(x - s - 1 + lat, lat)
-        spectra = spectra + dot3((l_high[source], l_low[source]), split(lat_rows(ref, pairs)))
+        matrix = lat_part(table_ref, start, size, part, source)
+        spectra = spectra + dot3(matrix, split(lat_rows(ref, pairs)))
 
     def of_points(start):
         rows = []
@@ -230,7 +240,8 @@
     for n in range(subs):
         piece = grad_spec[n * points : (n + 1) * points]
         lanes.append(jnp.concatenate([piece[:, :width], piece[:, width:]], axis=0))
-    back = dot3((t_high[0], t_low[0]), split(jnp.concatenate(lanes, axis=1)))
+    matrix = lat_part(table_ref, start, size, part, x)
+    back = dot3(matrix, split(jnp.concatenate(lanes, axis=1)), ((0,), (0,)))
     for q in range(pairs):
         for n in range(subs):
             pieces = [
@@ -255,17 +266,19 @@
         send_refs[s - 1][...] = w_ref[lax.rem(member + s, inner)]
 
 
-def synth_kernel(inner, place_ref, high_ref, low_ref, *refs):
+def synth_kernel(inner, start, place_ref, table_ref, *refs):
     backs, sums, (out_ref, wide_ref) = refs[:inner], refs[inner : 2 * inner], refs[2 * inner :]
     member = place_ref[1]
     pairs, modes, lanes = backs[0].shape
     blocks, total_rows, wide = out_ref.shape
     data_rows = pairs * HALF
+    share = lanes // 2 // inner
     for q in range(pairs):
         total = None
         for s, back in enumerate(backs):
             source = lax.rem(member - s + inner, inner)
-            term = dot3((high_ref[0, source], low_ref[0, source]), split(back[q]))
+            rows = table_rows(table_ref, start, 2 * blocks * HALF, member * inner + source)
+            term = dot3((rows[:, :modes], rows[:, modes : 2 * modes]), split(back[q]))
             total = term if total is None else total + term
         part = blocks * HALF
         columns = jnp.concatenate([total[:part], total[part:]], axis=1)
@@ -276,28 +289,47 @@
 
     top_w = jnp.max(jnp.abs(weights), axis=0, keepdims=True)
     weights, level_w = scaled(weights, top_w)
-    columns = wide_ref[:, :data_rows, :]
+    columns = wide_ref[...]
     top = jnp.max(jnp.max(jnp.abs(columns), axis=0), axis=0, keepdims=True)
     columns, level = scaled(columns, top)
-    sum_rows = weights.shape[0]
-    place_row = lax.broadcasted_iota(jnp.int32, (sum_rows, 1), 0)
-    tail = jnp.where(place_row == sum_rows - 2, level_w, encode(weights).astype(jnp.float32))
-    tail = jnp.where(place_row == sum_rows - 1, level, tail)
+    coded_w = encode(weights).astype(jnp.float32)
+    bias = coded_w[share : share + 1, :lanes]
+    spare = (bias, level_w[:, :lanes], level_w[:, lanes:], level[:, :lanes], level[:, lanes:])
+    extra = []
+    for n in range(pairs):
+        row = jnp.zeros((1, lanes), jnp.float32) if n >= len(spare) else spare[n]
+        row = jnp.concatenate([jnp.zeros((1, lanes), jnp.float32), row], axis=1)
+        place_row = lax.broadcasted_iota(jnp.int32, (HALF, 1), 0)
+        extra.append(jnp.where(place_row == SPARE, row, 0.0))
+    extra = jnp.concatenate(extra, axis=0)
     coded = encode(columns).astype(jnp.float32)
+    tail = coded_w[: total_rows - data_rows]
     for b in range(blocks):
-        out_ref[b] = jnp.concatenate([coded[b], tail], axis=0).astype(jnp.bfloat16)
-
-
-def columns_kernel(place_ref, data_ref, cot_ref, out_ref):
+        out_ref[b] = jnp.concatenate([coded[b] + extra, tail], axis=0).astype(jnp.bfloat16)
+
+
+def spare_rows(raw, first, count):
+    lanes = raw.shape[1] // 2
+    rows = [raw[n * HALF + SPARE : n * HALF + SPARE + 1, lanes:] for n in range(first, first + count)]
+    return jnp.concatenate(rows, axis=1)
+
+
+def weight_rows(raw, data_rows):
+    level = spare_rows(raw, 1, 2) * (1.0 / TOP)
+    bias = decode(spare_rows(raw, 0, 1)) * level[:, : raw.shape[1] // 2]
+    return decode(raw[data_rows:]) * level, bias
+
+
+def columns_kernel(place_ref, data_ref, cot_ref, out_ref, held_ref, bias_ref):
     rows, cols, _ = cot_ref.shape
     blocks, total_rows, wide = data_ref.shape
     width = wide // 4
     pairs = rows // 2
-    top = -(-pairs * HALF // 16) * 16
     values = []
     for b in range(blocks):
-        level = data_ref[b, total_rows - 16 :, :].astype(jnp.float32)[15:16]
-        values.append(decode(data_ref[b, :top, :]) * (level * (1.0 / TOP)))
+        raw = data_ref[b].astype(jnp.float32)
+        values.append(decode(raw[: pairs * HALF]) * (spare_rows(raw, 3, 2) * (1.0 / TOP)))
+        held_ref[b], bias_ref[b : b + 1, :] = weight_rows(raw, pairs * HALF)
     for q in range(pairs):
         for h in range(2):
             parts = []
@@ -310,29 +342,27 @@
             out_ref[row] = (cot_ref[row].astype(jnp.float32) + column).astype(jnp.bfloat16)
 
 
-def weights_kernel(inner, data_rows, place_ref, *refs):
-    pieces, (win_ref, bin_ref, wout_ref) = refs[:inner], refs[inner:]
+def weights_kernel(inner, share, place_ref, held_ref, own_bias_ref, *refs):
+    pieces, (win_ref, bin_ref, wout_ref) = refs[: inner - 1], refs[inner - 1 :]
     member = place_ref[1]
-    blocks, total_rows, wide = pieces[0].shape
+    blocks, rows, wide = held_ref.shape
     width = wide // 4
-    share = width // inner
-    base = data_rows // 16 * 16
-    skip = data_rows - base
+    data_rows = pieces[0].shape[1] - rows
     for b in range(blocks):
-        held = []
-        for ref in pieces:
-            raw = ref[b, base:, :]
-            level = raw.astype(jnp.float32)[total_rows - base - 2 : total_rows - base - 1]
-            held.append(decode(raw)[skip:] * (level * (1.0 / TOP)))
+        held = [(held_ref[b], own_bias_ref[b : b + 1, :])]
+        held += [weight_rows(ref[b].astype(jnp.float32), data_rows) for ref in pieces]
         for n in range(inner):
-            part = held[0]
+            part, bias = held[0]
             for s in range(1, inner):
-                part = jnp.where(lax.rem(member - s + inner, inner) == n, held[s], part)
-            for i, (ref, k) in enumerate(((win_ref, 0), (win_ref, 1), (wout_ref, 0), (wout_ref, 1))):
-                ref[k, b, n * share : (n + 1) * share, :] = part[:share, i * width : (i + 1) * width]
+                chosen = lax.rem(member - s + inner, inner) == n
+                part = jnp.where(chosen, held[s][0], part)
+                bias = jnp.where(chosen, held[s][1], bias)
+            for i in range(4):
+                target = (win_ref, wout_ref)[i // 2]
+                target[i % 2, b, n * share : (n + 1) * share, :] = part[:share, i * width : (i + 1) * width]
             if n == 0:
                 for k in range(2):
-                    bin_ref[k, b : b + 1, :] = part[share : share + 1, k * width : (k + 1) * width]
+                    bin_ref[k, b : b + 1, :] = bias[:, k * width : (k + 1) * width]
 
 
 def body(features, cotangent, weight_in, bias_in, weight_out):
@@ -349,13 +379,10 @@
     lat_place = lax.axis_index("lat")
     scalars = jnp.stack([lon_place // inner, lon_place % inner, lat_place]).astype(jnp.int32)
     scaling = (rows * lat_count * modes // 2 * inner) ** -0.5
-    forward, synth_high, synth_low = lon_tables(blocks, inner, cols)
-    table = lat_table(rows, lat_count, SUB)
-    l_high, l_low = halves(table.reshape(size, lat_count, -1).transpose(1, 0, 2))
-    t_high, t_low = halves(table.T.reshape(lat_count, size // lat_count, size))
+    tables, (lon_start, lat_start, synth_start, _) = all_tables(blocks, inner, cols, rows, lat_count)
     share = width // inner
-    total_rows = -(-(pairs * HALF + share + 1 + 2) // 16) * 16
-    sum_rows = total_rows - pairs * HALF
+    total_rows = pairs * HALF + -(-share // 8) * 8
+    sum_rows = -(-(share + 1) // 8) * 8
     f32, bf16 = jnp.float32, jnp.bfloat16
     shape = jax.ShapeDtypeStruct
 
@@ -373,72 +400,68 @@
     def to_lat(values, step):
         return lax.ppermute(values, "lat", [(i, (i + step) % lat_count) for i in range(lat_count)])
 
-    def member_block(array):
-        rest = array.shape[1:]
-        return pl.BlockSpec((1, *rest), lambda i, s: (s[1],) + (0,) * len(rest))
-
-    in_hbm = pl.BlockSpec(memory_space=pltpu.HBM)
-    field = pltpu.VMEM(features.shape, bf16)
-    packed, lon_part = call(
+    (packed,) = call(
         functools.partial(pack_kernel, width),
         scalars,
-        (features, cotangent, forward),
-        (shape((blocks, pairs * PAD, wide), bf16), shape(forward.shape[1:], bf16)),
-        specs={0: in_hbm, 1: in_hbm, 2: in_hbm},
-        scratch=(field, field, pltpu.SemaphoreType.DMA((2, pairs)), pltpu.SemaphoreType.DMA(())),
+        (features, cotangent),
+        (shape((blocks, pairs * PAD, wide), bf16),),
     )
     arrived = exchange(packed)
     fields = [arrived] + [to_member(arrived, s) for s in range(1, inner)]
     (coded,) = call(
         functools.partial(lon_kernel, inner),
         scalars,
-        (lon_part, *fields),
+        (tables, *fields),
         (shape((pairs * modes + PAD, wide), bf16),),
         scratch=(pltpu.VMEM((pairs, modes, wide), f32),),
     )
     others = [to_lat(coded, s) for s in range(1, lat_count)]
     block_spec = pl.BlockSpec((2, 1, width, width), lambda i, s: (0, s[0], 0, 0))
     part, forms, bias = call(
-        functools.partial(ready_kernel, pairs),
-        scalars,
-        (coded, l_high, l_low, weight_in, bias_in, weight_out),
+        functools.partial(ready_kernel, pairs, lat_start),
+        scalars,
+        (tables, coded, weight_in, bias_in, weight_out),
         (
             shape((size, 2 * subs * width), f32),
             shape((4, 2 * width, 2 * width), bf16),
             shape((8, 2 * width), f32),
         ),
-        specs={3: block_spec, 5: block_spec},
+        specs={2: block_spec, 4: block_spec},
         flops=6 * size * size // lat_count * 2 * subs * width,
     )
-    n = lat_count - 1
-    lat_block = pl.BlockSpec((1, *t_high.shape[1:]), lambda i, s: (s[2], 0, 0))
     back, keep, *send = call(
-        functools.partial(mlp_kernel, lat_count, inner, pairs, scaling),
-        scalars,
-        (*others, part, forms, bias, l_high, l_low, t_high, t_low),
+        functools.partial(mlp_kernel, lat_count, inner, pairs, lat_start, scaling),
+        scalars,
+        (tables, *others, part, forms, bias),
         (shape((pairs, modes, 2 * width), f32), *[shape((sum_rows, wide), f32)] * inner),
-        specs={n + 5: lat_block, n + 6: lat_block},
         scratch=(pltpu.VMEM((inner, sum_rows, wide), f32),),
     )
     backs = [back] + [to_member(back, s) for s in range(1, inner)]
     sums = [keep] + [to_member(send[s - 1], s) for s in range(1, inner)]
     (payload,) = call(
-        functools.partial(synth_kernel, inner),
-        scalars,
-        (synth_high, synth_low, *backs, *sums),
+        functools.partial(synth_kernel, inner, synth_start),
+        scalars,
+        (tables, *backs, *sums),
         (shape((blocks, total_rows, wide), bf16),),
-        specs={0: member_block(synth_high), 1: member_block(synth_low)},
         scratch=(pltpu.VMEM((blocks, pairs * HALF, wide), f32),),
     )
     returned = exchange(payload)
-    gathered = [returned] + [to_member(returned, s) for s in range(1, inner)]
-    (grad_features,) = call(
-        columns_kernel, scalars, (returned, cotangent), (shape(features.shape, bf16),)
+    gathered = [to_member(returned, s) for s in range(1, inner)]
+    weight_part = total_rows - pairs * HALF
+    grad_features, held, held_bias = call(
+        columns_kernel,
+        scalars,
+        (returned, cotangent),
+        (
+            shape(features.shape, bf16),
+            shape((blocks, weight_part, wide), f32),
+            shape((blocks, 2 * width), f32),
+        ),
     )
     grad_w_in, grad_b_in, grad_w_out = call(
-        functools.partial(weights_kernel, inner, pairs * HALF),
-        scalars,
-        gathered,
+        functools.partial(weights_kernel, inner, share),
+        scalars,
+        (held, held_bias, *gathered),
         (shape(weight_in.shape, f32), shape(bias_in.shape, f32), shape(weight_out.shape, f32)),
     )
     return grad_features, grad_w_in, grad_b_in, grad_w_out

time: 70.1 us -> 67.7 us (0.966)
  local copies, waits for them, and re-layouts: 2.84 us -> 1.91 us
  blocking collectives: 41.4 us -> 40.5 us
    unnamed x26 -> x14, local copies, waits for them, and re-layouts: 2.84 us -> 1.91 us
    all_to_all x2, blocking collectives: 41.4 us -> 40.5 us  [exchange(): lax.all_to_all(values, 'lon', split_axis=0, concat_axis=0, tiled=True, ax...]
  transfers between devices with their start and end apart: 5 -> 5, of which waited for: 4 -> 3; matrix products, arithmetic and copies ran while one was open for 0% -> 0% of each run, Pallas kernels for 4% -> 5%
where the time goes in v2:
time: 67.7 us; the launch traced here: 67.4 us
  blocking collectives  40.5 us (60%)
  Pallas kernels  13.5 us (20%)
  waiting for transfers between devices  8.59 us (13%)
  starting transfers between devices  2.13 us (3%)
  local copies, waits for them, and re-layouts  1.91 us (3%)
  between operations  0.72 us (1%)
    all_to_all x2, blocking collectives, exchange(): lax.all_to_all(values, 'lon', split_axis=0, concat_axis=0, tiled=True, ax...  40.5 us
    pallas_call x7, Pallas kernels, call(): pl.pallas_call(kernel, grid_spec=pltpu.PrefetchScalarGridSpec(num_scalar_...  13.5 us
    ppermute x1, waiting for transfers between devices, to_lat(): lax.ppermute(values, 'lat', [(i, (i + step) % lat_count) for i in range(l...  5.49 us
    ppermute x4, waiting for transfers between devices, to_member(): return lax.ppermute(values, 'lon', turn)  3.1 us
    unnamed x14, local copies, waits for them, and re-layouts  1.91 us
    ppermute x1, starting transfers between devices, to_lat(): lax.ppermute(values, 'lat', [(i, (i + step) % lat_count) for i in range(l...  1.56 us
  transfers between devices with their start and end apart: 5, of which 3 were waited for; matrix products, arithmetic and copies ran while one was open for 0% of the time, Pallas kernels for 5%

profile of v2, /device:TPU:0, one launch (start us, length us, event | category | flops | bytes accessed | tf_op | source)
XLA Modules:
  0.0 67.4 jit_solution(3421176503224635597)
XLA Ops:
  0.6 0.1 pad_add_fusion.place_ref
  0.7 0.0 copy-start.1
  0.7 0.9 %copy-done.1 = bf16[10,14,768]{2,1,0:T(8,128)(2,1)S(1)} copy-done((bf16[10,14,768]{2,1,0:T(8,128)(2,1)S(1)}, bf16[10,14,768]{2,1,0:T(8,128)(2,1)}, u32[]{:S(2)}) %copy-start.1) | copy-done | bytes 215064
  1.7 0.0 copy-start.5
  1.7 0.9 %copy-done.5 = bf16[10,14,768]{2,1,0:T(8,128)(2,1)S(1)} copy-done((bf16[10,14,768]{2,1,0:T(8,128)(2,1)S(1)}, bf16[10,14,768]{2,1,0:T(8,128)(2,1)}, u32[]{:S(2)}) %copy-start.5) | copy-done | bytes 215064
  2.6 0.8 %shard_map.93 = bf16[8,80,384]{2,1,0:T(8,128)(2,1)S(1)} custom-call(s32[3]{0:T(128)S(1)} %pad_add_fusion.place_ref, bf16[10,14,768]{2,1,0:T(8,128)(2,1)S(1)} %copy-done.5, bf16[10,14,768]{2,1,0:T(8,128)(2,1)S(1)} %copy-done.1), custom_call_target="tpu_custom_call" | custom-call | bytes 921600 | tf_op jit(solution)/shard_map/pallas_call | solution.py:122
  3.4 0.0 copy-start
  3.4 21.0 %all_to_all.10.refs_0_ = bf16[8,80,384]{2,1,0:T(8,128)(2,1)S(1)} all-to-all(bf16[8,80,384]{2,1,0:T(8,128)(2,1)S(1)} %shard_map.93), channel_id=1, replica_groups={{0,4,8,12,16,20,24,28},{2,6,10,14,18,22,26,30},{1,5,9,13,17,21,25,29},{..., dimensions={0} | all-to-all | bytes 983040 | tf_op jit(solution)/shard_map/all_to_all | solution.py:392
  24.5 0.0 copy-start.3
  24.5 0.0 collective-permute-start
  24.5 1.9 %collective-permute-done.refs_1_ = bf16[8,80,384]{2,1,0:T(8,128)(2,1)S(1)} collective-permute-done((bf16[8,80,384]{2,1,0:T(8,128)(2,1)S(1)}, bf16[8,80,384]{2,1,0:T(8,128)(2,1)S(1)}, u32[]{:S(2)}, u32[]{:S(2)}) %collective-permute-start) | collective-permute-done | bytes 491552 | tf_op jit(solution)/shard_map/ppermute | solution.py:398
  26.4 0.0 copy-done
  26.4 1.1 %shard_map.94.spec_ref = bf16[336,384]{1,0:T(8,128)(2,1)S(1)} custom-call(s32[3]{0:T(128)S(1)} %pad_add_fusion.place_ref, bf16[1664,128]{1,0:T(8,128)(2,1)S(1)} %copy-done, bf16[8,80,384]{2,1,0:T(8,128)(2,1)S(1)} %all_to_all.10.refs_0_, bf16[8,80,384]{2,1,0:T(8,128)(2,1)S(1)} %collective-permute-done.refs_1_), custom_call_target="tpu_custom_call" | custom-call | bytes 1667072 | tf_op jit(solution)/shard_map/pallas_call | solution.py:122
  27.5 1.6 %collective-permute-start.1 = (bf16[336,384]{1,0:T(8,128)(2,1)S(1)}, bf16[336,384]{1,0:T(8,128)(2,1)S(1)}, u32[]{:S(2)}, u32[]{:S(2)}) collective-permute-start(bf16[336,384]{1,0:T(8,128)(2,1)S(1)} %shard_map.94.spec_ref), channel_id=1, source_target_pairs={{0,1},{1,0},{2,3},{3,2},{4,5},{5,4},{6,7},{7,6},{8,9},{9,8},{10,11... | collective-permute-start | bytes 774152 | tf_op jit(solution)/shard_map/ppermute | solution.py:401
  29.0 0.0 copy-done.3
  29.0 0.0 copy-done.4
  29.0 0.0 copy-done.6
  29.0 1.3 %shard_map.95 = (f32[160,1536]{1,0:T(8,128)S(1)}, bf16[4,192,192]{2,1,0:T(8,128)(2,1)S(1)}, f32[8,192]{1,0:T(8,128)S(1)}) custom-call(s32[3]{0:T(128)S(1)} %pad_add_fusion.place_ref, bf16[1664,128]{1,0:T(8,128)(2,1)S(1)} %copy-done, bf16[336,384]{1,0:T(8,128)(2,1)S(1)} %shard_map.94.spec_ref, f32[2,8,96,96]{3,2,1,0:T(8,128)S(1)} %copy-done.3, ...), custom_call_target="tpu_custom_call" | custom-call | flops 117964800 | bytes 3153920 | tf_op jit(solution)/shard_map/pallas_call | solution.py:122
  30.3 5.5 %collective-permute-done.1.refs_0_ = bf16[336,384]{1,0:T(8,128)(2,1)S(1)} collective-permute-done((bf16[336,384]{1,0:T(8,128)(2,1)S(1)}, bf16[336,384]{1,0:T(8,128)(2,1)S(1)}, u32[]{:S(2)}, u32[]{:S(2)}) %collective-permute-start.1) | collective-permute-done | bytes 258080 | tf_op jit(solution)/shard_map/ppermute | solution.py:401
  35.8 3.9 %shard_map.96 = (f32[5,64,192]{2,1,0:T(8,128)S(1)}, f32[56,384]{1,0:T(8,128)S(1)}, f32[56,384]{1,0:T(8,128)S(1)}) custom-call(s32[3]{0:T(128)S(1)} %pad_add_fusion.place_ref, bf16[1664,128]{1,0:T(8,128)(2,1)S(1)} %copy-done, bf16[336,384]{1,0:T(8,128)(2,1)S(1)} %collective-permute-done.1.refs_0_, f32[160,1536]{1,0:T(8,128)S(1)} %get-tuple-element.16.refs_1_, ...), custom_call_target="tpu_custom_call" | custom-call | bytes 2385920 | tf_op jit(solution)/shard_map/pallas_call | solution.py:122
  39.7 0.1 collective-permute-start.2
  39.8 0.5 collective-permute-start.3
  40.3 1.2 %collective-permute-done.3.refs_3_ = f32[56,384]{1,0:T(8,128)S(1)} collective-permute-done((f32[56,384]{1,0:T(8,128)S(1)}, f32[56,384]{1,0:T(8,128)S(1)}, u32[]{:S(2)}, u32[]{:S(2)}) %collective-permute-start.3) | collective-permute-done | bytes 86048 | tf_op jit(solution)/shard_map/ppermute | solution.py:398
  41.5 0.0 collective-permute-done.2.refs_1_
  41.5 1.5 %shard_map.97 = bf16[8,88,384]{2,1,0:T(8,128)(2,1)S(1)} custom-call(s32[3]{0:T(128)S(1)} %pad_add_fusion.place_ref, bf16[1664,128]{1,0:T(8,128)(2,1)S(1)} %copy-done, f32[5,64,192]{2,1,0:T(8,128)S(1)} %get-tuple-element.19.refs_0_, f32[5,64,192]{2,1,0:T(8,128)S(1)} %collective-permute-done.2.refs_1_, f32[56,384]{1,0:T(8,128)S(1)} %get-tuple-element.20.refs_2_, ...), custom_call_target="tpu_custom_call" | custom-call | bytes 1630208 | tf_op jit(solution)/shard_map/pallas_call | solution.py:122
  43.0 0.0 copy-start.2
  43.1 19.5 %all_to_all.11.data_ref = bf16[8,88,384]{2,1,0:T(8,128)(2,1)S(1)} all-to-all(bf16[8,88,384]{2,1,0:T(8,128)(2,1)S(1)} %shard_map.97), channel_id=1, replica_groups={{0,4,8,12,16,20,24,28},{2,6,10,14,18,22,26,30},{1,5,9,13,17,21,25,29},{..., dimensions={0} | all-to-all | bytes 1081344 | tf_op jit(solution)/shard_map/all_to_all | solution.py:392
  62.5 0.0 collective-permute-start.4
  62.5 0.0 copy-done.2
  62.6 1.9 %shard_map.98 = (bf16[10,14,768]{2,1,0:T(8,128)(2,1)}, f32[8,48,384]{2,1,0:T(8,128)S(1)}, f32[8,192]{1,0:T(8,128)S(1)}) custom-call(s32[3]{0:T(128)S(1)} %pad_add_fusion.place_ref, bf16[8,88,384]{2,1,0:T(8,128)(2,1)S(1)} %all_to_all.11.data_ref, bf16[10,14,768]{2,1,0:T(8,128)(2,1)S(1)} %copy-done.2), custom_call_target="tpu_custom_call" | custom-call | bytes 1566720 | tf_op jit(solution)/shard_map/pallas_call | solution.py:122
  64.5 0.0 collective-permute-done.4.refs_0_
  64.5 2.9 %shard_map.99 = (f32[2,8,96,96]{3,2,1,0:T(8,128)}, f32[2,8,96]{2,1,0:T(8,128)}, f32[2,8,96,96]{3,2,1,0:T(8,128)}) custom-call(s32[3]{0:T(128)S(1)} %pad_add_fusion.place_ref, f32[8,48,384]{2,1,0:T(8,128)S(1)} %get-tuple-element.23.held_ref, f32[8,192]{1,0:T(8,128)S(1)} %get-tuple-element.24.own_bias_ref, bf16[8,88,384]{2,1,0:T(8,128)(2,1)S(1)} %collective-permute-done.4.refs_0_), custom_call_target="tpu_custom_call" | custom-call | bytes 2322432 | tf_op jit(solution)/shard_map/pallas_call | solution.py:122
  (2 shorter events, 0.0 us)
Async XLA Ops:
  0.7 0.9 %copy-start.1 = (bf16[10,14,768]{2,1,0:T(8,128)(2,1)S(1)}, bf16[10,14,768]{2,1,0:T(8,128)(2,1)}, u32[]{:S(2)}) copy-start(bf16[10,14,768]{2,1,0:T(8,128)(2,1)} %cot_ref.1) | copy-start | bytes 645124
  1.7 0.9 %copy-start.5 = (bf16[10,14,768]{2,1,0:T(8,128)(2,1)S(1)}, bf16[10,14,768]{2,1,0:T(8,128)(2,1)}, u32[]{:S(2)}) copy-start(bf16[10,14,768]{2,1,0:T(8,128)(2,1)} %x_ref.1) | copy-start | bytes 645124
  3.4 22.9 %copy-start = (bf16[1664,128]{1,0:T(8,128)(2,1)S(1)}, bf16[1664,128]{1,0:T(8,128)(2,1)}, u32[]{:S(2)}) copy-start(bf16[1664,128]{1,0:T(8,128)(2,1)} %constant.34.clone.table_ref) | copy-start | bytes 1277956
  24.5 4.6 %copy-start.3 = (f32[2,8,96,96]{3,2,1,0:T(8,128)S(1)}, f32[2,8,96,96]{3,2,1,0:T(8,128)}, u32[]{:S(2)}) copy-start(f32[2,8,96,96]{3,2,1,0:T(8,128)} %win_ref.1) | copy-start | bytes 1769476
  24.5 4.6 %copy-start.4 = (f32[2,8,96,96]{3,2,1,0:T(8,128)S(1)}, f32[2,8,96,96]{3,2,1,0:T(8,128)}, u32[]{:S(2)}) copy-start(f32[2,8,96,96]{3,2,1,0:T(8,128)} %wout_ref.1) | copy-start | bytes 1769476
  24.5 4.6 %copy-start.6 = (f32[2,8,96]{2,1,0:T(8,128)S(1)}, f32[2,8,96]{2,1,0:T(8,128)}, u32[]{:S(2)}) copy-start(f32[2,8,96]{2,1,0:T(8,128)} %bin_ref.1) | copy-start | bytes 18436
  24.5 1.9 %collective-permute-start = (bf16[8,80,384]{2,1,0:T(8,128)(2,1)S(1)}, bf16[8,80,384]{2,1,0:T(8,128)(2,1)S(1)}, u32[]{:S(2)}, u32[]{:S(2)}) collective-permute-start(bf16[8,80,384]{2,1,0:T(8,128)(2,1)S(1)} %all_to_all.10.refs_0_), channel_id=1, source_target_pairs={{0,2},{2,0},{4,6},{6,4},{8,10},{10,8},{12,14},{14,12},{16,18},{18,... | collective-permute-start | bytes 1474568 | tf_op jit(solution)/shard_map/ppermute | solution.py:398
  27.5 8.3 %collective-permute-start.1 = (bf16[336,384]{1,0:T(8,128)(2,1)S(1)}, bf16[336,384]{1,0:T(8,128)(2,1)S(1)}, u32[]{:S(2)}, u32[]{:S(2)}) collective-permute-start(bf16[336,384]{1,0:T(8,128)(2,1)S(1)} %shard_map.94.spec_ref), channel_id=1, source_target_pairs={{0,1},{1,0},{2,3},{3,2},{4,5},{5,4},{6,7},{7,6},{8,9},{9,8},{10,11... | collective-permute-start | bytes 774152 | tf_op jit(solution)/shard_map/ppermute | solution.py:401
  39.7 1.8 %collective-permute-start.2 = (f32[5,64,192]{2,1,0:T(8,128)S(1)}, f32[5,64,192]{2,1,0:T(8,128)S(1)}, u32[]{:S(2)}, u32[]{:S(2)}) collective-permute-start(f32[5,64,192]{2,1,0:T(8,128)S(1)} %get-tuple-element.19.refs_0_), channel_id=1, source_target_pairs={{0,2},{2,0},{4,6},{6,4},{8,10},{10,8},{12,14},{14,12},{16,18},{18,... | collective-permute-start | bytes 737288 | tf_op jit(solution)/shard_map/ppermute | solution.py:398
  39.8 1.7 %collective-permute-start.3 = (f32[56,384]{1,0:T(8,128)S(1)}, f32[56,384]{1,0:T(8,128)S(1)}, u32[]{:S(2)}, u32[]{:S(2)}) collective-permute-start(f32[56,384]{1,0:T(8,128)S(1)} %get-tuple-element.21), channel_id=1, source_target_pairs={{0,2},{2,0},{4,6},{6,4},{8,10},{10,8},{12,14},{14,12},{16,18},{18,... | collective-permute-start | bytes 258056 | tf_op jit(solution)/shard_map/ppermute | solution.py:398
  43.0 19.5 %copy-start.2 = (bf16[10,14,768]{2,1,0:T(8,128)(2,1)S(1)}, bf16[10,14,768]{2,1,0:T(8,128)(2,1)}, u32[]{:S(2)}) copy-start(bf16[10,14,768]{2,1,0:T(8,128)(2,1)} %cot_ref.1) | copy-start | bytes 645124
  62.5 1.9 %collective-permute-start.4 = (bf16[8,88,384]{2,1,0:T(8,128)(2,1)S(1)}, bf16[8,88,384]{2,1,0:T(8,128)(2,1)S(1)}, u32[]{:S(2)}, u32[]{:S(2)}) collective-permute-start(bf16[8,88,384]{2,1,0:T(8,128)(2,1)S(1)} %all_to_all.11.data_ref), channel_id=1, source_target_pairs={{0,2},{2,0},{4,6},{6,4},{8,10},{10,8},{12,14},{14,12},{16,18},{18,... | collective-permute-start | bytes 1622024 | tf_op jit(solution)/shard_map/ppermute | solution.py:398

commit v3 on v2

--- a/solution.py
+++ b/solution.py
@@ -13,6 +13,7 @@
 MODE_DEV = 4
 PAD = 16
 HALF = PAD // 2
+BASES = (4, 6, 2)
 SUB = 4
 SPARE = 6
 POWER = 13.0
@@ -47,6 +48,24 @@
     synth = split.transpose(1, 4, 2, 0, 3, 5).reshape(inner, inner, 2 * blocks * HALF, 2 * modes)
     forward, synth = np.concatenate(halves(forward), axis=2), np.concatenate(halves(synth), axis=3)
     return forward.reshape(-1, blocks * PAD), synth.reshape(-1, 4 * modes)
+
+
+def served(member):
+    return [(0, member), (1, member)] + [(base + member, m) for base in BASES for m in range(2)]
+
+
+def served_table(blocks, cols):
+    modes = 2 * MODE_DEV * blocks
+    table = lon_table(blocks * 2 * cols, modes).reshape(blocks, 2, cols, 2, modes)
+    table = np.pad(table, ((0, 0), (0, 0), (0, PAD - cols), (0, 0), (0, 0)))
+    whole = []
+    for place in range(blocks):
+        for member in range(2):
+            rows = np.stack([table[place ^ k, m] for k, m in served(member)])
+            rows = np.stack([rows[:, :, member], rows[:, :, 1 - member]], axis=2)
+            rows = rows.reshape(len(rows), 2, HALF, 2 * modes).transpose(1, 0, 2, 3)
+            whole.append(np.concatenate(halves(rows.reshape(-1, 2 * modes)), axis=1))
+    return np.stack(whole).reshape(blocks, 2, *whole[0].shape)
 
 
 def lat_table(rows, lat_count, group):
@@ -196,11 +215,11 @@
     part_ref[...] = dot3(lat_part(table_ref, start, part_ref.shape[0], rows[0].shape[0], x), rows)
 
 
-def mlp_kernel(lat, inner, pairs, start, scaling, place_ref, table_ref, *refs):
+def mlp_kernel(lat, inner, shares, pairs, start, scaling, place_ref, table_ref, *refs):
     others = refs[: lat - 1]
     part_ref, form_ref, bias_ref = refs[lat - 1 : lat + 2]
     back_ref, keep_ref, *rest = refs[lat + 2 :]
-    send_refs, (w_ref,) = rest[: inner - 1], rest[inner - 1 :]
+    send_refs, (w_ref,) = rest[: shares - 1], rest[shares - 1 :]
     member, x = place_ref[1], place_ref[2]
     wide = form_ref.shape[1]
     width = wide // 2
@@ -256,14 +275,17 @@
         pieces.append(total[:width, :width] + total[width:, width:])
         pieces.append(total[:width, width:] - total[width:, :width])
     weights = jnp.concatenate(pieces, axis=1) * scaling
-    share = width // inner
+    share = width // shares
     w_ref[...] = jnp.zeros_like(w_ref)
-    for n in range(inner):
+    for n in range(shares):
         w_ref[n, :share, :] = weights[n * share : (n + 1) * share]
     w_ref[0, share : share + 1, :wide] = jnp.sum(grad_pre, axis=0, keepdims=True) * scaling
+    if shares == 1:
+        keep_ref[...] = w_ref[0]
+        return
     keep_ref[...] = w_ref[member]
-    for s in range(1, inner):
-        send_refs[s - 1][...] = w_ref[lax.rem(member + s, inner)]
+    for s in range(1, shares):
+        send_refs[s - 1][...] = w_ref[lax.rem(member + s, shares)]
 
 
 def synth_kernel(inner, start, place_ref, table_ref, *refs):
@@ -286,26 +308,104 @@
     weights = sums[0][...]
     for ref in sums[1:]:
         weights = weights + ref[...]
-
-    top_w = jnp.max(jnp.abs(weights), axis=0, keepdims=True)
-    weights, level_w = scaled(weights, top_w)
-    columns = wide_ref[...]
+    coded, tail = code_all(wide_ref[...], weights, share)
+    tail = tail[: total_rows - data_rows]
+    for b in range(blocks):
+        out_ref[b] = jnp.concatenate([coded[b], tail], axis=0).astype(jnp.bfloat16)
+
+
+def code_all(columns, weights, share):
+    rows, wide = columns.shape[1:]
+    lanes = wide // 2
+    weights, level_w = scaled(weights, jnp.max(jnp.abs(weights), axis=0, keepdims=True))
     top = jnp.max(jnp.max(jnp.abs(columns), axis=0), axis=0, keepdims=True)
     columns, level = scaled(columns, top)
-    coded_w = encode(weights).astype(jnp.float32)
-    bias = coded_w[share : share + 1, :lanes]
+    tail = encode(weights).astype(jnp.float32)
+    bias = tail[share : share + 1, :lanes]
     spare = (bias, level_w[:, :lanes], level_w[:, lanes:], level[:, :lanes], level[:, lanes:])
     extra = []
-    for n in range(pairs):
+    for n in range(rows // HALF):
         row = jnp.zeros((1, lanes), jnp.float32) if n >= len(spare) else spare[n]
         row = jnp.concatenate([jnp.zeros((1, lanes), jnp.float32), row], axis=1)
         place_row = lax.broadcasted_iota(jnp.int32, (HALF, 1), 0)
         extra.append(jnp.where(place_row == SPARE, row, 0.0))
     extra = jnp.concatenate(extra, axis=0)
-    coded = encode(columns).astype(jnp.float32)
-    tail = coded_w[: total_rows - data_rows]
-    for b in range(blocks):
-        out_ref[b] = jnp.concatenate([coded[b] + extra, tail], axis=0).astype(jnp.bfloat16)
+    return encode(columns).astype(jnp.float32) + extra, tail
+
+
+def serve_kernel(place_ref, table_ref, own_ref, other_ref, sum_ref, more_ref, *refs):
+    outs, wide_ref = refs[:-1], refs[-1]
+    pairs, modes, lanes = own_ref.shape
+    count = wide_ref.shape[0]
+    share = lanes // 2
+    table = table_ref[0, 0]
+    matrix = (table[:, : 2 * modes], table[:, 2 * modes :])
+    for q in range(pairs):
+        total = dot3(matrix, split(jnp.concatenate([own_ref[q], other_ref[q]], axis=0)))
+        part = count * HALF
+        columns = jnp.concatenate([total[:part], total[part:]], axis=1)
+        wide_ref[:, q * HALF : (q + 1) * HALF, :] = columns.reshape(count, HALF, 2 * lanes)
+    coded, tail = code_all(wide_ref[...], sum_ref[...] + more_ref[...], share)
+    tail = tail[:share]
+    for n, ref in enumerate(outs):
+        parts = [coded[n]] if n < 2 else [coded[2 * n - 2], coded[2 * n - 1]]
+        ref[...] = jnp.concatenate([*parts, tail], axis=0).astype(jnp.bfloat16)
+
+
+def arrived(ref, member, data_rows):
+    raw = ref[...].astype(jnp.float32)
+    level = spare_rows(raw, 3, 2) * (1.0 / TOP)
+    columns = raw[:data_rows]
+    start = data_rows
+    if raw.shape[0] == 2 * data_rows + raw.shape[1] // 4:
+        start = 2 * data_rows
+        columns = jnp.where(member == 0, columns, raw[data_rows:start])
+    weights, bias = weight_rows(raw, start)
+    return decode(columns) * level, weights, bias
+
+
+def first_kernel(data_rows, place_ref, *refs):
+    member = place_ref[1]
+    count = len(refs) - 3
+    columns_ref, weights_ref, bias_ref = refs[count:]
+    for n in range(count):
+        columns_ref[n], weights_ref[n], bias_ref[n : n + 1, :] = arrived(refs[n], member, data_rows)
+
+
+def last_kernel(data_rows, place_ref, columns_ref, weights_ref, bias_ref, cot_ref, *refs):
+    place, member = place_ref[0], place_ref[1]
+    lates = refs[: len(BASES)]
+    out_ref, win_ref, bin_ref, wout_ref, held_ref = refs[len(BASES) :]
+    rows, cols, _ = cot_ref.shape
+    blocks = win_ref.shape[1]
+    width = win_ref.shape[2]
+    pairs = rows // 2
+
+    def settle(source, columns, weights, bias):
+        held_ref[source] = columns
+        for i in range(4):
+            target = (win_ref, wout_ref)[i // 2]
+            target[i % 2, source] = weights[:, i * width : (i + 1) * width]
+        for k in range(2):
+            bin_ref[k, pl.ds(source, 1), :] = bias[:, k * width : (k + 1) * width]
+
+    for n, base in enumerate((0, 1) + BASES):
+        source = place ^ (base + member) if n >= 2 else place ^ base
+        settle(source, columns_ref[n], weights_ref[n], bias_ref[n : n + 1, :])
+    for ref, base in zip(lates, BASES):
+        settle(place ^ (base + 1 - member), *arrived(ref, member, data_rows))
+    for q in range(pairs):
+        for h in range(2):
+            parts = []
+            for half in range(2):
+                start = (2 * half + h) * width
+                pieces = [
+                    held_ref[b, q * HALF : (q + 1) * HALF, :][:, start : start + width] for b in range(blocks)
+                ]
+                parts.append(jnp.concatenate(pieces, axis=1))
+            column = jnp.concatenate(parts, axis=0)[:cols]
+            row = 2 * q + h
+            out_ref[row] = (cot_ref[row].astype(jnp.float32) + column).astype(jnp.bfloat16)
 
 
 def spare_rows(raw, first, count):
@@ -380,8 +480,11 @@
     scalars = jnp.stack([lon_place // inner, lon_place % inner, lat_place]).astype(jnp.int32)
     scaling = (rows * lat_count * modes // 2 * inner) ** -0.5
     tables, (lon_start, lat_start, synth_start, _) = all_tables(blocks, inner, cols, rows, lat_count)
-    share = width // inner
-    total_rows = pairs * HALF + -(-share // 8) * 8
+    paired = inner == 2 and blocks == 2 + 2 * len(BASES)
+    shares = 1 if paired else inner
+    share = width // shares
+    data_rows = pairs * HALF
+    total_rows = data_rows + -(-share // 8) * 8
     sum_rows = -(-(share + 1) // 8) * 8
     f32, bf16 = jnp.float32, jnp.bfloat16
     shape = jax.ShapeDtypeStruct
@@ -395,6 +498,10 @@
 
     def to_member(values, step):
         turn = [(i, i // inner * inner + (i + step) % inner) for i in range(lon_count)]
+        return lax.ppermute(values, "lon", turn)
+
+    def to_place(values, first, second):
+        turn = [(i, (i // 2 ^ (second if i % 2 else first)) * 2 + i % 2) for i in range(lon_count)]
         return lax.ppermute(values, "lon", turn)
 
     def to_lat(values, step):
@@ -430,13 +537,46 @@
         flops=6 * size * size // lat_count * 2 * subs * width,
     )
     back, keep, *send = call(
-        functools.partial(mlp_kernel, lat_count, inner, pairs, lat_start, scaling),
+        functools.partial(mlp_kernel, lat_count, inner, shares, pairs, lat_start, scaling),
         scalars,
         (tables, *others, part, forms, bias),
-        (shape((pairs, modes, 2 * width), f32), *[shape((sum_rows, wide), f32)] * inner),
-        scratch=(pltpu.VMEM((inner, sum_rows, wide), f32),),
+        (shape((pairs, modes, 2 * width), f32), *[shape((sum_rows, wide), f32)] * shares),
+        scratch=(pltpu.VMEM((shares, sum_rows, wide), f32),),
     )
     backs = [back] + [to_member(back, s) for s in range(1, inner)]
+    if paired:
+        table = served_table(blocks, cols)
+        count = table.shape[2] // PAD
+        outs = [share + data_rows] * 2 + [share + 2 * data_rows] * len(BASES)
+        own, side, *slots = call(
+            serve_kernel,
+            scalars,
+            (table, *backs, keep, to_member(keep, 1)),
+            [shape((n, wide), bf16) for n in outs],
+            specs={0: pl.BlockSpec((1, 1, *table.shape[2:]), lambda i, s: (s[0], s[1], 0, 0))},
+            scratch=(pltpu.VMEM((count, data_rows, wide), f32),),
+        )
+        sent = [to_place(x, base, base + 1) for x, base in zip(slots, BASES)]
+        side, sent[-1] = lax.optimization_barrier((to_place(side, 1, 1), sent[-1]))
+        firsts = [own, side, *sent]
+        late = [to_member(x, 1) for x in sent]
+        held = call(
+            functools.partial(first_kernel, data_rows),
+            scalars,
+            firsts,
+            (
+                shape((len(firsts), data_rows, wide), f32),
+                shape((len(firsts), share, wide), f32),
+                shape((len(firsts), 2 * width), f32),
+            ),
+        )
+        return call(
+            functools.partial(last_kernel, data_rows),
+            scalars,
+            (*held, cotangent, *late),
+            [shape(x.shape, x.dtype) for x in (features, weight_in, bias_in, weight_out)],
+            scratch=(pltpu.VMEM((blocks, data_rows, wide), f32),),
+        )
     sums = [keep] + [to_member(send[s - 1], s) for s in range(1, inner)]
     (payload,) = call(
         functools.partial(synth_kernel, inner, synth_start),

time: 67.7 us -> 62.3 us (0.920)
  blocking collectives: 40.5 us -> 21 us
  waiting for transfers between devices: 8.59 us -> 16.8 us
  starting transfers between devices: 2.13 us -> 8.9 us
  Pallas kernels: 13.5 us -> 12.2 us
    all_to_all x2 -> x1, blocking collectives: 40.5 us -> 21 us  [exchange(): lax.all_to_all(values, 'lon', split_axis=0, concat_axis=0, tiled=True, ax...]
    ppermute x0 -> x4, waiting for transfers between devices: none -> 8.09 us  [to_place(): return lax.ppermute(values, 'lon', turn)]
    ppermute x0 -> x4, starting transfers between devices: none -> 5.91 us  [to_place(): return lax.ppermute(values, 'lon', turn)]
    pallas_call x7, Pallas kernels: 13.5 us -> 12.2 us  [call(): pl.pallas_call(kernel, grid_spec=pltpu.PrefetchScalarGridSpec(num_scalar_...]
    ppermute x4 -> x6, starting transfers between devices: 0.57 us -> 1.43 us  [to_member(): return lax.ppermute(values, 'lon', turn)]
    ppermute x4 -> x6, waiting for transfers between devices: 3.1 us -> 3.21 us  [to_member(): return lax.ppermute(values, 'lon', turn)]
    unnamed x14 -> x16, local copies, waits for them, and re-layouts: 1.91 us -> 1.92 us
  transfers between devices with their start and end apart: 5 -> 11, of which waited for: 3 -> 5; matrix products, arithmetic and copies ran while one was open for 0% -> 0% of each run, Pallas kernels for 5% -> 4%
where the time goes in v3:
time: 62.3 us; the launch traced here: 61.7 us
  blocking collectives  21 us (34%)
  waiting for transfers between devices  16.8 us (27%)
  Pallas kernels  12.2 us (20%)
  starting transfers between devices  8.9 us (14%)
  local copies, waits for them, and re-layouts  1.92 us (3%)
  between operations  0.76 us (1%)
    all_to_all x1, blocking collectives, exchange(): lax.all_to_all(values, 'lon', split_axis=0, concat_axis=0, tiled=True, ax...  21 us
    pallas_call x7, Pallas kernels, call(): pl.pallas_call(kernel, grid_spec=pltpu.PrefetchScalarGridSpec(num_scalar_...  12.2 us
    ppermute x4, waiting for transfers between devices, to_place(): return lax.ppermute(values, 'lon', turn)  8.09 us
    ppermute x4, starting transfers between devices, to_place(): return lax.ppermute(values, 'lon', turn)  5.91 us
    ppermute x1, waiting for transfers between devices, to_lat(): lax.ppermute(values, 'lat', [(i, (i + step) % lat_count) for i in range(l...  5.48 us
    ppermute x6, waiting for transfers between devices, to_member(): return lax.ppermute(values, 'lon', turn)  3.21 us
    unnamed x16, local copies, waits for them, and re-layouts  1.92 us
    ppermute x1, starting transfers between devices, to_lat(): lax.ppermute(values, 'lat', [(i, (i + step) % lat_count) for i in range(l...  1.56 us
  transfers between devices with their start and end apart: 11, of which 5 were waited for; matrix products, arithmetic and copies ran while one was open for 0% of the time, Pallas kernels for 4%

profile of v3, /device:TPU:0, one launch (start us, length us, event | category | flops | bytes accessed | tf_op | source)
XLA Modules:
  0.0 61.7 jit_solution(14955582134817427449)
XLA Ops:
  0.6 0.1 pad_add_fusion.place_ref
  0.7 0.9 %copy-done.2 = bf16[10,14,768]{2,1,0:T(8,128)(2,1)S(1)} copy-done((bf16[10,14,768]{2,1,0:T(8,128)(2,1)S(1)}, bf16[10,14,768]{2,1,0:T(8,128)(2,1)}, u32[]{:S(2)}) %copy-start.2) | copy-done | bytes 215064
  1.7 0.9 %copy-done.6 = bf16[10,14,768]{2,1,0:T(8,128)(2,1)S(1)} copy-done((bf16[10,14,768]{2,1,0:T(8,128)(2,1)S(1)}, bf16[10,14,768]{2,1,0:T(8,128)(2,1)}, u32[]{:S(2)}) %copy-start.6) | copy-done | bytes 215064
  2.6 0.8 %shard_map.102 = bf16[8,80,384]{2,1,0:T(8,128)(2,1)S(1)} custom-call(s32[3]{0:T(128)S(1)} %pad_add_fusion.place_ref, bf16[10,14,768]{2,1,0:T(8,128)(2,1)S(1)} %copy-done.6, bf16[10,14,768]{2,1,0:T(8,128)(2,1)S(1)} %copy-done.2), custom_call_target="tpu_custom_call" | custom-call | bytes 921600 | tf_op jit(solution)/shard_map/pallas_call | solution.py:141
  3.4 0.0 copy-start
  3.4 21.0 %all_to_all.5.refs_0_ = bf16[8,80,384]{2,1,0:T(8,128)(2,1)S(1)} all-to-all(bf16[8,80,384]{2,1,0:T(8,128)(2,1)S(1)} %shard_map.102), channel_id=1, replica_groups={{0,4,8,12,16,20,24,28},{2,6,10,14,18,22,26,30},{1,5,9,13,17,21,25,29},{..., dimensions={0} | all-to-all | bytes 983040 | tf_op jit(solution)/shard_map/all_to_all | solution.py:495
  24.5 1.9 %collective-permute-done.refs_1_ = bf16[8,80,384]{2,1,0:T(8,128)(2,1)S(1)} collective-permute-done((bf16[8,80,384]{2,1,0:T(8,128)(2,1)S(1)}, bf16[8,80,384]{2,1,0:T(8,128)(2,1)S(1)}, u32[]{:S(2)}, u32[]{:S(2)}) %collective-permute-start) | collective-permute-done | bytes 491552 | tf_op jit(solution)/shard_map/ppermute | solution.py:501
  26.4 1.1 %shard_map.103.spec_ref = bf16[336,384]{1,0:T(8,128)(2,1)S(1)} custom-call(s32[3]{0:T(128)S(1)} %pad_add_fusion.place_ref, bf16[1664,128]{1,0:T(8,128)(2,1)S(1)} %copy-done, bf16[8,80,384]{2,1,0:T(8,128)(2,1)S(1)} %all_to_all.5.refs_0_, bf16[8,80,384]{2,1,0:T(8,128)(2,1)S(1)} %collective-permute-done.refs_1_), custom_call_target="tpu_custom_call" | custom-call | bytes 1667072 | tf_op jit(solution)/shard_map/pallas_call | solution.py:141
  27.5 1.6 %collective-permute-start.1 = (bf16[336,384]{1,0:T(8,128)(2,1)S(1)}, bf16[336,384]{1,0:T(8,128)(2,1)S(1)}, u32[]{:S(2)}, u32[]{:S(2)}) collective-permute-start(bf16[336,384]{1,0:T(8,128)(2,1)S(1)} %shard_map.103.spec_ref), channel_id=1, source_target_pairs={{0,1},{1,0},{2,3},{3,2},{4,5},{5,4},{6,7},{7,6},{8,9},{9,8},{10,11... | collective-permute-start | bytes 774152 | tf_op jit(solution)/shard_map/ppermute | solution.py:508
  29.0 1.3 %shard_map.104 = (f32[160,1536]{1,0:T(8,128)S(1)}, bf16[4,192,192]{2,1,0:T(8,128)(2,1)S(1)}, f32[8,192]{1,0:T(8,128)S(1)}) custom-call(s32[3]{0:T(128)S(1)} %pad_add_fusion.place_ref, bf16[1664,128]{1,0:T(8,128)(2,1)S(1)} %copy-done, bf16[336,384]{1,0:T(8,128)(2,1)S(1)} %shard_map.103.spec_ref, f32[2,8,96,96]{3,2,1,0:T(8,128)S(1)} %copy-done.4, ...), custom_call_target="tpu_custom_call" | custom-call | flops 117964800 | bytes 3153920 | tf_op jit(solution)/shard_map/pallas_call | solution.py:141
  30.3 0.0 copy-start.1
  30.3 5.5 %collective-permute-done.1.refs_0_ = bf16[336,384]{1,0:T(8,128)(2,1)S(1)} collective-permute-done((bf16[336,384]{1,0:T(8,128)(2,1)S(1)}, bf16[336,384]{1,0:T(8,128)(2,1)S(1)}, u32[]{:S(2)}, u32[]{:S(2)}) %collective-permute-start.1) | collective-permute-done | bytes 258080 | tf_op jit(solution)/shard_map/ppermute | solution.py:508
  35.8 3.9 %shard_map.105 = (f32[5,64,192]{2,1,0:T(8,128)S(1)}, f32[104,384]{1,0:T(8,128)S(1)}) custom-call(s32[3]{0:T(128)S(1)} %pad_add_fusion.place_ref, bf16[1664,128]{1,0:T(8,128)(2,1)S(1)} %copy-done, bf16[336,384]{1,0:T(8,128)(2,1)S(1)} %collective-permute-done.1.refs_0_, f32[160,1536]{1,0:T(8,128)S(1)} %get-tuple-element.19.refs_1_, ...), custom_call_target="tpu_custom_call" | custom-call | bytes 2373632 | tf_op jit(solution)/shard_map/pallas_call | solution.py:141
  39.7 0.1 collective-permute-start.2
  39.8 0.5 collective-permute-start.3
  40.3 1.3 %collective-permute-done.3.more_ref = f32[104,384]{1,0:T(8,128)S(1)} collective-permute-done((f32[104,384]{1,0:T(8,128)S(1)}, f32[104,384]{1,0:T(8,128)S(1)}, u32[]{:S(2)}, u32[]{:S(2)}) %collective-permute-start.3) | collective-permute-done | bytes 159776 | tf_op jit(solution)/shard_map/ppermute | solution.py:501
  41.6 0.0 collective-permute-done.2.other_ref
  41.6 1.2 %shard_map.106 = (bf16[136,384]{1,0:T(8,128)(2,1)S(1)}, bf16[136,384]{1,0:T(8,128)(2,1)S(1)}, bf16[176,384]{1,0:T(8,128)(2,1)S(1)}, bf16[176,384]{1,0:T(8,128)(2,1)S(1)}, bf16[176,384]{1,0:T(8,128)(2,1)S(1)}) custom-call(s32[3]{0:T(128)S(1)} %pad_add_fusion.place_ref, bf16[8,2,128,256]{3,2,1,0:T(8,128)(2,1)S(1)} %copy-done.1, ...), custom_call_target="tpu_custom_call" | custom-call | bytes 2473984 | tf_op jit(solution)/shard_map/pallas_call | solution.py:141
  42.8 1.2 %collective-permute-start.5 = (bf16[176,384]{1,0:T(8,128)(2,1)S(1)}, bf16[176,384]{1,0:T(8,128)(2,1)S(1)}, u32[]{:S(2)}, u32[]{:S(2)}) collective-permute-start(bf16[176,384]{1,0:T(8,128)(2,1)S(1)} %get-tuple-element.26), channel_id=1, source_target_pairs={{0,8},{2,14},{4,12},{6,10},{8,0},{10,6},{12,4},{14,2},{16,24},{18,... | collective-permute-start | bytes 405512 | tf_op jit(solution)/shard_map/ppermute | solution.py:505
  44.0 0.6 collective-permute-start.6
  44.6 2.7 %collective-permute-start.7 = (bf16[176,384]{1,0:T(8,128)(2,1)S(1)}, bf16[176,384]{1,0:T(8,128)(2,1)S(1)}, u32[]{:S(2)}, u32[]{:S(2)}) collective-permute-start(bf16[176,384]{1,0:T(8,128)(2,1)S(1)} %get-tuple-element.29), channel_id=1, source_target_pairs={{0,24},{2,30},{4,28},{6,26},{8,16},{10,22},{12,20},{14,18},{16,8},... | collective-permute-start | bytes 405512 | tf_op jit(solution)/shard_map/ppermute | solution.py:505
  47.3 1.5 %collective-permute-start.4 = (bf16[136,384]{1,0:T(8,128)(2,1)S(1)}, bf16[136,384]{1,0:T(8,128)(2,1)S(1)}, u32[]{:S(2)}, u32[]{:S(2)}) collective-permute-start(bf16[136,384]{1,0:T(8,128)(2,1)S(1)} %get-tuple-element.25), channel_id=1, source_target_pairs={{0,4},{2,6},{4,0},{6,2},{8,12},{10,14},{12,8},{14,10},{16,20},{18,... | collective-permute-start | bytes 313352 | tf_op jit(solution)/shard_map/ppermute | solution.py:505
  48.7 4.7 %collective-permute-done.4.refs_1_ = bf16[136,384]{1,0:T(8,128)(2,1)S(1)} collective-permute-done((bf16[136,384]{1,0:T(8,128)(2,1)S(1)}, bf16[136,384]{1,0:T(8,128)(2,1)S(1)}, u32[]{:S(2)}, u32[]{:S(2)}) %collective-permute-start.4) | collective-permute-done | bytes 104480 | tf_op jit(solution)/shard_map/ppermute | solution.py:505
  53.4 0.0 collective-permute-done.5.refs_4_
  53.4 0.4 collective-permute-start.10
  53.8 3.4 %collective-permute-done.6.refs_2_ = bf16[176,384]{1,0:T(8,128)(2,1)S(1)} collective-permute-done((bf16[176,384]{1,0:T(8,128)(2,1)S(1)}, bf16[176,384]{1,0:T(8,128)(2,1)S(1)}, u32[]{:S(2)}, u32[]{:S(2)}) %collective-permute-start.6) | collective-permute-done | bytes 135200 | tf_op jit(solution)/shard_map/ppermute | solution.py:505
  57.2 0.0 collective-permute-start.8
  57.2 0.0 collective-permute-done.7.refs_3_
  57.2 0.5 collective-permute-start.9
  57.7 1.2 %shard_map.107 = (f32[5,40,384]{2,1,0:T(8,128)S(1)}, f32[5,96,384]{2,1,0:T(8,128)S(1)}, f32[5,192]{1,0:T(8,128)S(1)}) custom-call(s32[3]{0:T(128)S(1)} %pad_add_fusion.place_ref, bf16[136,384]{1,0:T(8,128)(2,1)S(1)} %get-tuple-element.24.refs_0_, bf16[136,384]{1,0:T(8,128)(2,1)S(1)} %collective-permute-done.4.refs_1_, ...), custom_call_target="tpu_custom_call" | custom-call | bytes 1662720 | tf_op jit(solution)/shard_map/pallas_call | solution.py:141
  58.9 0.0 collective-permute-done.10.refs_2_
  59.0 2.7 %shard_map.108 = (bf16[10,14,768]{2,1,0:T(8,128)(2,1)}, f32[2,8,96,96]{3,2,1,0:T(8,128)}, f32[2,8,96]{2,1,0:T(8,128)}, f32[2,8,96,96]{3,2,1,0:T(8,128)}) custom-call(s32[3]{0:T(128)S(1)} %pad_add_fusion.place_ref, f32[5,40,384]{2,1,0:T(8,128)S(1)} %get-tuple-element.31.columns_ref, f32[5,96,384]{2,1,0:T(8,128)S(1)} %get-tuple-element.32.weights_ref, ...), custom_call_target="tpu_custom_call" | custom-call | bytes 3069696 | tf_op jit(solution)/shard_map/pallas_call | solution.py:141
  (15 shorter events, 0.0 us)
Async XLA Ops:
  0.7 0.9 %copy-start.2 = (bf16[10,14,768]{2,1,0:T(8,128)(2,1)S(1)}, bf16[10,14,768]{2,1,0:T(8,128)(2,1)}, u32[]{:S(2)}) copy-start(bf16[10,14,768]{2,1,0:T(8,128)(2,1)} %cot_ref.1) | copy-start | bytes 645124
  1.7 0.9 %copy-start.6 = (bf16[10,14,768]{2,1,0:T(8,128)(2,1)S(1)}, bf16[10,14,768]{2,1,0:T(8,128)(2,1)}, u32[]{:S(2)}) copy-start(bf16[10,14,768]{2,1,0:T(8,128)(2,1)} %x_ref.1) | copy-start | bytes 645124
  3.4 22.9 %copy-start = (bf16[1664,128]{1,0:T(8,128)(2,1)S(1)}, bf16[1664,128]{1,0:T(8,128)(2,1)}, u32[]{:S(2)}) copy-start(bf16[1664,128]{1,0:T(8,128)(2,1)} %constant.36.clone.table_ref) | copy-start | bytes 1277956
  24.5 4.6 %copy-start.4 = (f32[2,8,96,96]{3,2,1,0:T(8,128)S(1)}, f32[2,8,96,96]{3,2,1,0:T(8,128)}, u32[]{:S(2)}) copy-start(f32[2,8,96,96]{3,2,1,0:T(8,128)} %win_ref.1) | copy-start | bytes 1769476
  24.5 4.6 %copy-start.5 = (f32[2,8,96,96]{3,2,1,0:T(8,128)S(1)}, f32[2,8,96,96]{3,2,1,0:T(8,128)}, u32[]{:S(2)}) copy-start(f32[2,8,96,96]{3,2,1,0:T(8,128)} %wout_ref.1) | copy-start | bytes 1769476
  24.5 4.6 %copy-start.7 = (f32[2,8,96]{2,1,0:T(8,128)S(1)}, f32[2,8,96]{2,1,0:T(8,128)}, u32[]{:S(2)}) copy-start(f32[2,8,96]{2,1,0:T(8,128)} %bin_ref.1) | copy-start | bytes 18436
  24.5 1.9 %collective-permute-start = (bf16[8,80,384]{2,1,0:T(8,128)(2,1)S(1)}, bf16[8,80,384]{2,1,0:T(8,128)(2,1)S(1)}, u32[]{:S(2)}, u32[]{:S(2)}) collective-permute-start(bf16[8,80,384]{2,1,0:T(8,128)(2,1)S(1)} %all_to_all.5.refs_0_), channel_id=1, source_target_pairs={{0,2},{2,0},{4,6},{6,4},{8,10},{10,8},{12,14},{14,12},{16,18},{18,... | collective-permute-start | bytes 1474568 | tf_op jit(solution)/shard_map/ppermute | solution.py:501
  27.5 8.3 %collective-permute-start.1 = (bf16[336,384]{1,0:T(8,128)(2,1)S(1)}, bf16[336,384]{1,0:T(8,128)(2,1)S(1)}, u32[]{:S(2)}, u32[]{:S(2)}) collective-permute-start(bf16[336,384]{1,0:T(8,128)(2,1)S(1)} %shard_map.103.spec_ref), channel_id=1, source_target_pairs={{0,1},{1,0},{2,3},{3,2},{4,5},{5,4},{6,7},{7,6},{8,9},{9,8},{10,11... | collective-permute-start | bytes 774152 | tf_op jit(solution)/shard_map/ppermute | solution.py:508
  30.3 11.3 %copy-start.1 = (bf16[8,2,128,256]{3,2,1,0:T(8,128)(2,1)S(1)}, bf16[8,2,128,256]{3,2,1,0:T(8,128)(2,1)}, u32[]{:S(2)}) copy-start(bf16[8,2,128,256]{3,2,1,0:T(8,128)(2,1)} %constant.37.clone.table_ref) | copy-start | bytes 3145732
  39.7 1.9 %collective-permute-start.2 = (f32[5,64,192]{2,1,0:T(8,128)S(1)}, f32[5,64,192]{2,1,0:T(8,128)S(1)}, u32[]{:S(2)}, u32[]{:S(2)}) collective-permute-start(f32[5,64,192]{2,1,0:T(8,128)S(1)} %get-tuple-element.22.own_ref), channel_id=1, source_target_pairs={{0,2},{2,0},{4,6},{6,4},{8,10},{10,8},{12,14},{14,12},{16,18},{18,... | collective-permute-start | bytes 737288 | tf_op jit(solution)/shard_map/ppermute | solution.py:501
  39.8 1.8 %collective-permute-start.3 = (f32[104,384]{1,0:T(8,128)S(1)}, f32[104,384]{1,0:T(8,128)S(1)}, u32[]{:S(2)}, u32[]{:S(2)}) collective-permute-start(f32[104,384]{1,0:T(8,128)S(1)} %get-tuple-element.23.sum_ref), channel_id=1, source_target_pairs={{0,2},{2,0},{4,6},{6,4},{8,10},{10,8},{12,14},{14,12},{16,18},{18,... | collective-permute-start | bytes 479240 | tf_op jit(solution)/shard_map/ppermute | solution.py:501
  42.8 10.6 %collective-permute-start.5 = (bf16[176,384]{1,0:T(8,128)(2,1)S(1)}, bf16[176,384]{1,0:T(8,128)(2,1)S(1)}, u32[]{:S(2)}, u32[]{:S(2)}) collective-permute-start(bf16[176,384]{1,0:T(8,128)(2,1)S(1)} %get-tuple-element.26), channel_id=1, source_target_pairs={{0,8},{2,14},{4,12},{6,10},{8,0},{10,6},{12,4},{14,2},{16,24},{18,... | collective-permute-start | bytes 405512 | tf_op jit(solution)/shard_map/ppermute | solution.py:505
  44.0 13.1 %collective-permute-start.6 = (bf16[176,384]{1,0:T(8,128)(2,1)S(1)}, bf16[176,384]{1,0:T(8,128)(2,1)S(1)}, u32[]{:S(2)}, u32[]{:S(2)}) collective-permute-start(bf16[176,384]{1,0:T(8,128)(2,1)S(1)} %get-tuple-element.28), channel_id=1, source_target_pairs={{0,16},{2,22},{4,20},{6,18},{8,24},{10,30},{12,28},{14,26},{16,0},... | collective-permute-start | bytes 405512 | tf_op jit(solution)/shard_map/ppermute | solution.py:505
  44.6 12.6 %collective-permute-start.7 = (bf16[176,384]{1,0:T(8,128)(2,1)S(1)}, bf16[176,384]{1,0:T(8,128)(2,1)S(1)}, u32[]{:S(2)}, u32[]{:S(2)}) collective-permute-start(bf16[176,384]{1,0:T(8,128)(2,1)S(1)} %get-tuple-element.29), channel_id=1, source_target_pairs={{0,24},{2,30},{4,28},{6,26},{8,16},{10,22},{12,20},{14,18},{16,8},... | collective-permute-start | bytes 405512 | tf_op jit(solution)/shard_map/ppermute | solution.py:505
  47.3 6.1 %collective-permute-start.4 = (bf16[136,384]{1,0:T(8,128)(2,1)S(1)}, bf16[136,384]{1,0:T(8,128)(2,1)S(1)}, u32[]{:S(2)}, u32[]{:S(2)}) collective-permute-start(bf16[136,384]{1,0:T(8,128)(2,1)S(1)} %get-tuple-element.25), channel_id=1, source_target_pairs={{0,4},{2,6},{4,0},{6,2},{8,12},{10,14},{12,8},{14,10},{16,20},{18,... | collective-permute-start | bytes 313352 | tf_op jit(solution)/shard_map/ppermute | solution.py:505
  53.4 5.5 %collective-permute-start.10 = (bf16[176,384]{1,0:T(8,128)(2,1)S(1)}, bf16[176,384]{1,0:T(8,128)(2,1)S(1)}, u32[]{:S(2)}, u32[]{:S(2)}) collective-permute-start(bf16[176,384]{1,0:T(8,128)(2,1)S(1)} %collective-permute-done.5.refs_4_), channel_id=1, source_target_pairs={{0,2},{2,0},{4,6},{6,4},{8,10},{10,8},{12,14},{14,12},{16,18},{18,... | collective-permute-start | bytes 405512 | tf_op jit(solution)/shard_map/ppermute | solution.py:501
  57.2 1.7 %collective-permute-start.8 = (bf16[176,384]{1,0:T(8,128)(2,1)S(1)}, bf16[176,384]{1,0:T(8,128)(2,1)S(1)}, u32[]{:S(2)}, u32[]{:S(2)}) collective-permute-start(bf16[176,384]{1,0:T(8,128)(2,1)S(1)} %collective-permute-done.6.refs_2_), channel_id=1, source_target_pairs={{0,2},{2,0},{4,6},{6,4},{8,10},{10,8},{12,14},{14,12},{16,18},{18,... | collective-permute-start | bytes 405512 | tf_op jit(solution)/shard_map/ppermute | solution.py:501
  57.2 1.7 %collective-permute-start.9 = (bf16[176,384]{1,0:T(8,128)(2,1)S(1)}, bf16[176,384]{1,0:T(8,128)(2,1)S(1)}, u32[]{:S(2)}, u32[]{:S(2)}) collective-permute-start(bf16[176,384]{1,0:T(8,128)(2,1)S(1)} %collective-permute-done.7.refs_3_), channel_id=1, source_target_pairs={{0,2},{2,0},{4,6},{6,4},{8,10},{10,8},{12,14},{14,12},{16,18},{18,... | collective-permute-start | bytes 405512 | tf_op jit(solution)/shard_map/ppermute | solution.py:501
  57.7 1.2 %copy-start.3 = (bf16[10,14,768]{2,1,0:T(8,128)(2,1)S(1)}, bf16[10,14,768]{2,1,0:T(8,128)(2,1)}, u32[]{:S(2)}) copy-start(bf16[10,14,768]{2,1,0:T(8,128)(2,1)} %cot_ref.1) | copy-start | bytes 645124

commit v4 on v3

--- a/solution.py
+++ b/solution.py
@@ -68,6 +68,20 @@
     return np.stack(whole).reshape(blocks, 2, *whole[0].shape)
 
 
+def paired_table(blocks, cols):
+    modes = 2 * MODE_DEV * blocks
+    table = lon_table(blocks * 2 * cols, modes).reshape(blocks, 2, cols, 2, modes)
+    table = np.pad(table, ((0, 0), (0, 0), (0, PAD - cols), (0, 0), (0, 0)))
+    whole = []
+    for place in range(blocks):
+        for member in range(2):
+            sources = [place, place ^ 1]
+            sources += [place ^ (base + m) for m in (member, 1 - member) for base in BASES]
+            rows = table[sources][:, :, :, member].transpose(3, 1, 0, 2).reshape(modes, -1)
+            whole.append(np.concatenate(halves(rows)))
+    return np.stack(whole).reshape(blocks, 2, *whole[0].shape)
+
+
 def lat_table(rows, lat_count, group):
     total = rows * lat_count
     product = np.arange(total)[:, None] * np.arange(total)[None, :] % total
@@ -79,12 +93,15 @@
     return np.einsum("akxhqb,mn->akmxhqnb", basis, np.eye(group)).reshape(size, size)
 
 
-def all_tables(blocks, inner, cols, rows, lat_count):
-    forward, synth = lon_tables(blocks, inner, cols)
+def all_tables(blocks, inner, cols, rows, lat_count, paired):
     table = lat_table(rows, lat_count, SUB)
     size = table.shape[0]
     lat = np.concatenate(halves(table.reshape(size, lat_count, -1).transpose(1, 0, 2)), axis=1)
-    parts = [forward, lat.reshape(2 * lat_count * size, -1), synth]
+    lat = lat.reshape(2 * lat_count * size, -1)
+    if paired:
+        return lat, [0] * 4
+    forward, synth = lon_tables(blocks, inner, cols)
+    parts = [forward, lat, synth]
     lanes = max(p.shape[1] for p in parts)
     parts = [np.pad(p, ((0, 0), (0, lanes - p.shape[1]))) for p in parts]
     starts = np.cumsum([0] + [len(p) for p in parts])
@@ -165,6 +182,60 @@
             out_ref[b, q * PAD : (q + 1) * PAD, :] = jnp.concatenate(pieces, axis=1).astype(jnp.bfloat16)
 
 
+def pack_served(width, place, member, x_ref, g_ref, pack_ref):
+    rows, cols, channels = x_ref.shape
+    lanes = []
+    for q in range(rows // 2):
+        order = [ref[2 * q + h].astype(jnp.float32) for h in range(2) for ref in (x_ref, g_ref)]
+        lanes.append([jnp.pad(x, ((0, PAD - cols), (0, 0))) for x in order])
+    for b in range(channels // width):
+        other = place ^ b
+
+        @pl.when((other < 2) | ((other & 1) == member))
+        def _(b=b, other=other):
+            slot = jnp.where(other < 2, other, 2 + (other >> 1))
+            for q, order in enumerate(lanes):
+                pieces = [x[:, b * width : (b + 1) * width] for x in order]
+                piece = jnp.concatenate(pieces, axis=1).astype(jnp.bfloat16)
+                pack_ref[slot, q * PAD : (q + 1) * PAD, :] = piece
+
+
+def own_pack_kernel(width, place_ref, x_ref, g_ref, pack_ref):
+    pack_ref[2] = jnp.zeros_like(pack_ref[2])
+    pack_served(width, place_ref[0], place_ref[1], x_ref, g_ref, pack_ref)
+
+
+def pair_kernel(width, place_ref, own_ref, x_ref, g_ref, *refs):
+    outs, pack_ref = refs[:-1], refs[-1]
+    member = place_ref[1]
+    pack_served(width, place_ref[0], member, x_ref, g_ref, pack_ref)
+    for n, ref in enumerate(outs):
+        slot = n if n < 2 else 2 + BASES[n - 2] // 2
+        ref[member] = own_ref[slot]
+        ref[1 - member] = pack_ref[slot]
+
+
+def paired_lon_kernel(place_ref, table_ref, *refs):
+    payloads, (coded_ref, spec_ref) = refs[:-2], refs[-2:]
+    pairs, modes, lanes = spec_ref.shape
+    table = table_ref[0, 0]
+    tops = []
+    for q in range(pairs):
+        data = [ref[m, q * PAD : (q + 1) * PAD, :] for m in range(2) for ref in payloads]
+        total = dot(table, jnp.concatenate(data, axis=0))
+        spec = total[:modes] + total[modes:]
+        spec_ref[q] = spec
+        tops.append(jnp.max(jnp.abs(spec), axis=0, keepdims=True))
+    code_spectrum(coded_ref, spec_ref, tops)
+
+
+def code_spectrum(coded_ref, spec_ref, tops):
+    pairs, modes, lanes = spec_ref.shape
+    values, level = scaled(spec_ref[...], functools.reduce(jnp.maximum, tops))
+    coded_ref[: pairs * modes, :] = encode(values).reshape(pairs * modes, lanes)
+    coded_ref[pairs * modes :, :] = jnp.broadcast_to(level, (PAD, lanes)).astype(jnp.bfloat16)
+
+
 def lon_kernel(inner, place_ref, table_ref, *refs):
     fields, (coded_ref, spec_ref) = refs[:inner], refs[inner:]
     member = place_ref[1]
@@ -181,9 +252,7 @@
         spec = total[:modes] + total[modes:]
         spec_ref[q] = spec
         tops.append(jnp.max(jnp.abs(spec), axis=0, keepdims=True))
-    values, level = scaled(spec_ref[...], functools.reduce(jnp.maximum, tops))
-    coded_ref[: pairs * modes, :] = encode(values).reshape(pairs * modes, lanes)
-    coded_ref[pairs * modes :, :] = jnp.broadcast_to(level, (PAD, lanes)).astype(jnp.bfloat16)
+    code_spectrum(coded_ref, spec_ref, tops)
 
 
 def lat_rows(ref, pairs):
@@ -479,8 +548,9 @@
     lat_place = lax.axis_index("lat")
     scalars = jnp.stack([lon_place // inner, lon_place % inner, lat_place]).astype(jnp.int32)
     scaling = (rows * lat_count * modes // 2 * inner) ** -0.5
-    tables, (lon_start, lat_start, synth_start, _) = all_tables(blocks, inner, cols, rows, lat_count)
     paired = inner == 2 and blocks == 2 + 2 * len(BASES)
+    tables, starts = all_tables(blocks, inner, cols, rows, lat_count, paired)
+    lon_start, lat_start, synth_start, _ = starts
     shares = 1 if paired else inner
     share = width // shares
     data_rows = pairs * HALF
@@ -507,21 +577,49 @@
     def to_lat(values, step):
         return lax.ppermute(values, "lat", [(i, (i + step) % lat_count) for i in range(lat_count)])
 
-    (packed,) = call(
-        functools.partial(pack_kernel, width),
-        scalars,
-        (features, cotangent),
-        (shape((blocks, pairs * PAD, wide), bf16),),
-    )
-    arrived = exchange(packed)
-    fields = [arrived] + [to_member(arrived, s) for s in range(1, inner)]
-    (coded,) = call(
-        functools.partial(lon_kernel, inner),
-        scalars,
-        (tables, *fields),
-        (shape((pairs * modes + PAD, wide), bf16),),
+    def by_place(table):
+        return pl.BlockSpec((1, 1, *table.shape[2:]), lambda i, s: (s[0], s[1], 0, 0))
+
+    def serve(side, slots):
+        sent = [to_place(x, base, base + 1) for x, base in zip(slots, BASES)]
+        side, sent[0] = lax.optimization_barrier((to_place(side, 1, 1), sent[0]))
+        return [side, *sent], [to_member(x, 1) for x in sent]
+
+    spectrum = dict(
+        outputs=(shape((pairs * modes + PAD, wide), bf16),),
         scratch=(pltpu.VMEM((pairs, modes, wide), f32),),
     )
+    if paired:
+        rows_in = pairs * PAD
+        (packed,) = call(
+            functools.partial(own_pack_kernel, width),
+            scalars,
+            (features, cotangent),
+            (shape((2 + blocks // 2, rows_in, wide), bf16),),
+            flops=10**8,
+        )
+        own, side, *slots = call(
+            functools.partial(pair_kernel, width),
+            scalars,
+            (packed, to_member(features, 1), to_member(cotangent, 1)),
+            [shape((2, rows_in, wide), bf16)] * (2 + len(BASES)),
+            scratch=(pltpu.VMEM((2 + blocks // 2, rows_in, wide), bf16),),
+        )
+        sent, late = serve(side, slots)
+        table = paired_table(blocks, cols)
+        (coded,) = call(
+            paired_lon_kernel, scalars, (table, own, *sent, *late), specs={0: by_place(table)}, **spectrum
+        )
+    else:
+        (packed,) = call(
+            functools.partial(pack_kernel, width),
+            scalars,
+            (features, cotangent),
+            (shape((blocks, pairs * PAD, wide), bf16),),
+        )
+        whole = exchange(packed)
+        fields = [whole] + [to_member(whole, s) for s in range(1, inner)]
+        (coded,) = call(functools.partial(lon_kernel, inner), scalars, (tables, *fields), **spectrum)
     others = [to_lat(coded, s) for s in range(1, lat_count)]
     block_spec = pl.BlockSpec((2, 1, width, width), lambda i, s: (0, s[0], 0, 0))
     part, forms, bias = call(
@@ -553,13 +651,11 @@
             scalars,
             (table, *backs, keep, to_member(keep, 1)),
             [shape((n, wide), bf16) for n in outs],
-            specs={0: pl.BlockSpec((1, 1, *table.shape[2:]), lambda i, s: (s[0], s[1], 0, 0))},
+            specs={0: by_place(table)},
             scratch=(pltpu.VMEM((count, data_rows, wide), f32),),
         )
-        sent = [to_place(x, base, base + 1) for x, base in zip(slots, BASES)]
-        side, sent[-1] = lax.optimization_barrier((to_place(side, 1, 1), sent[-1]))
-        firsts = [own, side, *sent]
-        late = [to_member(x, 1) for x in sent]
+        sent, late = serve(side, slots)
+        firsts = [own, *sent]
         held = call(
             functools.partial(first_kernel, data_rows),
             scalars,

time: 62.3 us -> 59.7 us (0.958)
  blocking collectives: 21 us -> 0 us
  waiting for transfers between devices: 16.8 us -> 25.9 us
  starting transfers between devices: 8.9 us -> 17.3 us
  Pallas kernels: 12.2 us -> 13.6 us
    all_to_all x1 -> x0, blocking collectives: 21 us -> none  [exchange(): lax.all_to_all(values, 'lon', split_axis=0, concat_axis=0, tiled=True, ax...]
    ppermute x4 -> x8, waiting for transfers between devices: 8.09 us -> 18 us  [to_place(): return lax.ppermute(values, 'lon', turn)]
    ppermute x4 -> x8, starting transfers between devices: 5.91 us -> 12.4 us  [to_place(): return lax.ppermute(values, 'lon', turn)]
    ppermute x6 -> x10, starting transfers between devices: 1.43 us -> 3.23 us  [to_member(): return lax.ppermute(values, 'lon', turn)]
    pallas_call x7 -> x8, Pallas kernels: 12.2 us -> 13.6 us  [call(): pl.pallas_call(kernel, grid_spec=pltpu.PrefetchScalarGridSpec(num_scalar_...]
    ppermute x6 -> x10, waiting for transfers between devices: 3.21 us -> 2.34 us  [to_member(): return lax.ppermute(values, 'lon', turn)]
    unnamed x16 -> x18, local copies, waits for them, and re-layouts: 1.92 us -> 1.92 us
  transfers between devices with their start and end apart: 11 -> 19, of which waited for: 5 -> 8; matrix products, arithmetic and copies ran while one was open for 0% -> 0% of each run, Pallas kernels for 4% -> 6%
where the time goes in v4:
time: 59.7 us; the launch traced here: 59.5 us
  waiting for transfers between devices  25.9 us (43%)
  starting transfers between devices  17.3 us (29%)
  Pallas kernels  13.6 us (23%)
  local copies, waits for them, and re-layouts  1.92 us (3%)
  between operations  0.78 us (1%)
    ppermute x8, waiting for transfers between devices, to_place(): return lax.ppermute(values, 'lon', turn)  18 us
    pallas_call x8, Pallas kernels, call(): pl.pallas_call(kernel, grid_spec=pltpu.PrefetchScalarGridSpec(num_scalar_...  13.6 us
    ppermute x8, starting transfers between devices, to_place(): return lax.ppermute(values, 'lon', turn)  12.4 us
    ppermute x1, waiting for transfers between devices, to_lat(): lax.ppermute(values, 'lat', [(i, (i + step) % lat_count) for i in range(l...  5.55 us
    ppermute x10, starting transfers between devices, to_member(): return lax.ppermute(values, 'lon', turn)  3.23 us
    ppermute x10, waiting for transfers between devices, to_member(): return lax.ppermute(values, 'lon', turn)  2.34 us
    unnamed x18, local copies, waits for them, and re-layouts  1.92 us
    ppermute x1, starting transfers between devices, to_lat(): lax.ppermute(values, 'lat', [(i, (i + step) % lat_count) for i in range(l...  1.69 us
  transfers between devices with their start and end apart: 19, of which 8 were waited for; matrix products, arithmetic and copies ran while one was open for 0% of the time, Pallas kernels for 6%

profile of v4, /device:TPU:0, one launch (start us, length us, event | category | flops | bytes accessed | tf_op | source)
XLA Modules:
  0.0 59.5 jit_solution(13183484610334977377)
XLA Ops:
  0.6 0.5 collective-permute-start
  1.3 0.9 %copy-done.2 = bf16[10,14,768]{2,1,0:T(8,128)(2,1)S(1)} copy-done((bf16[10,14,768]{2,1,0:T(8,128)(2,1)S(1)}, bf16[10,14,768]{2,1,0:T(8,128)(2,1)}, u32[]{:S(2)}) %copy-start.2) | copy-done | bytes 215064
  2.3 0.9 %copy-done.7 = bf16[10,14,768]{2,1,0:T(8,128)(2,1)S(1)} copy-done((bf16[10,14,768]{2,1,0:T(8,128)(2,1)S(1)}, bf16[10,14,768]{2,1,0:T(8,128)(2,1)}, u32[]{:S(2)}) %copy-start.7) | copy-done | bytes 215064
  3.2 1.1 %shard_map.111.own_ref = bf16[6,80,384]{2,1,0:T(8,128)(2,1)S(1)} custom-call(s32[3]{0:T(128)S(1)} %pad_add_fusion.place_ref, bf16[10,14,768]{2,1,0:T(8,128)(2,1)S(1)} %copy-done.7, bf16[10,14,768]{2,1,0:T(8,128)(2,1)S(1)} %copy-done.2), custom_call_target="tpu_custom_call" | custom-call | flops 100000000 | bytes 798720 | tf_op jit(solution)/shard_map/pallas_call | solution.py:158
  4.3 1.1 %shard_map.112 = (bf16[2,80,384]{2,1,0:T(8,128)(2,1)S(1)}, bf16[2,80,384]{2,1,0:T(8,128)(2,1)S(1)}, bf16[2,80,384]{2,1,0:T(8,128)(2,1)S(1)}, bf16[2,80,384]{2,1,0:T(8,128)(2,1)S(1)}, bf16[2,80,384]{2,1,0:T(8,128)(2,1)S(1)}) custom-call(s32[3]{0:T(128)S(1)} %pad_add_fusion.place_ref, bf16[6,80,384]{2,1,0:T(8,128)(2,1)S(1)} %shard_map.111.own_ref, ...), custom_call_target="tpu_custom_call" | custom-call | bytes 1413120 | tf_op jit(solution)/shard_map/pallas_call | solution.py:158
  5.5 3.0 %collective-permute-start.2 = (bf16[2,80,384]{2,1,0:T(8,128)(2,1)S(1)}, bf16[2,80,384]{2,1,0:T(8,128)(2,1)S(1)}, u32[]{:S(2)}, u32[]{:S(2)}) collective-permute-start(bf16[2,80,384]{2,1,0:T(8,128)(2,1)S(1)} %get-tuple-element.27), channel_id=1, source_target_pairs={{0,4},{2,6},{4,0},{6,2},{8,12},{10,14},{12,8},{14,10},{16,20},{18,... | collective-permute-start | bytes 368648 | tf_op jit(solution)/shard_map/ppermute | solution.py:575
  8.4 2.6 %collective-permute-start.3 = (bf16[2,80,384]{2,1,0:T(8,128)(2,1)S(1)}, bf16[2,80,384]{2,1,0:T(8,128)(2,1)S(1)}, u32[]{:S(2)}, u32[]{:S(2)}) collective-permute-start(bf16[2,80,384]{2,1,0:T(8,128)(2,1)S(1)} %get-tuple-element.28), channel_id=1, source_target_pairs={{0,16},{2,22},{4,20},{6,18},{8,24},{10,30},{12,28},{14,26},{16,0},... | collective-permute-start | bytes 368648 | tf_op jit(solution)/shard_map/ppermute | solution.py:575
  11.0 1.4 %collective-permute-start.4 = (bf16[2,80,384]{2,1,0:T(8,128)(2,1)S(1)}, bf16[2,80,384]{2,1,0:T(8,128)(2,1)S(1)}, u32[]{:S(2)}, u32[]{:S(2)}) collective-permute-start(bf16[2,80,384]{2,1,0:T(8,128)(2,1)S(1)} %get-tuple-element.31), channel_id=1, source_target_pairs={{0,24},{2,30},{4,28},{6,26},{8,16},{10,22},{12,20},{14,18},{16,8},... | collective-permute-start | bytes 368648 | tf_op jit(solution)/shard_map/ppermute | solution.py:575
  12.6 8.1 %collective-permute-done.3.refs_2_ = bf16[2,80,384]{2,1,0:T(8,128)(2,1)S(1)} collective-permute-done((bf16[2,80,384]{2,1,0:T(8,128)(2,1)S(1)}, bf16[2,80,384]{2,1,0:T(8,128)(2,1)S(1)}, u32[]{:S(2)}, u32[]{:S(2)}) %collective-permute-start.3) | collective-permute-done | bytes 122912 | tf_op jit(solution)/shard_map/ppermute | solution.py:575
  20.8 0.5 collective-permute-start.7
  21.3 0.6 %collective-permute-done.5.refs_4_ = bf16[2,80,384]{2,1,0:T(8,128)(2,1)S(1)} collective-permute-done((bf16[2,80,384]{2,1,0:T(8,128)(2,1)S(1)}, bf16[2,80,384]{2,1,0:T(8,128)(2,1)S(1)}, u32[]{:S(2)}, u32[]{:S(2)}) %collective-permute-start.5) | collective-permute-done | bytes 122912 | tf_op jit(solution)/shard_map/ppermute | solution.py:575
  21.9 0.5 collective-permute-start.8
  22.4 1.0 %collective-permute-done.8.refs_7_ = bf16[2,80,384]{2,1,0:T(8,128)(2,1)S(1)} collective-permute-done((bf16[2,80,384]{2,1,0:T(8,128)(2,1)S(1)}, bf16[2,80,384]{2,1,0:T(8,128)(2,1)S(1)}, u32[]{:S(2)}, u32[]{:S(2)}) %collective-permute-start.8) | collective-permute-done | bytes 122912 | tf_op jit(solution)/shard_map/ppermute | solution.py:571
  23.4 1.0 %shard_map.113.spec_ref = bf16[336,384]{1,0:T(8,128)(2,1)S(1)} custom-call(s32[3]{0:T(128)S(1)} %pad_add_fusion.place_ref, bf16[8,2,128,256]{3,2,1,0:T(8,128)(2,1)S(1)} %copy-done, bf16[2,80,384]{2,1,0:T(8,128)(2,1)S(1)} %get-tuple-element.26.refs_0_, bf16[2,80,384]{2,1,0:T(8,128)(2,1)S(1)} %collective-permute-done.2.refs_1_, ...), custom_call_target="tpu_custom_call" | custom-call | bytes 2289664 | tf_op jit(solution)/shard_map/pallas_call | solution.py:158
  24.4 1.7 %collective-permute-start.9 = (bf16[336,384]{1,0:T(8,128)(2,1)S(1)}, bf16[336,384]{1,0:T(8,128)(2,1)S(1)}, u32[]{:S(2)}, u32[]{:S(2)}) collective-permute-start(bf16[336,384]{1,0:T(8,128)(2,1)S(1)} %shard_map.113.spec_ref), channel_id=1, source_target_pairs={{0,1},{1,0},{2,3},{3,2},{4,5},{5,4},{6,7},{7,6},{8,9},{9,8},{10,11... | collective-permute-start | bytes 774152 | tf_op jit(solution)/shard_map/ppermute | solution.py:578
  26.1 1.3 %shard_map.114 = (f32[160,1536]{1,0:T(8,128)S(1)}, bf16[4,192,192]{2,1,0:T(8,128)(2,1)S(1)}, f32[8,192]{1,0:T(8,128)S(1)}) custom-call(s32[3]{0:T(128)S(1)} %pad_add_fusion.place_ref, bf16[640,80]{1,0:T(8,128)(2,1)S(1)} %copy-done.6, bf16[336,384]{1,0:T(8,128)(2,1)S(1)} %shard_map.113.spec_ref, f32[2,8,96,96]{3,2,1,0:T(8,128)S(1)} %copy-done.4, ...), custom_call_target="tpu_custom_call" | custom-call | flops 117964800 | bytes 2830336 | tf_op jit(solution)/shard_map/pallas_call | solution.py:158
  27.4 5.6 %collective-permute-done.9.refs_0_ = bf16[336,384]{1,0:T(8,128)(2,1)S(1)} collective-permute-done((bf16[336,384]{1,0:T(8,128)(2,1)S(1)}, bf16[336,384]{1,0:T(8,128)(2,1)S(1)}, u32[]{:S(2)}, u32[]{:S(2)}) %collective-permute-start.9) | collective-permute-done | bytes 258080 | tf_op jit(solution)/shard_map/ppermute | solution.py:578
  33.0 3.9 %shard_map.115 = (f32[5,64,192]{2,1,0:T(8,128)S(1)}, f32[104,384]{1,0:T(8,128)S(1)}) custom-call(s32[3]{0:T(128)S(1)} %pad_add_fusion.place_ref, bf16[640,80]{1,0:T(8,128)(2,1)S(1)} %copy-done.6, bf16[336,384]{1,0:T(8,128)(2,1)S(1)} %collective-permute-done.9.refs_0_, f32[160,1536]{1,0:T(8,128)S(1)} %get-tuple-element.33.refs_1_, ...), custom_call_target="tpu_custom_call" | custom-call | bytes 2050048 | tf_op jit(solution)/shard_map/pallas_call | solution.py:158
  37.0 0.5 collective-permute-start.11
  37.5 1.3 %collective-permute-done.11.more_ref = f32[104,384]{1,0:T(8,128)S(1)} collective-permute-done((f32[104,384]{1,0:T(8,128)S(1)}, f32[104,384]{1,0:T(8,128)S(1)}, u32[]{:S(2)}, u32[]{:S(2)}) %collective-permute-start.11) | collective-permute-done | bytes 159776 | tf_op jit(solution)/shard_map/ppermute | solution.py:571
  38.8 1.2 %shard_map.116 = (bf16[136,384]{1,0:T(8,128)(2,1)S(1)}, bf16[136,384]{1,0:T(8,128)(2,1)S(1)}, bf16[176,384]{1,0:T(8,128)(2,1)S(1)}, bf16[176,384]{1,0:T(8,128)(2,1)S(1)}, bf16[176,384]{1,0:T(8,128)(2,1)S(1)}) custom-call(s32[3]{0:T(128)S(1)} %pad_add_fusion.place_ref, bf16[8,2,128,256]{3,2,1,0:T(8,128)(2,1)S(1)} %copy-done.1, ...), custom_call_target="tpu_custom_call" | custom-call | bytes 2473984 | tf_op jit(solution)/shard_map/pallas_call | solution.py:158
  40.0 3.5 %collective-permute-start.13 = (bf16[176,384]{1,0:T(8,128)(2,1)S(1)}, bf16[176,384]{1,0:T(8,128)(2,1)S(1)}, u32[]{:S(2)}, u32[]{:S(2)}) collective-permute-start(bf16[176,384]{1,0:T(8,128)(2,1)S(1)} %get-tuple-element.40), channel_id=1, source_target_pairs={{0,16},{2,22},{4,20},{6,18},{8,24},{10,30},{12,28},{14,26},{16,0},... | collective-permute-start | bytes 405512 | tf_op jit(solution)/shard_map/ppermute | solution.py:575
  43.5 0.3 collective-permute-start.14
  43.8 0.5 collective-permute-start.15
  44.3 1.0 %collective-permute-start.12 = (bf16[136,384]{1,0:T(8,128)(2,1)S(1)}, bf16[136,384]{1,0:T(8,128)(2,1)S(1)}, u32[]{:S(2)}, u32[]{:S(2)}) collective-permute-start(bf16[136,384]{1,0:T(8,128)(2,1)S(1)} %get-tuple-element.39), channel_id=1, source_target_pairs={{0,4},{2,6},{4,0},{6,2},{8,12},{10,14},{12,8},{14,10},{16,20},{18,... | collective-permute-start | bytes 313352 | tf_op jit(solution)/shard_map/ppermute | solution.py:575
  45.2 6.6 %collective-permute-done.12.refs_1_ = bf16[136,384]{1,0:T(8,128)(2,1)S(1)} collective-permute-done((bf16[136,384]{1,0:T(8,128)(2,1)S(1)}, bf16[136,384]{1,0:T(8,128)(2,1)S(1)}, u32[]{:S(2)}, u32[]{:S(2)}) %collective-permute-start.12) | collective-permute-done | bytes 104480 | tf_op jit(solution)/shard_map/ppermute | solution.py:575
  51.8 1.9 %collective-permute-done.13.refs_2_ = bf16[176,384]{1,0:T(8,128)(2,1)S(1)} collective-permute-done((bf16[176,384]{1,0:T(8,128)(2,1)S(1)}, bf16[176,384]{1,0:T(8,128)(2,1)S(1)}, u32[]{:S(2)}, u32[]{:S(2)}) %collective-permute-start.13) | collective-permute-done | bytes 135200 | tf_op jit(solution)/shard_map/ppermute | solution.py:575
  53.7 0.5 collective-permute-start.17
  54.2 0.8 %collective-permute-done.15.refs_4_ = bf16[176,384]{1,0:T(8,128)(2,1)S(1)} collective-permute-done((bf16[176,384]{1,0:T(8,128)(2,1)S(1)}, bf16[176,384]{1,0:T(8,128)(2,1)S(1)}, u32[]{:S(2)}, u32[]{:S(2)}) %collective-permute-start.15) | collective-permute-done | bytes 135200 | tf_op jit(solution)/shard_map/ppermute | solution.py:575
  55.0 0.5 collective-permute-start.18
  55.5 1.2 %shard_map.117 = (f32[5,40,384]{2,1,0:T(8,128)S(1)}, f32[5,96,384]{2,1,0:T(8,128)S(1)}, f32[5,192]{1,0:T(8,128)S(1)}) custom-call(s32[3]{0:T(128)S(1)} %pad_add_fusion.place_ref, bf16[136,384]{1,0:T(8,128)(2,1)S(1)} %get-tuple-element.38.refs_0_, bf16[136,384]{1,0:T(8,128)(2,1)S(1)} %collective-permute-done.12.refs_1_, ...), custom_call_target="tpu_custom_call" | custom-call | bytes 1662720 | tf_op jit(solution)/shard_map/pallas_call | solution.py:158
  56.8 2.7 %shard_map.118 = (bf16[10,14,768]{2,1,0:T(8,128)(2,1)}, f32[2,8,96,96]{3,2,1,0:T(8,128)}, f32[2,8,96]{2,1,0:T(8,128)}, f32[2,8,96,96]{3,2,1,0:T(8,128)}) custom-call(s32[3]{0:T(128)S(1)} %pad_add_fusion.place_ref, f32[5,40,384]{2,1,0:T(8,128)S(1)} %get-tuple-element.45.columns_ref, f32[5,96,384]{2,1,0:T(8,128)S(1)} %get-tuple-element.46.weights_ref, ...), custom_call_target="tpu_custom_call" | custom-call | bytes 3069696 | tf_op jit(solution)/shard_map/pallas_call | solution.py:158
  (33 shorter events, 0.5 us)
Async XLA Ops:
  0.6 22.8 %copy-start = (bf16[8,2,128,256]{3,2,1,0:T(8,128)(2,1)S(1)}, bf16[8,2,128,256]{3,2,1,0:T(8,128)(2,1)}, u32[]{:S(2)}) copy-start(bf16[8,2,128,256]{3,2,1,0:T(8,128)(2,1)} %constant.38.clone.table_ref) | copy-start | bytes 3145732
  0.6 3.7 %collective-permute-start = (bf16[10,14,768]{2,1,0:T(8,128)(2,1)}, bf16[10,14,768]{2,1,0:T(8,128)(2,1)S(1)}, u32[]{:S(2)}, u32[]{:S(2)}) collective-permute-start(bf16[10,14,768]{2,1,0:T(8,128)(2,1)} %x_ref.1), channel_id=1, source_target_pairs={{0,2},{2,0},{4,6},{6,4},{8,10},{10,8},{12,14},{14,12},{16,18},{18,... | collective-permute-start | bytes 645128 | tf_op jit(solution)/shard_map/ppermute | solution.py:571
  1.2 3.1 %collective-permute-start.1 = (bf16[10,14,768]{2,1,0:T(8,128)(2,1)}, bf16[10,14,768]{2,1,0:T(8,128)(2,1)S(1)}, u32[]{:S(2)}, u32[]{:S(2)}) collective-permute-start(bf16[10,14,768]{2,1,0:T(8,128)(2,1)} %cot_ref.1), channel_id=1, source_target_pairs={{0,2},{2,0},{4,6},{6,4},{8,10},{10,8},{12,14},{14,12},{16,18},{18,... | collective-permute-start | bytes 645128 | tf_op jit(solution)/shard_map/ppermute | solution.py:571
  1.3 0.9 %copy-start.2 = (bf16[10,14,768]{2,1,0:T(8,128)(2,1)S(1)}, bf16[10,14,768]{2,1,0:T(8,128)(2,1)}, u32[]{:S(2)}) copy-start(bf16[10,14,768]{2,1,0:T(8,128)(2,1)} %cot_ref.1) | copy-start | bytes 645124
  2.3 0.9 %copy-start.7 = (bf16[10,14,768]{2,1,0:T(8,128)(2,1)S(1)}, bf16[10,14,768]{2,1,0:T(8,128)(2,1)}, u32[]{:S(2)}) copy-start(bf16[10,14,768]{2,1,0:T(8,128)(2,1)} %x_ref.1) | copy-start | bytes 645124
  5.5 7.2 %collective-permute-start.2 = (bf16[2,80,384]{2,1,0:T(8,128)(2,1)S(1)}, bf16[2,80,384]{2,1,0:T(8,128)(2,1)S(1)}, u32[]{:S(2)}, u32[]{:S(2)}) collective-permute-start(bf16[2,80,384]{2,1,0:T(8,128)(2,1)S(1)} %get-tuple-element.27), channel_id=1, source_target_pairs={{0,4},{2,6},{4,0},{6,2},{8,12},{10,14},{12,8},{14,10},{16,20},{18,... | collective-permute-start | bytes 368648 | tf_op jit(solution)/shard_map/ppermute | solution.py:575
  8.4 12.3 %collective-permute-start.3 = (bf16[2,80,384]{2,1,0:T(8,128)(2,1)S(1)}, bf16[2,80,384]{2,1,0:T(8,128)(2,1)S(1)}, u32[]{:S(2)}, u32[]{:S(2)}) collective-permute-start(bf16[2,80,384]{2,1,0:T(8,128)(2,1)S(1)} %get-tuple-element.28), channel_id=1, source_target_pairs={{0,16},{2,22},{4,20},{6,18},{8,24},{10,30},{12,28},{14,26},{16,0},... | collective-permute-start | bytes 368648 | tf_op jit(solution)/shard_map/ppermute | solution.py:575
  11.0 9.7 %collective-permute-start.4 = (bf16[2,80,384]{2,1,0:T(8,128)(2,1)S(1)}, bf16[2,80,384]{2,1,0:T(8,128)(2,1)S(1)}, u32[]{:S(2)}, u32[]{:S(2)}) collective-permute-start(bf16[2,80,384]{2,1,0:T(8,128)(2,1)S(1)} %get-tuple-element.31), channel_id=1, source_target_pairs={{0,24},{2,30},{4,28},{6,26},{8,16},{10,22},{12,20},{14,18},{16,8},... | collective-permute-start | bytes 368648 | tf_op jit(solution)/shard_map/ppermute | solution.py:575
  12.4 9.5 %collective-permute-start.5 = (bf16[2,80,384]{2,1,0:T(8,128)(2,1)S(1)}, bf16[2,80,384]{2,1,0:T(8,128)(2,1)S(1)}, u32[]{:S(2)}, u32[]{:S(2)}) collective-permute-start(bf16[2,80,384]{2,1,0:T(8,128)(2,1)S(1)} %get-tuple-element.32), channel_id=1, source_target_pairs={{0,8},{2,14},{4,12},{6,10},{8,0},{10,6},{12,4},{14,2},{16,24},{18,... | collective-permute-start | bytes 368648 | tf_op jit(solution)/shard_map/ppermute | solution.py:575
  20.8 1.6 %collective-permute-start.6 = (bf16[2,80,384]{2,1,0:T(8,128)(2,1)S(1)}, bf16[2,80,384]{2,1,0:T(8,128)(2,1)S(1)}, u32[]{:S(2)}, u32[]{:S(2)}) collective-permute-start(bf16[2,80,384]{2,1,0:T(8,128)(2,1)S(1)} %collective-permute-done.3.refs_2_), channel_id=1, source_target_pairs={{0,2},{2,0},{4,6},{6,4},{8,10},{10,8},{12,14},{14,12},{16,18},{18,... | collective-permute-start | bytes 368648 | tf_op jit(solution)/shard_map/ppermute | solution.py:571
  20.8 1.6 %collective-permute-start.7 = (bf16[2,80,384]{2,1,0:T(8,128)(2,1)S(1)}, bf16[2,80,384]{2,1,0:T(8,128)(2,1)S(1)}, u32[]{:S(2)}, u32[]{:S(2)}) collective-permute-start(bf16[2,80,384]{2,1,0:T(8,128)(2,1)S(1)} %collective-permute-done.4.refs_3_), channel_id=1, source_target_pairs={{0,2},{2,0},{4,6},{6,4},{8,10},{10,8},{12,14},{14,12},{16,18},{18,... | collective-permute-start | bytes 368648 | tf_op jit(solution)/shard_map/ppermute | solution.py:571
  21.9 1.5 %collective-permute-start.8 = (bf16[2,80,384]{2,1,0:T(8,128)(2,1)S(1)}, bf16[2,80,384]{2,1,0:T(8,128)(2,1)S(1)}, u32[]{:S(2)}, u32[]{:S(2)}) collective-permute-start(bf16[2,80,384]{2,1,0:T(8,128)(2,1)S(1)} %collective-permute-done.5.refs_4_), channel_id=1, source_target_pairs={{0,2},{2,0},{4,6},{6,4},{8,10},{10,8},{12,14},{14,12},{16,18},{18,... | collective-permute-start | bytes 368648 | tf_op jit(solution)/shard_map/ppermute | solution.py:571
  23.4 2.8 %copy-start.4 = (f32[2,8,96,96]{3,2,1,0:T(8,128)S(1)}, f32[2,8,96,96]{3,2,1,0:T(8,128)}, u32[]{:S(2)}) copy-start(f32[2,8,96,96]{3,2,1,0:T(8,128)} %win_ref.1) | copy-start | bytes 1769476
  23.4 2.8 %copy-start.5 = (f32[2,8,96,96]{3,2,1,0:T(8,128)S(1)}, f32[2,8,96,96]{3,2,1,0:T(8,128)}, u32[]{:S(2)}) copy-start(f32[2,8,96,96]{3,2,1,0:T(8,128)} %wout_ref.1) | copy-start | bytes 1769476
  23.4 2.8 %copy-start.6 = (bf16[640,80]{1,0:T(8,128)(2,1)S(1)}, bf16[640,80]{1,0:T(8,128)(2,1)}, u32[]{:S(2)}) copy-start(bf16[640,80]{1,0:T(8,128)(2,1)} %constant.39.clone.table_ref) | copy-start | bytes 307204
  23.4 2.8 %copy-start.8 = (f32[2,8,96]{2,1,0:T(8,128)S(1)}, f32[2,8,96]{2,1,0:T(8,128)}, u32[]{:S(2)}) copy-start(f32[2,8,96]{2,1,0:T(8,128)} %bin_ref.1) | copy-start | bytes 18436
  24.4 8.6 %collective-permute-start.9 = (bf16[336,384]{1,0:T(8,128)(2,1)S(1)}, bf16[336,384]{1,0:T(8,128)(2,1)S(1)}, u32[]{:S(2)}, u32[]{:S(2)}) collective-permute-start(bf16[336,384]{1,0:T(8,128)(2,1)S(1)} %shard_map.113.spec_ref), channel_id=1, source_target_pairs={{0,1},{1,0},{2,3},{3,2},{4,5},{5,4},{6,7},{7,6},{8,9},{9,8},{10,11... | collective-permute-start | bytes 774152 | tf_op jit(solution)/shard_map/ppermute | solution.py:578
  27.4 11.4 %copy-start.1 = (bf16[8,2,128,256]{3,2,1,0:T(8,128)(2,1)S(1)}, bf16[8,2,128,256]{3,2,1,0:T(8,128)(2,1)}, u32[]{:S(2)}) copy-start(bf16[8,2,128,256]{3,2,1,0:T(8,128)(2,1)} %constant.40.clone.table_ref) | copy-start | bytes 3145732
  36.9 1.9 %collective-permute-start.10 = (f32[5,64,192]{2,1,0:T(8,128)S(1)}, f32[5,64,192]{2,1,0:T(8,128)S(1)}, u32[]{:S(2)}, u32[]{:S(2)}) collective-permute-start(f32[5,64,192]{2,1,0:T(8,128)S(1)} %get-tuple-element.36.own_ref), channel_id=1, source_target_pairs={{0,2},{2,0},{4,6},{6,4},{8,10},{10,8},{12,14},{14,12},{16,18},{18,... | collective-permute-start | bytes 737288 | tf_op jit(solution)/shard_map/ppermute | solution.py:571
  37.0 1.8 %collective-permute-start.11 = (f32[104,384]{1,0:T(8,128)S(1)}, f32[104,384]{1,0:T(8,128)S(1)}, u32[]{:S(2)}, u32[]{:S(2)}) collective-permute-start(f32[104,384]{1,0:T(8,128)S(1)} %get-tuple-element.37.sum_ref), channel_id=1, source_target_pairs={{0,2},{2,0},{4,6},{6,4},{8,10},{10,8},{12,14},{14,12},{16,18},{18,... | collective-permute-start | bytes 479240 | tf_op jit(solution)/shard_map/ppermute | solution.py:571
  40.0 13.7 %collective-permute-start.13 = (bf16[176,384]{1,0:T(8,128)(2,1)S(1)}, bf16[176,384]{1,0:T(8,128)(2,1)S(1)}, u32[]{:S(2)}, u32[]{:S(2)}) collective-permute-start(bf16[176,384]{1,0:T(8,128)(2,1)S(1)} %get-tuple-element.40), channel_id=1, source_target_pairs={{0,16},{2,22},{4,20},{6,18},{8,24},{10,30},{12,28},{14,26},{16,0},... | collective-permute-start | bytes 405512 | tf_op jit(solution)/shard_map/ppermute | solution.py:575
  43.5 10.2 %collective-permute-start.14 = (bf16[176,384]{1,0:T(8,128)(2,1)S(1)}, bf16[176,384]{1,0:T(8,128)(2,1)S(1)}, u32[]{:S(2)}, u32[]{:S(2)}) collective-permute-start(bf16[176,384]{1,0:T(8,128)(2,1)S(1)} %get-tuple-element.43), channel_id=1, source_target_pairs={{0,24},{2,30},{4,28},{6,26},{8,16},{10,22},{12,20},{14,18},{16,8},... | collective-permute-start | bytes 405512 | tf_op jit(solution)/shard_map/ppermute | solution.py:575
  43.8 11.2 %collective-permute-start.15 = (bf16[176,384]{1,0:T(8,128)(2,1)S(1)}, bf16[176,384]{1,0:T(8,128)(2,1)S(1)}, u32[]{:S(2)}, u32[]{:S(2)}) collective-permute-start(bf16[176,384]{1,0:T(8,128)(2,1)S(1)} %get-tuple-element.44), channel_id=1, source_target_pairs={{0,8},{2,14},{4,12},{6,10},{8,0},{10,6},{12,4},{14,2},{16,24},{18,... | collective-permute-start | bytes 405512 | tf_op jit(solution)/shard_map/ppermute | solution.py:575
  44.3 7.6 %collective-permute-start.12 = (bf16[136,384]{1,0:T(8,128)(2,1)S(1)}, bf16[136,384]{1,0:T(8,128)(2,1)S(1)}, u32[]{:S(2)}, u32[]{:S(2)}) collective-permute-start(bf16[136,384]{1,0:T(8,128)(2,1)S(1)} %get-tuple-element.39), channel_id=1, source_target_pairs={{0,4},{2,6},{4,0},{6,2},{8,12},{10,14},{12,8},{14,10},{16,20},{18,... | collective-permute-start | bytes 313352 | tf_op jit(solution)/shard_map/ppermute | solution.py:575
  53.7 3.0 %collective-permute-start.16 = (bf16[176,384]{1,0:T(8,128)(2,1)S(1)}, bf16[176,384]{1,0:T(8,128)(2,1)S(1)}, u32[]{:S(2)}, u32[]{:S(2)}) collective-permute-start(bf16[176,384]{1,0:T(8,128)(2,1)S(1)} %collective-permute-done.13.refs_2_), channel_id=1, source_target_pairs={{0,2},{2,0},{4,6},{6,4},{8,10},{10,8},{12,14},{14,12},{16,18},{18,... | collective-permute-start | bytes 405512 | tf_op jit(solution)/shard_map/ppermute | solution.py:571
  53.7 3.0 %collective-permute-start.17 = (bf16[176,384]{1,0:T(8,128)(2,1)S(1)}, bf16[176,384]{1,0:T(8,128)(2,1)S(1)}, u32[]{:S(2)}, u32[]{:S(2)}) collective-permute-start(bf16[176,384]{1,0:T(8,128)(2,1)S(1)} %collective-permute-done.14.refs_3_), channel_id=1, source_target_pairs={{0,2},{2,0},{4,6},{6,4},{8,10},{10,8},{12,14},{14,12},{16,18},{18,... | collective-permute-start | bytes 405512 | tf_op jit(solution)/shard_map/ppermute | solution.py:571
  55.0 1.8 %collective-permute-start.18 = (bf16[176,384]{1,0:T(8,128)(2,1)S(1)}, bf16[176,384]{1,0:T(8,128)(2,1)S(1)}, u32[]{:S(2)}, u32[]{:S(2)}) collective-permute-start(bf16[176,384]{1,0:T(8,128)(2,1)S(1)} %collective-permute-done.15.refs_4_), channel_id=1, source_target_pairs={{0,2},{2,0},{4,6},{6,4},{8,10},{10,8},{12,14},{14,12},{16,18},{18,... | collective-permute-start | bytes 405512 | tf_op jit(solution)/shard_map/ppermute | solution.py:571
  55.5 1.2 %copy-start.3 = (bf16[10,14,768]{2,1,0:T(8,128)(2,1)S(1)}, bf16[10,14,768]{2,1,0:T(8,128)(2,1)}, u32[]{:S(2)}) copy-start(bf16[10,14,768]{2,1,0:T(8,128)(2,1)} %cot_ref.1) | copy-start | bytes 645124

commit v5 on v4

--- a/solution.py
+++ b/solution.py
@@ -75,9 +75,10 @@
     whole = []
     for place in range(blocks):
         for member in range(2):
-            sources = [place, place ^ 1]
-            sources += [place ^ (base + m) for m in (member, 1 - member) for base in BASES]
-            rows = table[sources][:, :, :, member].transpose(3, 1, 0, 2).reshape(modes, -1)
+            sources = [(0, 0), (0, 1), (1, member), (1, 1 - member)]
+            sources += [(base + m, n) for m in (member, 1 - member) for base in BASES for n in range(2)]
+            rows = np.stack([table[place ^ k, n, :, member] for k, n in sources])
+            rows = rows.transpose(2, 0, 1).reshape(modes, -1)
             whole.append(np.concatenate(halves(rows)))
     return np.stack(whole).reshape(blocks, 2, *whole[0].shape)
 
@@ -200,9 +201,10 @@
                 pack_ref[slot, q * PAD : (q + 1) * PAD, :] = piece
 
 
-def own_pack_kernel(width, place_ref, x_ref, g_ref, pack_ref):
+def own_pack_kernel(width, place_ref, fields_ref, pack_ref, side_ref):
     pack_ref[2] = jnp.zeros_like(pack_ref[2])
-    pack_served(width, place_ref[0], place_ref[1], x_ref, g_ref, pack_ref)
+    pack_served(width, place_ref[0], place_ref[1], fields_ref.at[0], fields_ref.at[1], pack_ref)
+    side_ref[...] = pack_ref[1]
 
 
 def pair_kernel(width, place_ref, own_ref, x_ref, g_ref, *refs):
@@ -210,18 +212,20 @@
     member = place_ref[1]
     pack_served(width, place_ref[0], member, x_ref, g_ref, pack_ref)
     for n, ref in enumerate(outs):
-        slot = n if n < 2 else 2 + BASES[n - 2] // 2
+        slot = 0 if n == 0 else 2 + BASES[n - 1] // 2
         ref[member] = own_ref[slot]
         ref[1 - member] = pack_ref[slot]
 
 
-def paired_lon_kernel(place_ref, table_ref, *refs):
-    payloads, (coded_ref, spec_ref) = refs[:-2], refs[-2:]
+def paired_lon_kernel(place_ref, table_ref, own_ref, side_ref, other_side_ref, *refs):
+    pieces = [own_ref.at[0], own_ref.at[1], side_ref, other_side_ref]
+    pieces += [ref.at[n] for ref in refs[:-2] for n in range(2)]
+    coded_ref, spec_ref = refs[-2:]
     pairs, modes, lanes = spec_ref.shape
     table = table_ref[0, 0]
     tops = []
     for q in range(pairs):
-        data = [ref[m, q * PAD : (q + 1) * PAD, :] for m in range(2) for ref in payloads]
+        data = [piece[q * PAD : (q + 1) * PAD, :] for piece in pieces]
         total = dot(table, jnp.concatenate(data, axis=0))
         spec = total[:modes] + total[modes:]
         spec_ref[q] = spec
@@ -580,10 +584,8 @@
     def by_place(table):
         return pl.BlockSpec((1, 1, *table.shape[2:]), lambda i, s: (s[0], s[1], 0, 0))
 
-    def serve(side, slots):
-        sent = [to_place(x, base, base + 1) for x, base in zip(slots, BASES)]
-        side, sent[0] = lax.optimization_barrier((to_place(side, 1, 1), sent[0]))
-        return [side, *sent], [to_member(x, 1) for x in sent]
+    def serve(slots):
+        return [to_place(x, base, base + 1) for x, base in zip(slots, BASES)]
 
     spectrum = dict(
         outputs=(shape((pairs * modes + PAD, wide), bf16),),
@@ -591,21 +593,24 @@
     )
     if paired:
         rows_in = pairs * PAD
-        (packed,) = call(
+        packed, side = call(
             functools.partial(own_pack_kernel, width),
             scalars,
-            (features, cotangent),
-            (shape((2 + blocks // 2, rows_in, wide), bf16),),
+            (jnp.stack([features, cotangent]),),
+            (shape((2 + blocks // 2, rows_in, wide), bf16), shape((rows_in, wide), bf16)),
             flops=10**8,
         )
-        own, side, *slots = call(
+        own, *slots = call(
             functools.partial(pair_kernel, width),
             scalars,
             (packed, to_member(features, 1), to_member(cotangent, 1)),
-            [shape((2, rows_in, wide), bf16)] * (2 + len(BASES)),
+            [shape((2, rows_in, wide), bf16)] * (1 + len(BASES)),
             scratch=(pltpu.VMEM((2 + blocks // 2, rows_in, wide), bf16),),
         )
-        sent, late = serve(side, slots)
+        side = to_place(side, 1, 1)
+        sent = [side, *serve(slots)]
+        late = [to_member(x, 1) for x in sent]
+        sent, late = [side, late[0], *sent[1:]], late[1:]
         table = paired_table(blocks, cols)
         (coded,) = call(
             paired_lon_kernel, scalars, (table, own, *sent, *late), specs={0: by_place(table)}, **spectrum
@@ -654,8 +659,9 @@
             specs={0: by_place(table)},
             scratch=(pltpu.VMEM((count, data_rows, wide), f32),),
         )
-        sent, late = serve(side, slots)
-        firsts = [own, *sent]
+        sent = serve(slots)
+        side, sent[0] = lax.optimization_barrier((to_place(side, 1, 1), sent[0]))
+        firsts, late = [own, side, *sent], [to_member(x, 1) for x in sent]
         held = call(
             functools.partial(first_kernel, data_rows),
             scalars,

time: 59.7 us -> 58.5 us (0.980)
  local copies, waits for them, and re-layouts: 1.92 us -> 0.04 us
  other arithmetic: 0.08 us -> 1.29 us
  waiting for transfers between devices: 25.9 us -> 25.2 us
    unnamed x18 -> x14, local copies, waits for them, and re-layouts: 1.92 us -> 0.04 us
    another operation x0 -> x1, other arithmetic: none -> 1.21 us  [body(): jnp.stack([features, cotangent])]
    ppermute x8, waiting for transfers between devices: 18 us -> 17.1 us  [to_place(): return lax.ppermute(values, 'lon', turn)]
    ppermute x8, starting transfers between devices: 12.4 us -> 13 us  [to_place(): return lax.ppermute(values, 'lon', turn)]
    ppermute x10 -> x11, starting transfers between devices: 3.23 us -> 2.87 us  [to_member(): return lax.ppermute(values, 'lon', turn)]
    ppermute x10 -> x11, waiting for transfers between devices: 2.34 us -> 2.61 us  [to_member(): return lax.ppermute(values, 'lon', turn)]
  transfers between devices with their start and end apart: 19 -> 20, of which waited for: 8 -> 8; matrix products, arithmetic and copies ran while one was open for 0% -> 2% of each run, Pallas kernels for 6% -> 6%
where the time goes in v5:
time: 58.5 us; the launch traced here: 58.3 us
  waiting for transfers between devices  25.2 us (43%)
  starting transfers between devices  17.4 us (30%)
  Pallas kernels  13.6 us (23%)
  other arithmetic  1.29 us (2%)
  between operations  0.8 us (1%)
    ppermute x8, waiting for transfers between devices, to_place(): return lax.ppermute(values, 'lon', turn)  17.1 us
    pallas_call x8, Pallas kernels, call(): pl.pallas_call(kernel, grid_spec=pltpu.PrefetchScalarGridSpec(num_scalar_...  13.6 us
    ppermute x8, starting transfers between devices, to_place(): return lax.ppermute(values, 'lon', turn)  13 us
    ppermute x1, waiting for transfers between devices, to_lat(): lax.ppermute(values, 'lat', [(i, (i + step) % lat_count) for i in range(l...  5.49 us
    ppermute x11, starting transfers between devices, to_member(): return lax.ppermute(values, 'lon', turn)  2.87 us
    ppermute x11, waiting for transfers between devices, to_member(): return lax.ppermute(values, 'lon', turn)  2.61 us
    ppermute x1, starting transfers between devices, to_lat(): lax.ppermute(values, 'lat', [(i, (i + step) % lat_count) for i in range(l...  1.56 us
    another operation x1, other arithmetic, body(): jnp.stack([features, cotangent])  1.21 us
  transfers between devices with their start and end apart: 20, of which 8 were waited for; matrix products, arithmetic and copies ran while one was open for 2% of the time, Pallas kernels for 6%

profile of v5, /device:TPU:0, one launch (start us, length us, event | category | flops | bytes accessed | tf_op | source)
XLA Modules:
  0.0 58.3 jit_solution(16053755025795165291)
XLA Ops:
  0.6 0.5 collective-permute-start
  1.3 1.2 %pad_maximum_fusion.fields_ref = bf16[2,10,14,768]{3,2,1,0:T(8,128)(2,1)S(1)} fusion(bf16[1,10,14,768]{3,2,1,0:T(8,128)(2,1)} %bitcast.5, bf16[1,10,14,768]{3,2,1,0:T(8,128)(2,1)} %bitcast.6), kind=kLoop, calls=%fused_computation | loop fusion | flops 215040 | bytes 860160 | tf_op jit(solution)/shard_map/stack | solution.py:599
  2.5 1.1 %shard_map.111 = (bf16[6,80,384]{2,1,0:T(8,128)(2,1)S(1)}, bf16[80,384]{1,0:T(8,128)(2,1)S(1)}) custom-call(s32[3]{0:T(128)S(1)} %pad_add_fusion.place_ref, bf16[2,10,14,768]{3,2,1,0:T(8,128)(2,1)S(1)} %pad_maximum_fusion.fields_ref), custom_call_target="tpu_custom_call" | custom-call | flops 100000000 | bytes 860160 | tf_op jit(solution)/shard_map/pallas_call | solution.py:159
  3.6 1.1 %shard_map.112 = (bf16[2,80,384]{2,1,0:T(8,128)(2,1)S(1)}, bf16[2,80,384]{2,1,0:T(8,128)(2,1)S(1)}, bf16[2,80,384]{2,1,0:T(8,128)(2,1)S(1)}, bf16[2,80,384]{2,1,0:T(8,128)(2,1)S(1)}) custom-call(s32[3]{0:T(128)S(1)} %pad_add_fusion.place_ref, bf16[6,80,384]{2,1,0:T(8,128)(2,1)S(1)} %get-tuple-element.25.own_ref, ...), custom_call_target="tpu_custom_call" | custom-call | bytes 1290240 | tf_op jit(solution)/shard_map/pallas_call | solution.py:159
  4.8 4.1 %collective-permute-start.4 = (bf16[2,80,384]{2,1,0:T(8,128)(2,1)S(1)}, bf16[2,80,384]{2,1,0:T(8,128)(2,1)S(1)}, u32[]{:S(2)}, u32[]{:S(2)}) collective-permute-start(bf16[2,80,384]{2,1,0:T(8,128)(2,1)S(1)} %get-tuple-element.28), channel_id=1, source_target_pairs={{0,16},{2,22},{4,20},{6,18},{8,24},{10,30},{12,28},{14,26},{16,0},... | collective-permute-start | bytes 368648 | tf_op jit(solution)/shard_map/ppermute | solution.py:579
  8.9 1.3 %collective-permute-start.5 = (bf16[2,80,384]{2,1,0:T(8,128)(2,1)S(1)}, bf16[2,80,384]{2,1,0:T(8,128)(2,1)S(1)}, u32[]{:S(2)}, u32[]{:S(2)}) collective-permute-start(bf16[2,80,384]{2,1,0:T(8,128)(2,1)S(1)} %get-tuple-element.29), channel_id=1, source_target_pairs={{0,24},{2,30},{4,28},{6,26},{8,16},{10,22},{12,20},{14,18},{16,8},... | collective-permute-start | bytes 368648 | tf_op jit(solution)/shard_map/ppermute | solution.py:579
  10.2 0.2 collective-permute-start.6
  10.4 1.6 %collective-permute-start.2 = (bf16[80,384]{1,0:T(8,128)(2,1)S(1)}, bf16[80,384]{1,0:T(8,128)(2,1)S(1)}, u32[]{:S(2)}, u32[]{:S(2)}) collective-permute-start(bf16[80,384]{1,0:T(8,128)(2,1)S(1)} %get-tuple-element.27), channel_id=1, source_target_pairs={{0,4},{2,6},{4,0},{6,2},{8,12},{10,14},{12,8},{14,10},{16,20},{18,... | collective-permute-start | bytes 184328 | tf_op jit(solution)/shard_map/ppermute | solution.py:579
  12.0 6.1 %collective-permute-done.4.refs_0_ = bf16[2,80,384]{2,1,0:T(8,128)(2,1)S(1)} collective-permute-done((bf16[2,80,384]{2,1,0:T(8,128)(2,1)S(1)}, bf16[2,80,384]{2,1,0:T(8,128)(2,1)S(1)}, u32[]{:S(2)}, u32[]{:S(2)}) %collective-permute-start.4) | collective-permute-done | bytes 122912 | tf_op jit(solution)/shard_map/ppermute | solution.py:579
  18.1 0.5 collective-permute-start.8
  18.6 1.3 %collective-permute-done.6.refs_2_ = bf16[2,80,384]{2,1,0:T(8,128)(2,1)S(1)} collective-permute-done((bf16[2,80,384]{2,1,0:T(8,128)(2,1)S(1)}, bf16[2,80,384]{2,1,0:T(8,128)(2,1)S(1)}, u32[]{:S(2)}, u32[]{:S(2)}) %collective-permute-start.6) | collective-permute-done | bytes 122912 | tf_op jit(solution)/shard_map/ppermute | solution.py:579
  19.9 0.5 collective-permute-start.9
  20.4 1.2 %collective-permute-done.3.other_side_ref = bf16[80,384]{1,0:T(8,128)(2,1)S(1)} collective-permute-done((bf16[80,384]{1,0:T(8,128)(2,1)S(1)}, bf16[80,384]{1,0:T(8,128)(2,1)S(1)}, u32[]{:S(2)}, u32[]{:S(2)}) %collective-permute-start.3) | collective-permute-done | bytes 61472 | tf_op jit(solution)/shard_map/ppermute | solution.py:575
  21.7 1.0 %shard_map.113.spec_ref = bf16[336,384]{1,0:T(8,128)(2,1)S(1)} custom-call(s32[3]{0:T(128)S(1)} %pad_add_fusion.place_ref, bf16[8,2,128,256]{3,2,1,0:T(8,128)(2,1)S(1)} %copy-done, bf16[2,80,384]{2,1,0:T(8,128)(2,1)S(1)} %get-tuple-element.26.own_ref, bf16[80,384]{1,0:T(8,128)(2,1)S(1)} %collective-permute-done.2.side_ref, ...), custom_call_target="tpu_custom_call" | custom-call | bytes 2289664 | tf_op jit(solution)/shard_map/pallas_call | solution.py:159
  22.8 1.6 %collective-permute-start.10 = (bf16[336,384]{1,0:T(8,128)(2,1)S(1)}, bf16[336,384]{1,0:T(8,128)(2,1)S(1)}, u32[]{:S(2)}, u32[]{:S(2)}) collective-permute-start(bf16[336,384]{1,0:T(8,128)(2,1)S(1)} %shard_map.113.spec_ref), channel_id=1, source_target_pairs={{0,1},{1,0},{2,3},{3,2},{4,5},{5,4},{6,7},{7,6},{8,9},{9,8},{10,11... | collective-permute-start | bytes 774152 | tf_op jit(solution)/shard_map/ppermute | solution.py:582
  24.4 1.3 %shard_map.114 = (f32[160,1536]{1,0:T(8,128)S(1)}, bf16[4,192,192]{2,1,0:T(8,128)(2,1)S(1)}, f32[8,192]{1,0:T(8,128)S(1)}) custom-call(s32[3]{0:T(128)S(1)} %pad_add_fusion.place_ref, bf16[640,80]{1,0:T(8,128)(2,1)S(1)} %copy-done.5, bf16[336,384]{1,0:T(8,128)(2,1)S(1)} %shard_map.113.spec_ref, f32[2,8,96,96]{3,2,1,0:T(8,128)S(1)} %copy-done.3, ...), custom_call_target="tpu_custom_call" | custom-call | flops 117964800 | bytes 2830336 | tf_op jit(solution)/shard_map/pallas_call | solution.py:159
  25.6 5.5 %collective-permute-done.10.refs_0_ = bf16[336,384]{1,0:T(8,128)(2,1)S(1)} collective-permute-done((bf16[336,384]{1,0:T(8,128)(2,1)S(1)}, bf16[336,384]{1,0:T(8,128)(2,1)S(1)}, u32[]{:S(2)}, u32[]{:S(2)}) %collective-permute-start.10) | collective-permute-done | bytes 258080 | tf_op jit(solution)/shard_map/ppermute | solution.py:582
  31.1 3.9 %shard_map.115 = (f32[5,64,192]{2,1,0:T(8,128)S(1)}, f32[104,384]{1,0:T(8,128)S(1)}) custom-call(s32[3]{0:T(128)S(1)} %pad_add_fusion.place_ref, bf16[640,80]{1,0:T(8,128)(2,1)S(1)} %copy-done.5, bf16[336,384]{1,0:T(8,128)(2,1)S(1)} %collective-permute-done.10.refs_0_, f32[160,1536]{1,0:T(8,128)S(1)} %get-tuple-element.31.refs_1_, ...), custom_call_target="tpu_custom_call" | custom-call | bytes 2050048 | tf_op jit(solution)/shard_map/pallas_call | solution.py:159
  35.1 0.5 collective-permute-start.12
  35.6 1.3 %collective-permute-done.12.more_ref = f32[104,384]{1,0:T(8,128)S(1)} collective-permute-done((f32[104,384]{1,0:T(8,128)S(1)}, f32[104,384]{1,0:T(8,128)S(1)}, u32[]{:S(2)}, u32[]{:S(2)}) %collective-permute-start.12) | collective-permute-done | bytes 159776 | tf_op jit(solution)/shard_map/ppermute | solution.py:575
  37.0 1.2 %shard_map.116 = (bf16[136,384]{1,0:T(8,128)(2,1)S(1)}, bf16[136,384]{1,0:T(8,128)(2,1)S(1)}, bf16[176,384]{1,0:T(8,128)(2,1)S(1)}, bf16[176,384]{1,0:T(8,128)(2,1)S(1)}, bf16[176,384]{1,0:T(8,128)(2,1)S(1)}) custom-call(s32[3]{0:T(128)S(1)} %pad_add_fusion.place_ref, bf16[8,2,128,256]{3,2,1,0:T(8,128)(2,1)S(1)} %copy-done.1, ...), custom_call_target="tpu_custom_call" | custom-call | bytes 2473984 | tf_op jit(solution)/shard_map/pallas_call | solution.py:159
  38.2 4.1 %collective-permute-start.14 = (bf16[176,384]{1,0:T(8,128)(2,1)S(1)}, bf16[176,384]{1,0:T(8,128)(2,1)S(1)}, u32[]{:S(2)}, u32[]{:S(2)}) collective-permute-start(bf16[176,384]{1,0:T(8,128)(2,1)S(1)} %get-tuple-element.38), channel_id=1, source_target_pairs={{0,16},{2,22},{4,20},{6,18},{8,24},{10,30},{12,28},{14,26},{16,0},... | collective-permute-start | bytes 405512 | tf_op jit(solution)/shard_map/ppermute | solution.py:579
  42.2 0.4 collective-permute-start.15
  42.7 0.2 collective-permute-start.16
  42.9 1.1 %collective-permute-start.13 = (bf16[136,384]{1,0:T(8,128)(2,1)S(1)}, bf16[136,384]{1,0:T(8,128)(2,1)S(1)}, u32[]{:S(2)}, u32[]{:S(2)}) collective-permute-start(bf16[136,384]{1,0:T(8,128)(2,1)S(1)} %get-tuple-element.37), channel_id=1, source_target_pairs={{0,4},{2,6},{4,0},{6,2},{8,12},{10,14},{12,8},{14,10},{16,20},{18,... | collective-permute-start | bytes 313352 | tf_op jit(solution)/shard_map/ppermute | solution.py:579
  44.0 5.9 %collective-permute-done.13.refs_1_ = bf16[136,384]{1,0:T(8,128)(2,1)S(1)} collective-permute-done((bf16[136,384]{1,0:T(8,128)(2,1)S(1)}, bf16[136,384]{1,0:T(8,128)(2,1)S(1)}, u32[]{:S(2)}, u32[]{:S(2)}) %collective-permute-start.13) | collective-permute-done | bytes 104480 | tf_op jit(solution)/shard_map/ppermute | solution.py:579
  49.9 2.4 %collective-permute-done.14.refs_2_ = bf16[176,384]{1,0:T(8,128)(2,1)S(1)} collective-permute-done((bf16[176,384]{1,0:T(8,128)(2,1)S(1)}, bf16[176,384]{1,0:T(8,128)(2,1)S(1)}, u32[]{:S(2)}, u32[]{:S(2)}) %collective-permute-start.14) | collective-permute-done | bytes 135200 | tf_op jit(solution)/shard_map/ppermute | solution.py:579
  52.3 0.5 collective-permute-start.18
  52.9 1.3 %collective-permute-done.16.refs_4_ = bf16[176,384]{1,0:T(8,128)(2,1)S(1)} collective-permute-done((bf16[176,384]{1,0:T(8,128)(2,1)S(1)}, bf16[176,384]{1,0:T(8,128)(2,1)S(1)}, u32[]{:S(2)}, u32[]{:S(2)}) %collective-permute-start.16) | collective-permute-done | bytes 135200 | tf_op jit(solution)/shard_map/ppermute | solution.py:579
  54.2 0.2 collective-permute-start.19
  54.3 1.2 %shard_map.117 = (f32[5,40,384]{2,1,0:T(8,128)S(1)}, f32[5,96,384]{2,1,0:T(8,128)S(1)}, f32[5,192]{1,0:T(8,128)S(1)}) custom-call(s32[3]{0:T(128)S(1)} %pad_add_fusion.place_ref, bf16[136,384]{1,0:T(8,128)(2,1)S(1)} %get-tuple-element.36.refs_0_, bf16[136,384]{1,0:T(8,128)(2,1)S(1)} %collective-permute-done.13.refs_1_, ...), custom_call_target="tpu_custom_call" | custom-call | bytes 1662720 | tf_op jit(solution)/shard_map/pallas_call | solution.py:159
  55.6 2.7 %shard_map.118 = (bf16[10,14,768]{2,1,0:T(8,128)(2,1)}, f32[2,8,96,96]{3,2,1,0:T(8,128)}, f32[2,8,96]{2,1,0:T(8,128)}, f32[2,8,96,96]{3,2,1,0:T(8,128)}) custom-call(s32[3]{0:T(128)S(1)} %pad_add_fusion.place_ref, f32[5,40,384]{2,1,0:T(8,128)S(1)} %get-tuple-element.43.columns_ref, f32[5,96,384]{2,1,0:T(8,128)S(1)} %get-tuple-element.44.weights_ref, ...), custom_call_target="tpu_custom_call" | custom-call | bytes 3069696 | tf_op jit(solution)/shard_map/pallas_call | solution.py:159
  (32 shorter events, 0.3 us)
Async XLA Ops:
  0.6 3.0 %collective-permute-start = (bf16[10,14,768]{2,1,0:T(8,128)(2,1)}, bf16[10,14,768]{2,1,0:T(8,128)(2,1)S(1)}, u32[]{:S(2)}, u32[]{:S(2)}) collective-permute-start(bf16[10,14,768]{2,1,0:T(8,128)(2,1)} %param.8), channel_id=1, source_target_pairs={{0,2},{2,0},{4,6},{6,4},{8,10},{10,8},{12,14},{14,12},{16,18},{18,... | collective-permute-start | bytes 645128 | tf_op jit(solution)/shard_map/ppermute | solution.py:575
  1.1 2.5 %collective-permute-start.1 = (bf16[10,14,768]{2,1,0:T(8,128)(2,1)}, bf16[10,14,768]{2,1,0:T(8,128)(2,1)S(1)}, u32[]{:S(2)}, u32[]{:S(2)}) collective-permute-start(bf16[10,14,768]{2,1,0:T(8,128)(2,1)} %cot_ref.1), channel_id=1, source_target_pairs={{0,2},{2,0},{4,6},{6,4},{8,10},{10,8},{12,14},{14,12},{16,18},{18,... | collective-permute-start | bytes 645128 | tf_op jit(solution)/shard_map/ppermute | solution.py:575
  1.3 20.4 %copy-start = (bf16[8,2,128,256]{3,2,1,0:T(8,128)(2,1)S(1)}, bf16[8,2,128,256]{3,2,1,0:T(8,128)(2,1)}, u32[]{:S(2)}) copy-start(bf16[8,2,128,256]{3,2,1,0:T(8,128)(2,1)} %constant.38.clone.table_ref) | copy-start | bytes 3145732
  4.8 13.3 %collective-permute-start.4 = (bf16[2,80,384]{2,1,0:T(8,128)(2,1)S(1)}, bf16[2,80,384]{2,1,0:T(8,128)(2,1)S(1)}, u32[]{:S(2)}, u32[]{:S(2)}) collective-permute-start(bf16[2,80,384]{2,1,0:T(8,128)(2,1)S(1)} %get-tuple-element.28), channel_id=1, source_target_pairs={{0,16},{2,22},{4,20},{6,18},{8,24},{10,30},{12,28},{14,26},{16,0},... | collective-permute-start | bytes 368648 | tf_op jit(solution)/shard_map/ppermute | solution.py:579
  8.9 9.2 %collective-permute-start.5 = (bf16[2,80,384]{2,1,0:T(8,128)(2,1)S(1)}, bf16[2,80,384]{2,1,0:T(8,128)(2,1)S(1)}, u32[]{:S(2)}, u32[]{:S(2)}) collective-permute-start(bf16[2,80,384]{2,1,0:T(8,128)(2,1)S(1)} %get-tuple-element.29), channel_id=1, source_target_pairs={{0,24},{2,30},{4,28},{6,26},{8,16},{10,22},{12,20},{14,18},{16,8},... | collective-permute-start | bytes 368648 | tf_op jit(solution)/shard_map/ppermute | solution.py:579
  10.2 9.7 %collective-permute-start.6 = (bf16[2,80,384]{2,1,0:T(8,128)(2,1)S(1)}, bf16[2,80,384]{2,1,0:T(8,128)(2,1)S(1)}, u32[]{:S(2)}, u32[]{:S(2)}) collective-permute-start(bf16[2,80,384]{2,1,0:T(8,128)(2,1)S(1)} %get-tuple-element.30), channel_id=1, source_target_pairs={{0,8},{2,14},{4,12},{6,10},{8,0},{10,6},{12,4},{14,2},{16,24},{18,... | collective-permute-start | bytes 368648 | tf_op jit(solution)/shard_map/ppermute | solution.py:579
  10.4 10.0 %collective-permute-start.2 = (bf16[80,384]{1,0:T(8,128)(2,1)S(1)}, bf16[80,384]{1,0:T(8,128)(2,1)S(1)}, u32[]{:S(2)}, u32[]{:S(2)}) collective-permute-start(bf16[80,384]{1,0:T(8,128)(2,1)S(1)} %get-tuple-element.27), channel_id=1, source_target_pairs={{0,4},{2,6},{4,0},{6,2},{8,12},{10,14},{12,8},{14,10},{16,20},{18,... | collective-permute-start | bytes 184328 | tf_op jit(solution)/shard_map/ppermute | solution.py:579
  18.1 3.6 %collective-permute-start.7 = (bf16[2,80,384]{2,1,0:T(8,128)(2,1)S(1)}, bf16[2,80,384]{2,1,0:T(8,128)(2,1)S(1)}, u32[]{:S(2)}, u32[]{:S(2)}) collective-permute-start(bf16[2,80,384]{2,1,0:T(8,128)(2,1)S(1)} %collective-permute-done.4.refs_0_), channel_id=1, source_target_pairs={{0,2},{2,0},{4,6},{6,4},{8,10},{10,8},{12,14},{14,12},{16,18},{18,... | collective-permute-start | bytes 368648 | tf_op jit(solution)/shard_map/ppermute | solution.py:575
  18.1 3.6 %collective-permute-start.8 = (bf16[2,80,384]{2,1,0:T(8,128)(2,1)S(1)}, bf16[2,80,384]{2,1,0:T(8,128)(2,1)S(1)}, u32[]{:S(2)}, u32[]{:S(2)}) collective-permute-start(bf16[2,80,384]{2,1,0:T(8,128)(2,1)S(1)} %collective-permute-done.5.refs_1_), channel_id=1, source_target_pairs={{0,2},{2,0},{4,6},{6,4},{8,10},{10,8},{12,14},{14,12},{16,18},{18,... | collective-permute-start | bytes 368648 | tf_op jit(solution)/shard_map/ppermute | solution.py:575
  19.9 1.8 %collective-permute-start.9 = (bf16[2,80,384]{2,1,0:T(8,128)(2,1)S(1)}, bf16[2,80,384]{2,1,0:T(8,128)(2,1)S(1)}, u32[]{:S(2)}, u32[]{:S(2)}) collective-permute-start(bf16[2,80,384]{2,1,0:T(8,128)(2,1)S(1)} %collective-permute-done.6.refs_2_), channel_id=1, source_target_pairs={{0,2},{2,0},{4,6},{6,4},{8,10},{10,8},{12,14},{14,12},{16,18},{18,... | collective-permute-start | bytes 368648 | tf_op jit(solution)/shard_map/ppermute | solution.py:575
  20.4 1.2 %collective-permute-start.3 = (bf16[80,384]{1,0:T(8,128)(2,1)S(1)}, bf16[80,384]{1,0:T(8,128)(2,1)S(1)}, u32[]{:S(2)}, u32[]{:S(2)}) collective-permute-start(bf16[80,384]{1,0:T(8,128)(2,1)S(1)} %collective-permute-done.2.side_ref), channel_id=1, source_target_pairs={{0,2},{2,0},{4,6},{6,4},{8,10},{10,8},{12,14},{14,12},{16,18},{18,... | collective-permute-start | bytes 184328 | tf_op jit(solution)/shard_map/ppermute | solution.py:575
  21.7 2.6 %copy-start.3 = (f32[2,8,96,96]{3,2,1,0:T(8,128)S(1)}, f32[2,8,96,96]{3,2,1,0:T(8,128)}, u32[]{:S(2)}) copy-start(f32[2,8,96,96]{3,2,1,0:T(8,128)} %win_ref.1) | copy-start | bytes 1769476
  21.7 2.6 %copy-start.4 = (f32[2,8,96,96]{3,2,1,0:T(8,128)S(1)}, f32[2,8,96,96]{3,2,1,0:T(8,128)}, u32[]{:S(2)}) copy-start(f32[2,8,96,96]{3,2,1,0:T(8,128)} %wout_ref.1) | copy-start | bytes 1769476
  21.7 2.6 %copy-start.5 = (bf16[640,80]{1,0:T(8,128)(2,1)S(1)}, bf16[640,80]{1,0:T(8,128)(2,1)}, u32[]{:S(2)}) copy-start(bf16[640,80]{1,0:T(8,128)(2,1)} %constant.39.clone.table_ref) | copy-start | bytes 307204
  21.7 2.6 %copy-start.6 = (f32[2,8,96]{2,1,0:T(8,128)S(1)}, f32[2,8,96]{2,1,0:T(8,128)}, u32[]{:S(2)}) copy-start(f32[2,8,96]{2,1,0:T(8,128)} %bin_ref.1) | copy-start | bytes 18436
  22.8 8.4 %collective-permute-start.10 = (bf16[336,384]{1,0:T(8,128)(2,1)S(1)}, bf16[336,384]{1,0:T(8,128)(2,1)S(1)}, u32[]{:S(2)}, u32[]{:S(2)}) collective-permute-start(bf16[336,384]{1,0:T(8,128)(2,1)S(1)} %shard_map.113.spec_ref), channel_id=1, source_target_pairs={{0,1},{1,0},{2,3},{3,2},{4,5},{5,4},{6,7},{7,6},{8,9},{9,8},{10,11... | collective-permute-start | bytes 774152 | tf_op jit(solution)/shard_map/ppermute | solution.py:582
  25.6 11.3 %copy-start.1 = (bf16[8,2,128,256]{3,2,1,0:T(8,128)(2,1)S(1)}, bf16[8,2,128,256]{3,2,1,0:T(8,128)(2,1)}, u32[]{:S(2)}) copy-start(bf16[8,2,128,256]{3,2,1,0:T(8,128)(2,1)} %constant.40.clone.table_ref) | copy-start | bytes 3145732
  35.0 1.9 %collective-permute-start.11 = (f32[5,64,192]{2,1,0:T(8,128)S(1)}, f32[5,64,192]{2,1,0:T(8,128)S(1)}, u32[]{:S(2)}, u32[]{:S(2)}) collective-permute-start(f32[5,64,192]{2,1,0:T(8,128)S(1)} %get-tuple-element.34.own_ref), channel_id=1, source_target_pairs={{0,2},{2,0},{4,6},{6,4},{8,10},{10,8},{12,14},{14,12},{16,18},{18,... | collective-permute-start | bytes 737288 | tf_op jit(solution)/shard_map/ppermute | solution.py:575
  35.1 1.8 %collective-permute-start.12 = (f32[104,384]{1,0:T(8,128)S(1)}, f32[104,384]{1,0:T(8,128)S(1)}, u32[]{:S(2)}, u32[]{:S(2)}) collective-permute-start(f32[104,384]{1,0:T(8,128)S(1)} %get-tuple-element.35.sum_ref), channel_id=1, source_target_pairs={{0,2},{2,0},{4,6},{6,4},{8,10},{10,8},{12,14},{14,12},{16,18},{18,... | collective-permute-start | bytes 479240 | tf_op jit(solution)/shard_map/ppermute | solution.py:575
  38.2 14.2 %collective-permute-start.14 = (bf16[176,384]{1,0:T(8,128)(2,1)S(1)}, bf16[176,384]{1,0:T(8,128)(2,1)S(1)}, u32[]{:S(2)}, u32[]{:S(2)}) collective-permute-start(bf16[176,384]{1,0:T(8,128)(2,1)S(1)} %get-tuple-element.38), channel_id=1, source_target_pairs={{0,16},{2,22},{4,20},{6,18},{8,24},{10,30},{12,28},{14,26},{16,0},... | collective-permute-start | bytes 405512 | tf_op jit(solution)/shard_map/ppermute | solution.py:579
  42.2 10.1 %collective-permute-start.15 = (bf16[176,384]{1,0:T(8,128)(2,1)S(1)}, bf16[176,384]{1,0:T(8,128)(2,1)S(1)}, u32[]{:S(2)}, u32[]{:S(2)}) collective-permute-start(bf16[176,384]{1,0:T(8,128)(2,1)S(1)} %get-tuple-element.41), channel_id=1, source_target_pairs={{0,24},{2,30},{4,28},{6,26},{8,16},{10,22},{12,20},{14,18},{16,8},... | collective-permute-start | bytes 405512 | tf_op jit(solution)/shard_map/ppermute | solution.py:579
  42.7 11.5 %collective-permute-start.16 = (bf16[176,384]{1,0:T(8,128)(2,1)S(1)}, bf16[176,384]{1,0:T(8,128)(2,1)S(1)}, u32[]{:S(2)}, u32[]{:S(2)}) collective-permute-start(bf16[176,384]{1,0:T(8,128)(2,1)S(1)} %get-tuple-element.42), channel_id=1, source_target_pairs={{0,8},{2,14},{4,12},{6,10},{8,0},{10,6},{12,4},{14,2},{16,24},{18,... | collective-permute-start | bytes 405512 | tf_op jit(solution)/shard_map/ppermute | solution.py:579
  42.9 7.0 %collective-permute-start.13 = (bf16[136,384]{1,0:T(8,128)(2,1)S(1)}, bf16[136,384]{1,0:T(8,128)(2,1)S(1)}, u32[]{:S(2)}, u32[]{:S(2)}) collective-permute-start(bf16[136,384]{1,0:T(8,128)(2,1)S(1)} %get-tuple-element.37), channel_id=1, source_target_pairs={{0,4},{2,6},{4,0},{6,2},{8,12},{10,14},{12,8},{14,10},{16,20},{18,... | collective-permute-start | bytes 313352 | tf_op jit(solution)/shard_map/ppermute | solution.py:579
  52.3 3.2 %collective-permute-start.17 = (bf16[176,384]{1,0:T(8,128)(2,1)S(1)}, bf16[176,384]{1,0:T(8,128)(2,1)S(1)}, u32[]{:S(2)}, u32[]{:S(2)}) collective-permute-start(bf16[176,384]{1,0:T(8,128)(2,1)S(1)} %collective-permute-done.14.refs_2_), channel_id=1, source_target_pairs={{0,2},{2,0},{4,6},{6,4},{8,10},{10,8},{12,14},{14,12},{16,18},{18,... | collective-permute-start | bytes 405512 | tf_op jit(solution)/shard_map/ppermute | solution.py:575
  52.3 3.2 %collective-permute-start.18 = (bf16[176,384]{1,0:T(8,128)(2,1)S(1)}, bf16[176,384]{1,0:T(8,128)(2,1)S(1)}, u32[]{:S(2)}, u32[]{:S(2)}) collective-permute-start(bf16[176,384]{1,0:T(8,128)(2,1)S(1)} %collective-permute-done.15.refs_3_), channel_id=1, source_target_pairs={{0,2},{2,0},{4,6},{6,4},{8,10},{10,8},{12,14},{14,12},{16,18},{18,... | collective-permute-start | bytes 405512 | tf_op jit(solution)/shard_map/ppermute | solution.py:575
  54.2 1.4 %collective-permute-start.19 = (bf16[176,384]{1,0:T(8,128)(2,1)S(1)}, bf16[176,384]{1,0:T(8,128)(2,1)S(1)}, u32[]{:S(2)}, u32[]{:S(2)}) collective-permute-start(bf16[176,384]{1,0:T(8,128)(2,1)S(1)} %collective-permute-done.16.refs_4_), channel_id=1, source_target_pairs={{0,2},{2,0},{4,6},{6,4},{8,10},{10,8},{12,14},{14,12},{16,18},{18,... | collective-permute-start | bytes 405512 | tf_op jit(solution)/shard_map/ppermute | solution.py:575
  54.3 1.2 %copy-start.2 = (bf16[10,14,768]{2,1,0:T(8,128)(2,1)S(1)}, bf16[10,14,768]{2,1,0:T(8,128)(2,1)}, u32[]{:S(2)}) copy-start(bf16[10,14,768]{2,1,0:T(8,128)(2,1)} %cot_ref.1) | copy-start | bytes 645124

commit v6 on v5

--- a/solution.py
+++ b/solution.py
@@ -172,49 +172,32 @@
 
 
 def pack_kernel(width, place_ref, x_ref, g_ref, out_ref):
+    pack_all(width, x_ref, g_ref, out_ref)
+
+
+def pack_all(width, x_ref, g_ref, out_ref):
     rows, cols, channels = x_ref.shape
-    blocks = channels // width
-    pairs = rows // 2
-    for q in range(pairs):
+    for q in range(rows // 2):
         lanes = [ref[2 * q + h].astype(jnp.float32) for h in range(2) for ref in (x_ref, g_ref)]
         lanes = [jnp.pad(x, ((0, PAD - cols), (0, 0))) for x in lanes]
-        for b in range(blocks):
+        for b in range(channels // width):
             pieces = [x[:, b * width : (b + 1) * width] for x in lanes]
             out_ref[b, q * PAD : (q + 1) * PAD, :] = jnp.concatenate(pieces, axis=1).astype(jnp.bfloat16)
 
 
-def pack_served(width, place, member, x_ref, g_ref, pack_ref):
-    rows, cols, channels = x_ref.shape
-    lanes = []
-    for q in range(rows // 2):
-        order = [ref[2 * q + h].astype(jnp.float32) for h in range(2) for ref in (x_ref, g_ref)]
-        lanes.append([jnp.pad(x, ((0, PAD - cols), (0, 0))) for x in order])
-    for b in range(channels // width):
-        other = place ^ b
-
-        @pl.when((other < 2) | ((other & 1) == member))
-        def _(b=b, other=other):
-            slot = jnp.where(other < 2, other, 2 + (other >> 1))
-            for q, order in enumerate(lanes):
-                pieces = [x[:, b * width : (b + 1) * width] for x in order]
-                piece = jnp.concatenate(pieces, axis=1).astype(jnp.bfloat16)
-                pack_ref[slot, q * PAD : (q + 1) * PAD, :] = piece
-
-
 def own_pack_kernel(width, place_ref, fields_ref, pack_ref, side_ref):
-    pack_ref[2] = jnp.zeros_like(pack_ref[2])
-    pack_served(width, place_ref[0], place_ref[1], fields_ref.at[0], fields_ref.at[1], pack_ref)
-    side_ref[...] = pack_ref[1]
+    pack_all(width, fields_ref.at[0], fields_ref.at[1], pack_ref)
+    side_ref[...] = pack_ref[place_ref[0] ^ 1]
 
 
 def pair_kernel(width, place_ref, own_ref, x_ref, g_ref, *refs):
     outs, pack_ref = refs[:-1], refs[-1]
-    member = place_ref[1]
-    pack_served(width, place_ref[0], member, x_ref, g_ref, pack_ref)
+    place, member = place_ref[0], place_ref[1]
+    pack_all(width, x_ref, g_ref, pack_ref)
     for n, ref in enumerate(outs):
-        slot = 0 if n == 0 else 2 + BASES[n - 1] // 2
-        ref[member] = own_ref[slot]
-        ref[1 - member] = pack_ref[slot]
+        target = place if n == 0 else place ^ (BASES[n - 1] + member)
+        ref[member] = own_ref[target]
+        ref[1 - member] = pack_ref[target]
 
 
 def paired_lon_kernel(place_ref, table_ref, own_ref, side_ref, other_side_ref, *refs):
@@ -291,8 +274,9 @@
 def mlp_kernel(lat, inner, shares, pairs, start, scaling, place_ref, table_ref, *refs):
     others = refs[: lat - 1]
     part_ref, form_ref, bias_ref = refs[lat - 1 : lat + 2]
-    back_ref, keep_ref, *rest = refs[lat + 2 :]
-    send_refs, (w_ref,) = rest[: shares - 1], rest[shares - 1 :]
+    back_ref, *rest = refs[lat + 2 :]
+    if shares > 1:
+        keep_ref, *send_refs, w_ref = rest
     member, x = place_ref[1], place_ref[2]
     wide = form_ref.shape[1]
     width = wide // 2
@@ -335,12 +319,19 @@
     matrix = lat_part(table_ref, start, size, part, x)
     back = dot3(matrix, split(jnp.concatenate(lanes, axis=1)), ((0,), (0,)))
     for q in range(pairs):
+        band = []
         for n in range(subs):
             pieces = [
                 back[(h * pairs + q) * tile : (h * pairs + q + 1) * tile, n * width : (n + 1) * width]
                 for h in range(2)
             ]
-            back_ref[q, n * tile : (n + 1) * tile, :] = jnp.concatenate(pieces, axis=1)
+            band.append(jnp.concatenate(pieces, axis=1))
+        for n in range(subs):
+            if shares > 1:
+                back_ref[q, n * tile : (n + 1) * tile, :] = band[n]
+            elif n < subs // 2:
+                row = (q * subs // 2 + n) * tile
+                back_ref[row : row + tile, :] = jnp.concatenate([band[n], band[n + subs // 2]], axis=1)
 
     pieces = []
     for left, right in ((x_parts, p_parts), (split(hidden), g_parts)):
@@ -348,14 +339,18 @@
         pieces.append(total[:width, :width] + total[width:, width:])
         pieces.append(total[:width, width:] - total[width:, :width])
     weights = jnp.concatenate(pieces, axis=1) * scaling
+    bias = jnp.sum(grad_pre, axis=0, keepdims=True) * scaling
+    if shares == 1:
+        start = pairs * subs // 2 * tile
+        back_ref[start : start + width, :] = weights
+        rest = jnp.concatenate([bias, jnp.zeros_like(bias)], axis=1)
+        back_ref[start + width :, :] = jnp.broadcast_to(rest, (back_ref.shape[0] - start - width, 2 * wide))
+        return
     share = width // shares
     w_ref[...] = jnp.zeros_like(w_ref)
     for n in range(shares):
         w_ref[n, :share, :] = weights[n * share : (n + 1) * share]
-    w_ref[0, share : share + 1, :wide] = jnp.sum(grad_pre, axis=0, keepdims=True) * scaling
-    if shares == 1:
-        keep_ref[...] = w_ref[0]
-        return
+    w_ref[0, share : share + 1, :wide] = bias
     keep_ref[...] = w_ref[member]
     for s in range(1, shares):
         send_refs[s - 1][...] = w_ref[lax.rem(member + s, shares)]
@@ -406,19 +401,22 @@
     return encode(columns).astype(jnp.float32) + extra, tail
 
 
-def serve_kernel(place_ref, table_ref, own_ref, other_ref, sum_ref, more_ref, *refs):
+def serve_kernel(pairs, place_ref, table_ref, own_ref, other_ref, *refs):
     outs, wide_ref = refs[:-1], refs[-1]
-    pairs, modes, lanes = own_ref.shape
     count = wide_ref.shape[0]
+    modes, lanes = table_ref.shape[3] // 4, own_ref.shape[1] // 2
+    half = modes // 2
     share = lanes // 2
     table = table_ref[0, 0]
     matrix = (table[:, : 2 * modes], table[:, 2 * modes :])
     for q in range(pairs):
-        total = dot3(matrix, split(jnp.concatenate([own_ref[q], other_ref[q]], axis=0)))
+        bands = [ref[q * half : (q + 1) * half, :] for ref in (own_ref, other_ref)]
+        bands = [x[:, start : start + lanes] for x in bands for start in (0, lanes)]
+        total = dot3(matrix, split(jnp.concatenate(bands, axis=0)))
         part = count * HALF
         columns = jnp.concatenate([total[:part], total[part:]], axis=1)
         wide_ref[:, q * HALF : (q + 1) * HALF, :] = columns.reshape(count, HALF, 2 * lanes)
-    coded, tail = code_all(wide_ref[...], sum_ref[...] + more_ref[...], share)
+    coded, tail = code_all(wide_ref[...], own_ref[pairs * half :, :] + other_ref[pairs * half :, :], share)
     tail = tail[:share]
     for n, ref in enumerate(outs):
         parts = [coded[n]] if n < 2 else [coded[2 * n - 2], coded[2 * n - 1]]
@@ -597,7 +595,7 @@
             functools.partial(own_pack_kernel, width),
             scalars,
             (jnp.stack([features, cotangent]),),
-            (shape((2 + blocks // 2, rows_in, wide), bf16), shape((rows_in, wide), bf16)),
+            (shape((blocks, rows_in, wide), bf16), shape((rows_in, wide), bf16)),
             flops=10**8,
         )
         own, *slots = call(
@@ -605,7 +603,7 @@
             scalars,
             (packed, to_member(features, 1), to_member(cotangent, 1)),
             [shape((2, rows_in, wide), bf16)] * (1 + len(BASES)),
-            scratch=(pltpu.VMEM((2 + blocks // 2, rows_in, wide), bf16),),
+            scratch=(pltpu.VMEM((blocks, rows_in, wide), bf16),),
         )
         side = to_place(side, 1, 1)
         sent = [side, *serve(slots)]
@@ -639,12 +637,16 @@
         specs={2: block_spec, 4: block_spec},
         flops=6 * size * size // lat_count * 2 * subs * width,
     )
-    back, keep, *send = call(
+    if paired:
+        outs = [shape((pairs * modes // 2 + sum_rows, wide), f32)]
+    else:
+        outs = [shape((pairs, modes, 2 * width), f32), *[shape((sum_rows, wide), f32)] * shares]
+    back, *rest = call(
         functools.partial(mlp_kernel, lat_count, inner, shares, pairs, lat_start, scaling),
         scalars,
         (tables, *others, part, forms, bias),
-        (shape((pairs, modes, 2 * width), f32), *[shape((sum_rows, wide), f32)] * shares),
-        scratch=(pltpu.VMEM((shares, sum_rows, wide), f32),),
+        outs,
+        scratch=() if paired else (pltpu.VMEM((shares, sum_rows, wide), f32),),
     )
     backs = [back] + [to_member(back, s) for s in range(1, inner)]
     if paired:
@@ -652,9 +654,9 @@
         count = table.shape[2] // PAD
         outs = [share + data_rows] * 2 + [share + 2 * data_rows] * len(BASES)
         own, side, *slots = call(
-            serve_kernel,
+            functools.partial(serve_kernel, pairs),
             scalars,
-            (table, *backs, keep, to_member(keep, 1)),
+            (table, *backs),
             [shape((n, wide), bf16) for n in outs],
             specs={0: by_place(table)},
             scratch=(pltpu.VMEM((count, data_rows, wide), f32),),
@@ -679,6 +681,7 @@
             [shape(x.shape, x.dtype) for x in (features, weight_in, bias_in, weight_out)],
             scratch=(pltpu.VMEM((blocks, data_rows, wide), f32),),
         )
+    keep, *send = rest
     sums = [keep] + [to_member(send[s - 1], s) for s in range(1, inner)]
     (payload,) = call(
         functools.partial(synth_kernel, inner, synth_start),

time: 58.5 us -> 57.9 us (0.990)
    ppermute x11 -> x10, starting transfers between devices: 2.87 us -> 2.43 us  [to_member(): return lax.ppermute(values, 'lon', turn)]
    ppermute x11 -> x10, waiting for transfers between devices: 2.61 us -> 2.99 us  [to_member(): return lax.ppermute(values, 'lon', turn)]
  transfers between devices with their start and end apart: 20 -> 19, of which waited for: 8 -> 8; matrix products, arithmetic and copies ran while one was open for 2% -> 2% of each run, Pallas kernels for 6% -> 6%
where the time goes in v6:
time: 57.9 us; the launch traced here: 57.7 us
  waiting for transfers between devices  25.6 us (44%)
  starting transfers between devices  16.9 us (29%)
  Pallas kernels  13.1 us (23%)
  other arithmetic  1.29 us (2%)
  between operations  0.79 us (1%)
    ppermute x8, waiting for transfers between devices, to_place(): return lax.ppermute(values, 'lon', turn)  17.1 us
    pallas_call x8, Pallas kernels, call(): pl.pallas_call(kernel, grid_spec=pltpu.PrefetchScalarGridSpec(num_scalar_...  13.1 us
    ppermute x8, starting transfers between devices, to_place(): return lax.ppermute(values, 'lon', turn)  12.9 us
    ppermute x1, waiting for transfers between devices, to_lat(): lax.ppermute(values, 'lat', [(i, (i + step) % lat_count) for i in range(l...  5.5 us
    ppermute x10, waiting for transfers between devices, to_member(): return lax.ppermute(values, 'lon', turn)  2.99 us
    ppermute x10, starting transfers between devices, to_member(): return lax.ppermute(values, 'lon', turn)  2.43 us
    ppermute x1, starting transfers between devices, to_lat(): lax.ppermute(values, 'lat', [(i, (i + step) % lat_count) for i in range(l...  1.56 us
    another operation x1, other arithmetic, body(): jnp.stack([features, cotangent])  1.21 us
  transfers between devices with their start and end apart: 19, of which 8 were waited for; matrix products, arithmetic and copies ran while one was open for 2% of the time, Pallas kernels for 6%

profile of v6, /device:TPU:0, one launch (start us, length us, event | category | flops | bytes accessed | tf_op | source)
XLA Modules:
  0.0 57.7 jit_solution(5080607051458539873)
XLA Ops:
  0.6 0.5 collective-permute-start
  1.1 0.1 collective-permute-start.1
  1.3 1.2 %pad_maximum_fusion.fields_ref = bf16[2,10,14,768]{3,2,1,0:T(8,128)(2,1)S(1)} fusion(bf16[1,10,14,768]{3,2,1,0:T(8,128)(2,1)} %bitcast.5, bf16[1,10,14,768]{3,2,1,0:T(8,128)(2,1)} %bitcast.6), kind=kLoop, calls=%fused_computation | loop fusion | flops 215040 | bytes 860160 | tf_op jit(solution)/shard_map/stack | solution.py:597
  2.5 0.8 %shard_map.111 = (bf16[8,80,384]{2,1,0:T(8,128)(2,1)S(1)}, bf16[80,384]{1,0:T(8,128)(2,1)S(1)}) custom-call(s32[3]{0:T(128)S(1)} %pad_add_fusion.place_ref, bf16[2,10,14,768]{3,2,1,0:T(8,128)(2,1)S(1)} %pad_maximum_fusion.fields_ref), custom_call_target="tpu_custom_call" | custom-call | flops 100000000 | bytes 983040 | tf_op jit(solution)/shard_map/pallas_call | solution.py:159
  3.4 0.8 %shard_map.112 = (bf16[2,80,384]{2,1,0:T(8,128)(2,1)S(1)}, bf16[2,80,384]{2,1,0:T(8,128)(2,1)S(1)}, bf16[2,80,384]{2,1,0:T(8,128)(2,1)S(1)}, bf16[2,80,384]{2,1,0:T(8,128)(2,1)S(1)}) custom-call(s32[3]{0:T(128)S(1)} %pad_add_fusion.place_ref, bf16[8,80,384]{2,1,0:T(8,128)(2,1)S(1)} %get-tuple-element.23.own_ref, ...), custom_call_target="tpu_custom_call" | custom-call | bytes 1413120 | tf_op jit(solution)/shard_map/pallas_call | solution.py:159
  4.2 4.1 %collective-permute-start.4 = (bf16[2,80,384]{2,1,0:T(8,128)(2,1)S(1)}, bf16[2,80,384]{2,1,0:T(8,128)(2,1)S(1)}, u32[]{:S(2)}, u32[]{:S(2)}) collective-permute-start(bf16[2,80,384]{2,1,0:T(8,128)(2,1)S(1)} %get-tuple-element.26), channel_id=1, source_target_pairs={{0,16},{2,22},{4,20},{6,18},{8,24},{10,30},{12,28},{14,26},{16,0},... | collective-permute-start | bytes 368648 | tf_op jit(solution)/shard_map/ppermute | solution.py:577
  8.3 1.3 %collective-permute-start.5 = (bf16[2,80,384]{2,1,0:T(8,128)(2,1)S(1)}, bf16[2,80,384]{2,1,0:T(8,128)(2,1)S(1)}, u32[]{:S(2)}, u32[]{:S(2)}) collective-permute-start(bf16[2,80,384]{2,1,0:T(8,128)(2,1)S(1)} %get-tuple-element.27), channel_id=1, source_target_pairs={{0,24},{2,30},{4,28},{6,26},{8,16},{10,22},{12,20},{14,18},{16,8},... | collective-permute-start | bytes 368648 | tf_op jit(solution)/shard_map/ppermute | solution.py:577
  9.6 0.2 collective-permute-start.6
  9.9 1.5 %collective-permute-start.2 = (bf16[80,384]{1,0:T(8,128)(2,1)S(1)}, bf16[80,384]{1,0:T(8,128)(2,1)S(1)}, u32[]{:S(2)}, u32[]{:S(2)}) collective-permute-start(bf16[80,384]{1,0:T(8,128)(2,1)S(1)} %get-tuple-element.25), channel_id=1, source_target_pairs={{0,4},{2,6},{4,0},{6,2},{8,12},{10,14},{12,8},{14,10},{16,20},{18,... | collective-permute-start | bytes 184328 | tf_op jit(solution)/shard_map/ppermute | solution.py:577
  11.4 6.1 %collective-permute-done.4.refs_0_ = bf16[2,80,384]{2,1,0:T(8,128)(2,1)S(1)} collective-permute-done((bf16[2,80,384]{2,1,0:T(8,128)(2,1)S(1)}, bf16[2,80,384]{2,1,0:T(8,128)(2,1)S(1)}, u32[]{:S(2)}, u32[]{:S(2)}) %collective-permute-start.4) | collective-permute-done | bytes 122912 | tf_op jit(solution)/shard_map/ppermute | solution.py:577
  17.5 0.5 collective-permute-start.8
  18.0 1.3 %collective-permute-done.6.refs_2_ = bf16[2,80,384]{2,1,0:T(8,128)(2,1)S(1)} collective-permute-done((bf16[2,80,384]{2,1,0:T(8,128)(2,1)S(1)}, bf16[2,80,384]{2,1,0:T(8,128)(2,1)S(1)}, u32[]{:S(2)}, u32[]{:S(2)}) %collective-permute-start.6) | collective-permute-done | bytes 122912 | tf_op jit(solution)/shard_map/ppermute | solution.py:577
  19.3 0.6 collective-permute-start.9
  19.9 1.2 %collective-permute-done.3.other_side_ref = bf16[80,384]{1,0:T(8,128)(2,1)S(1)} collective-permute-done((bf16[80,384]{1,0:T(8,128)(2,1)S(1)}, bf16[80,384]{1,0:T(8,128)(2,1)S(1)}, u32[]{:S(2)}, u32[]{:S(2)}) %collective-permute-start.3) | collective-permute-done | bytes 61472 | tf_op jit(solution)/shard_map/ppermute | solution.py:573
  21.2 1.0 %shard_map.113.spec_ref = bf16[336,384]{1,0:T(8,128)(2,1)S(1)} custom-call(s32[3]{0:T(128)S(1)} %pad_add_fusion.place_ref, bf16[8,2,128,256]{3,2,1,0:T(8,128)(2,1)S(1)} %copy-done, bf16[2,80,384]{2,1,0:T(8,128)(2,1)S(1)} %get-tuple-element.24.own_ref, bf16[80,384]{1,0:T(8,128)(2,1)S(1)} %collective-permute-done.2.side_ref, ...), custom_call_target="tpu_custom_call" | custom-call | bytes 2289664 | tf_op jit(solution)/shard_map/pallas_call | solution.py:159
  22.3 1.6 %collective-permute-start.10 = (bf16[336,384]{1,0:T(8,128)(2,1)S(1)}, bf16[336,384]{1,0:T(8,128)(2,1)S(1)}, u32[]{:S(2)}, u32[]{:S(2)}) collective-permute-start(bf16[336,384]{1,0:T(8,128)(2,1)S(1)} %shard_map.113.spec_ref), channel_id=1, source_target_pairs={{0,1},{1,0},{2,3},{3,2},{4,5},{5,4},{6,7},{7,6},{8,9},{9,8},{10,11... | collective-permute-start | bytes 774152 | tf_op jit(solution)/shard_map/ppermute | solution.py:580
  23.8 1.3 %shard_map.114 = (f32[160,1536]{1,0:T(8,128)S(1)}, bf16[4,192,192]{2,1,0:T(8,128)(2,1)S(1)}, f32[8,192]{1,0:T(8,128)S(1)}) custom-call(s32[3]{0:T(128)S(1)} %pad_add_fusion.place_ref, bf16[640,80]{1,0:T(8,128)(2,1)S(1)} %copy-done.5, bf16[336,384]{1,0:T(8,128)(2,1)S(1)} %shard_map.113.spec_ref, f32[2,8,96,96]{3,2,1,0:T(8,128)S(1)} %copy-done.3, ...), custom_call_target="tpu_custom_call" | custom-call | flops 117964800 | bytes 2830336 | tf_op jit(solution)/shard_map/pallas_call | solution.py:159
  25.1 5.5 %collective-permute-done.10.refs_0_ = bf16[336,384]{1,0:T(8,128)(2,1)S(1)} collective-permute-done((bf16[336,384]{1,0:T(8,128)(2,1)S(1)}, bf16[336,384]{1,0:T(8,128)(2,1)S(1)}, u32[]{:S(2)}, u32[]{:S(2)}) %collective-permute-start.10) | collective-permute-done | bytes 258080 | tf_op jit(solution)/shard_map/ppermute | solution.py:580
  30.6 3.9 %shard_map.115.own_ref = f32[264,384]{1,0:T(8,128)S(1)} custom-call(s32[3]{0:T(128)S(1)} %pad_add_fusion.place_ref, bf16[640,80]{1,0:T(8,128)(2,1)S(1)} %copy-done.5, bf16[336,384]{1,0:T(8,128)(2,1)S(1)} %collective-permute-done.10.refs_0_, f32[160,1536]{1,0:T(8,128)S(1)} %get-tuple-element.29.refs_1_, bf16[4,192,192]{2,1,0:T(8,128)(2,1)S(1)} %get-tuple-element.30.refs_2_, ...), custom_call_target="tpu_custom_call" | custom-call | bytes 2050048 | tf_op jit(solution)/shard_map/pallas_call | solution.py:159
  34.6 1.7 %collective-permute-done.11.other_ref = f32[264,384]{1,0:T(8,128)S(1)} collective-permute-done((f32[264,384]{1,0:T(8,128)S(1)}, f32[264,384]{1,0:T(8,128)S(1)}, u32[]{:S(2)}, u32[]{:S(2)}) %collective-permute-start.11) | collective-permute-done | bytes 405536 | tf_op jit(solution)/shard_map/ppermute | solution.py:573
  36.3 1.3 %shard_map.116 = (bf16[136,384]{1,0:T(8,128)(2,1)S(1)}, bf16[136,384]{1,0:T(8,128)(2,1)S(1)}, bf16[176,384]{1,0:T(8,128)(2,1)S(1)}, bf16[176,384]{1,0:T(8,128)(2,1)S(1)}, bf16[176,384]{1,0:T(8,128)(2,1)S(1)}) custom-call(s32[3]{0:T(128)S(1)} %pad_add_fusion.place_ref, bf16[8,2,128,256]{3,2,1,0:T(8,128)(2,1)S(1)} %copy-done.1, ...), custom_call_target="tpu_custom_call" | custom-call | bytes 2473984 | tf_op jit(solution)/shard_map/pallas_call | solution.py:159
  37.6 4.0 %collective-permute-start.13 = (bf16[176,384]{1,0:T(8,128)(2,1)S(1)}, bf16[176,384]{1,0:T(8,128)(2,1)S(1)}, u32[]{:S(2)}, u32[]{:S(2)}) collective-permute-start(bf16[176,384]{1,0:T(8,128)(2,1)S(1)} %get-tuple-element.34), channel_id=1, source_target_pairs={{0,16},{2,22},{4,20},{6,18},{8,24},{10,30},{12,28},{14,26},{16,0},... | collective-permute-start | bytes 405512 | tf_op jit(solution)/shard_map/ppermute | solution.py:577
  41.6 0.4 collective-permute-start.14
  42.1 0.2 collective-permute-start.15
  42.3 1.1 %collective-permute-start.12 = (bf16[136,384]{1,0:T(8,128)(2,1)S(1)}, bf16[136,384]{1,0:T(8,128)(2,1)S(1)}, u32[]{:S(2)}, u32[]{:S(2)}) collective-permute-start(bf16[136,384]{1,0:T(8,128)(2,1)S(1)} %get-tuple-element.33), channel_id=1, source_target_pairs={{0,4},{2,6},{4,0},{6,2},{8,12},{10,14},{12,8},{14,10},{16,20},{18,... | collective-permute-start | bytes 313352 | tf_op jit(solution)/shard_map/ppermute | solution.py:577
  43.4 5.9 %collective-permute-done.12.refs_1_ = bf16[136,384]{1,0:T(8,128)(2,1)S(1)} collective-permute-done((bf16[136,384]{1,0:T(8,128)(2,1)S(1)}, bf16[136,384]{1,0:T(8,128)(2,1)S(1)}, u32[]{:S(2)}, u32[]{:S(2)}) %collective-permute-start.12) | collective-permute-done | bytes 104480 | tf_op jit(solution)/shard_map/ppermute | solution.py:577
  49.3 2.4 %collective-permute-done.13.refs_2_ = bf16[176,384]{1,0:T(8,128)(2,1)S(1)} collective-permute-done((bf16[176,384]{1,0:T(8,128)(2,1)S(1)}, bf16[176,384]{1,0:T(8,128)(2,1)S(1)}, u32[]{:S(2)}, u32[]{:S(2)}) %collective-permute-start.13) | collective-permute-done | bytes 135200 | tf_op jit(solution)/shard_map/ppermute | solution.py:577
  51.7 0.5 collective-permute-start.17
  52.2 1.3 %collective-permute-done.15.refs_4_ = bf16[176,384]{1,0:T(8,128)(2,1)S(1)} collective-permute-done((bf16[176,384]{1,0:T(8,128)(2,1)S(1)}, bf16[176,384]{1,0:T(8,128)(2,1)S(1)}, u32[]{:S(2)}, u32[]{:S(2)}) %collective-permute-start.15) | collective-permute-done | bytes 135200 | tf_op jit(solution)/shard_map/ppermute | solution.py:577
  53.6 0.2 collective-permute-start.18
  53.7 1.2 %shard_map.117 = (f32[5,40,384]{2,1,0:T(8,128)S(1)}, f32[5,96,384]{2,1,0:T(8,128)S(1)}, f32[5,192]{1,0:T(8,128)S(1)}) custom-call(s32[3]{0:T(128)S(1)} %pad_add_fusion.place_ref, bf16[136,384]{1,0:T(8,128)(2,1)S(1)} %get-tuple-element.32.refs_0_, bf16[136,384]{1,0:T(8,128)(2,1)S(1)} %collective-permute-done.12.refs_1_, ...), custom_call_target="tpu_custom_call" | custom-call | bytes 1662720 | tf_op jit(solution)/shard_map/pallas_call | solution.py:159
  55.0 2.7 %shard_map.118 = (bf16[10,14,768]{2,1,0:T(8,128)(2,1)}, f32[2,8,96,96]{3,2,1,0:T(8,128)}, f32[2,8,96]{2,1,0:T(8,128)}, f32[2,8,96,96]{3,2,1,0:T(8,128)}) custom-call(s32[3]{0:T(128)S(1)} %pad_add_fusion.place_ref, f32[5,40,384]{2,1,0:T(8,128)S(1)} %get-tuple-element.39.columns_ref, f32[5,96,384]{2,1,0:T(8,128)S(1)} %get-tuple-element.40.weights_ref, ...), custom_call_target="tpu_custom_call" | custom-call | bytes 3069696 | tf_op jit(solution)/shard_map/pallas_call | solution.py:159
  (30 shorter events, 0.2 us)
Async XLA Ops:
  0.6 2.7 %collective-permute-start = (bf16[10,14,768]{2,1,0:T(8,128)(2,1)}, bf16[10,14,768]{2,1,0:T(8,128)(2,1)S(1)}, u32[]{:S(2)}, u32[]{:S(2)}) collective-permute-start(bf16[10,14,768]{2,1,0:T(8,128)(2,1)} %param.8), channel_id=1, source_target_pairs={{0,2},{2,0},{4,6},{6,4},{8,10},{10,8},{12,14},{14,12},{16,18},{18,... | collective-permute-start | bytes 645128 | tf_op jit(solution)/shard_map/ppermute | solution.py:573
  1.1 2.2 %collective-permute-start.1 = (bf16[10,14,768]{2,1,0:T(8,128)(2,1)}, bf16[10,14,768]{2,1,0:T(8,128)(2,1)S(1)}, u32[]{:S(2)}, u32[]{:S(2)}) collective-permute-start(bf16[10,14,768]{2,1,0:T(8,128)(2,1)} %cot_ref.1), channel_id=1, source_target_pairs={{0,2},{2,0},{4,6},{6,4},{8,10},{10,8},{12,14},{14,12},{16,18},{18,... | collective-permute-start | bytes 645128 | tf_op jit(solution)/shard_map/ppermute | solution.py:573
  1.3 19.9 %copy-start = (bf16[8,2,128,256]{3,2,1,0:T(8,128)(2,1)S(1)}, bf16[8,2,128,256]{3,2,1,0:T(8,128)(2,1)}, u32[]{:S(2)}) copy-start(bf16[8,2,128,256]{3,2,1,0:T(8,128)(2,1)} %constant.38.clone.table_ref) | copy-start | bytes 3145732
  4.2 13.3 %collective-permute-start.4 = (bf16[2,80,384]{2,1,0:T(8,128)(2,1)S(1)}, bf16[2,80,384]{2,1,0:T(8,128)(2,1)S(1)}, u32[]{:S(2)}, u32[]{:S(2)}) collective-permute-start(bf16[2,80,384]{2,1,0:T(8,128)(2,1)S(1)} %get-tuple-element.26), channel_id=1, source_target_pairs={{0,16},{2,22},{4,20},{6,18},{8,24},{10,30},{12,28},{14,26},{16,0},... | collective-permute-start | bytes 368648 | tf_op jit(solution)/shard_map/ppermute | solution.py:577
  8.3 9.2 %collective-permute-start.5 = (bf16[2,80,384]{2,1,0:T(8,128)(2,1)S(1)}, bf16[2,80,384]{2,1,0:T(8,128)(2,1)S(1)}, u32[]{:S(2)}, u32[]{:S(2)}) collective-permute-start(bf16[2,80,384]{2,1,0:T(8,128)(2,1)S(1)} %get-tuple-element.27), channel_id=1, source_target_pairs={{0,24},{2,30},{4,28},{6,26},{8,16},{10,22},{12,20},{14,18},{16,8},... | collective-permute-start | bytes 368648 | tf_op jit(solution)/shard_map/ppermute | solution.py:577
  9.6 9.7 %collective-permute-start.6 = (bf16[2,80,384]{2,1,0:T(8,128)(2,1)S(1)}, bf16[2,80,384]{2,1,0:T(8,128)(2,1)S(1)}, u32[]{:S(2)}, u32[]{:S(2)}) collective-permute-start(bf16[2,80,384]{2,1,0:T(8,128)(2,1)S(1)} %get-tuple-element.28), channel_id=1, source_target_pairs={{0,8},{2,14},{4,12},{6,10},{8,0},{10,6},{12,4},{14,2},{16,24},{18,... | collective-permute-start | bytes 368648 | tf_op jit(solution)/shard_map/ppermute | solution.py:577
  9.9 10.0 %collective-permute-start.2 = (bf16[80,384]{1,0:T(8,128)(2,1)S(1)}, bf16[80,384]{1,0:T(8,128)(2,1)S(1)}, u32[]{:S(2)}, u32[]{:S(2)}) collective-permute-start(bf16[80,384]{1,0:T(8,128)(2,1)S(1)} %get-tuple-element.25), channel_id=1, source_target_pairs={{0,4},{2,6},{4,0},{6,2},{8,12},{10,14},{12,8},{14,10},{16,20},{18,... | collective-permute-start | bytes 184328 | tf_op jit(solution)/shard_map/ppermute | solution.py:577
  17.5 3.6 %collective-permute-start.7 = (bf16[2,80,384]{2,1,0:T(8,128)(2,1)S(1)}, bf16[2,80,384]{2,1,0:T(8,128)(2,1)S(1)}, u32[]{:S(2)}, u32[]{:S(2)}) collective-permute-start(bf16[2,80,384]{2,1,0:T(8,128)(2,1)S(1)} %collective-permute-done.4.refs_0_), channel_id=1, source_target_pairs={{0,2},{2,0},{4,6},{6,4},{8,10},{10,8},{12,14},{14,12},{16,18},{18,... | collective-permute-start | bytes 368648 | tf_op jit(solution)/shard_map/ppermute | solution.py:573
  17.5 3.6 %collective-permute-start.8 = (bf16[2,80,384]{2,1,0:T(8,128)(2,1)S(1)}, bf16[2,80,384]{2,1,0:T(8,128)(2,1)S(1)}, u32[]{:S(2)}, u32[]{:S(2)}) collective-permute-start(bf16[2,80,384]{2,1,0:T(8,128)(2,1)S(1)} %collective-permute-done.5.refs_1_), channel_id=1, source_target_pairs={{0,2},{2,0},{4,6},{6,4},{8,10},{10,8},{12,14},{14,12},{16,18},{18,... | collective-permute-start | bytes 368648 | tf_op jit(solution)/shard_map/ppermute | solution.py:573
  19.3 1.8 %collective-permute-start.9 = (bf16[2,80,384]{2,1,0:T(8,128)(2,1)S(1)}, bf16[2,80,384]{2,1,0:T(8,128)(2,1)S(1)}, u32[]{:S(2)}, u32[]{:S(2)}) collective-permute-start(bf16[2,80,384]{2,1,0:T(8,128)(2,1)S(1)} %collective-permute-done.6.refs_2_), channel_id=1, source_target_pairs={{0,2},{2,0},{4,6},{6,4},{8,10},{10,8},{12,14},{14,12},{16,18},{18,... | collective-permute-start | bytes 368648 | tf_op jit(solution)/shard_map/ppermute | solution.py:573
  19.9 1.2 %collective-permute-start.3 = (bf16[80,384]{1,0:T(8,128)(2,1)S(1)}, bf16[80,384]{1,0:T(8,128)(2,1)S(1)}, u32[]{:S(2)}, u32[]{:S(2)}) collective-permute-start(bf16[80,384]{1,0:T(8,128)(2,1)S(1)} %collective-permute-done.2.side_ref), channel_id=1, source_target_pairs={{0,2},{2,0},{4,6},{6,4},{8,10},{10,8},{12,14},{14,12},{16,18},{18,... | collective-permute-start | bytes 184328 | tf_op jit(solution)/shard_map/ppermute | solution.py:573
  21.2 2.7 %copy-start.3 = (f32[2,8,96,96]{3,2,1,0:T(8,128)S(1)}, f32[2,8,96,96]{3,2,1,0:T(8,128)}, u32[]{:S(2)}) copy-start(f32[2,8,96,96]{3,2,1,0:T(8,128)} %win_ref.1) | copy-start | bytes 1769476
  21.2 2.6 %copy-start.4 = (f32[2,8,96,96]{3,2,1,0:T(8,128)S(1)}, f32[2,8,96,96]{3,2,1,0:T(8,128)}, u32[]{:S(2)}) copy-start(f32[2,8,96,96]{3,2,1,0:T(8,128)} %wout_ref.1) | copy-start | bytes 1769476
  21.2 2.6 %copy-start.5 = (bf16[640,80]{1,0:T(8,128)(2,1)S(1)}, bf16[640,80]{1,0:T(8,128)(2,1)}, u32[]{:S(2)}) copy-start(bf16[640,80]{1,0:T(8,128)(2,1)} %constant.39.clone.table_ref) | copy-start | bytes 307204
  21.2 2.6 %copy-start.6 = (f32[2,8,96]{2,1,0:T(8,128)S(1)}, f32[2,8,96]{2,1,0:T(8,128)}, u32[]{:S(2)}) copy-start(f32[2,8,96]{2,1,0:T(8,128)} %bin_ref.1) | copy-start | bytes 18436
  22.3 8.4 %collective-permute-start.10 = (bf16[336,384]{1,0:T(8,128)(2,1)S(1)}, bf16[336,384]{1,0:T(8,128)(2,1)S(1)}, u32[]{:S(2)}, u32[]{:S(2)}) collective-permute-start(bf16[336,384]{1,0:T(8,128)(2,1)S(1)} %shard_map.113.spec_ref), channel_id=1, source_target_pairs={{0,1},{1,0},{2,3},{3,2},{4,5},{5,4},{6,7},{7,6},{8,9},{9,8},{10,11... | collective-permute-start | bytes 774152 | tf_op jit(solution)/shard_map/ppermute | solution.py:580
  30.6 5.7 %copy-start.1 = (bf16[8,2,128,256]{3,2,1,0:T(8,128)(2,1)S(1)}, bf16[8,2,128,256]{3,2,1,0:T(8,128)(2,1)}, u32[]{:S(2)}) copy-start(bf16[8,2,128,256]{3,2,1,0:T(8,128)(2,1)} %constant.40.clone.table_ref) | copy-start | bytes 3145732
  34.5 1.8 %collective-permute-start.11 = (f32[264,384]{1,0:T(8,128)S(1)}, f32[264,384]{1,0:T(8,128)S(1)}, u32[]{:S(2)}, u32[]{:S(2)}) collective-permute-start(f32[264,384]{1,0:T(8,128)S(1)} %shard_map.115.own_ref), channel_id=1, source_target_pairs={{0,2},{2,0},{4,6},{6,4},{8,10},{10,8},{12,14},{14,12},{16,18},{18,... | collective-permute-start | bytes 1216520 | tf_op jit(solution)/shard_map/ppermute | solution.py:573
  37.6 14.1 %collective-permute-start.13 = (bf16[176,384]{1,0:T(8,128)(2,1)S(1)}, bf16[176,384]{1,0:T(8,128)(2,1)S(1)}, u32[]{:S(2)}, u32[]{:S(2)}) collective-permute-start(bf16[176,384]{1,0:T(8,128)(2,1)S(1)} %get-tuple-element.34), channel_id=1, source_target_pairs={{0,16},{2,22},{4,20},{6,18},{8,24},{10,30},{12,28},{14,26},{16,0},... | collective-permute-start | bytes 405512 | tf_op jit(solution)/shard_map/ppermute | solution.py:577
  41.6 10.1 %collective-permute-start.14 = (bf16[176,384]{1,0:T(8,128)(2,1)S(1)}, bf16[176,384]{1,0:T(8,128)(2,1)S(1)}, u32[]{:S(2)}, u32[]{:S(2)}) collective-permute-start(bf16[176,384]{1,0:T(8,128)(2,1)S(1)} %get-tuple-element.37), channel_id=1, source_target_pairs={{0,24},{2,30},{4,28},{6,26},{8,16},{10,22},{12,20},{14,18},{16,8},... | collective-permute-start | bytes 405512 | tf_op jit(solution)/shard_map/ppermute | solution.py:577
  42.1 11.5 %collective-permute-start.15 = (bf16[176,384]{1,0:T(8,128)(2,1)S(1)}, bf16[176,384]{1,0:T(8,128)(2,1)S(1)}, u32[]{:S(2)}, u32[]{:S(2)}) collective-permute-start(bf16[176,384]{1,0:T(8,128)(2,1)S(1)} %get-tuple-element.38), channel_id=1, source_target_pairs={{0,8},{2,14},{4,12},{6,10},{8,0},{10,6},{12,4},{14,2},{16,24},{18,... | collective-permute-start | bytes 405512 | tf_op jit(solution)/shard_map/ppermute | solution.py:577
  42.3 7.1 %collective-permute-start.12 = (bf16[136,384]{1,0:T(8,128)(2,1)S(1)}, bf16[136,384]{1,0:T(8,128)(2,1)S(1)}, u32[]{:S(2)}, u32[]{:S(2)}) collective-permute-start(bf16[136,384]{1,0:T(8,128)(2,1)S(1)} %get-tuple-element.33), channel_id=1, source_target_pairs={{0,4},{2,6},{4,0},{6,2},{8,12},{10,14},{12,8},{14,10},{16,20},{18,... | collective-permute-start | bytes 313352 | tf_op jit(solution)/shard_map/ppermute | solution.py:577
  51.7 3.2 %collective-permute-start.16 = (bf16[176,384]{1,0:T(8,128)(2,1)S(1)}, bf16[176,384]{1,0:T(8,128)(2,1)S(1)}, u32[]{:S(2)}, u32[]{:S(2)}) collective-permute-start(bf16[176,384]{1,0:T(8,128)(2,1)S(1)} %collective-permute-done.13.refs_2_), channel_id=1, source_target_pairs={{0,2},{2,0},{4,6},{6,4},{8,10},{10,8},{12,14},{14,12},{16,18},{18,... | collective-permute-start | bytes 405512 | tf_op jit(solution)/shard_map/ppermute | solution.py:573
  51.7 3.2 %collective-permute-start.17 = (bf16[176,384]{1,0:T(8,128)(2,1)S(1)}, bf16[176,384]{1,0:T(8,128)(2,1)S(1)}, u32[]{:S(2)}, u32[]{:S(2)}) collective-permute-start(bf16[176,384]{1,0:T(8,128)(2,1)S(1)} %collective-permute-done.14.refs_3_), channel_id=1, source_target_pairs={{0,2},{2,0},{4,6},{6,4},{8,10},{10,8},{12,14},{14,12},{16,18},{18,... | collective-permute-start | bytes 405512 | tf_op jit(solution)/shard_map/ppermute | solution.py:573
  53.6 1.4 %collective-permute-start.18 = (bf16[176,384]{1,0:T(8,128)(2,1)S(1)}, bf16[176,384]{1,0:T(8,128)(2,1)S(1)}, u32[]{:S(2)}, u32[]{:S(2)}) collective-permute-start(bf16[176,384]{1,0:T(8,128)(2,1)S(1)} %collective-permute-done.15.refs_4_), channel_id=1, source_target_pairs={{0,2},{2,0},{4,6},{6,4},{8,10},{10,8},{12,14},{14,12},{16,18},{18,... | collective-permute-start | bytes 405512 | tf_op jit(solution)/shard_map/ppermute | solution.py:573
  53.7 1.2 %copy-start.2 = (bf16[10,14,768]{2,1,0:T(8,128)(2,1)S(1)}, bf16[10,14,768]{2,1,0:T(8,128)(2,1)}, u32[]{:S(2)}) copy-start(bf16[10,14,768]{2,1,0:T(8,128)(2,1)} %cot_ref.1) | copy-start | bytes 645124

commit v7 on v6

--- a/solution.py
+++ b/solution.py
@@ -13,7 +13,7 @@
 MODE_DEV = 4
 PAD = 16
 HALF = PAD // 2
-BASES = (4, 6, 2)
+BASES = (6, 2, 4)
 SUB = 4
 SPARE = 6
 POWER = 13.0

time: 57.9 us -> 57.2 us (0.988)
  waiting for transfers between devices: 25.6 us -> 24.9 us
where the time goes in v7:
time: 57.2 us; the launch traced here: 57 us
  waiting for transfers between devices  24.9 us (44%)
  starting transfers between devices  17 us (30%)
  Pallas kernels  13.1 us (23%)
  other arithmetic  1.29 us (2%)
  between operations  0.79 us (1%)
    ppermute x8, waiting for transfers between devices, to_place(): return lax.ppermute(values, 'lon', turn)  16.5 us
    pallas_call x8, Pallas kernels, call(): pl.pallas_call(kernel, grid_spec=pltpu.PrefetchScalarGridSpec(num_scalar_...  13.1 us
    ppermute x8, starting transfers between devices, to_place(): return lax.ppermute(values, 'lon', turn)  12.9 us
    ppermute x1, waiting for transfers between devices, to_lat(): lax.ppermute(values, 'lat', [(i, (i + step) % lat_count) for i in range(l...  5.69 us
    ppermute x10, waiting for transfers between devices, to_member(): return lax.ppermute(values, 'lon', turn)  2.66 us
    ppermute x10, starting transfers between devices, to_member(): return lax.ppermute(values, 'lon', turn)  2.54 us
    ppermute x1, starting transfers between devices, to_lat(): lax.ppermute(values, 'lat', [(i, (i + step) % lat_count) for i in range(l...  1.56 us
    another operation x1, other arithmetic, body(): jnp.stack([features, cotangent])  1.21 us
  transfers between devices with their start and end apart: 19, of which 8 were waited for; matrix products, arithmetic and copies ran while one was open for 2% of the time, Pallas kernels for 6%

profile of v7, /device:TPU:0, one launch (start us, length us, event | category | flops | bytes accessed | tf_op | source)
XLA Modules:
  0.0 57.0 jit_solution(17942790868424289110)
XLA Ops:
  0.6 0.5 collective-permute-start
  1.1 0.1 collective-permute-start.1
  1.2 0.1 pad_add_fusion.place_ref
  1.3 1.2 %pad_maximum_fusion.fields_ref = bf16[2,10,14,768]{3,2,1,0:T(8,128)(2,1)S(1)} fusion(bf16[1,10,14,768]{3,2,1,0:T(8,128)(2,1)} %bitcast.5, bf16[1,10,14,768]{3,2,1,0:T(8,128)(2,1)} %bitcast.6), kind=kLoop, calls=%fused_computation | loop fusion | flops 215040 | bytes 860160 | tf_op jit(solution)/shard_map/stack | solution.py:597
  2.5 0.8 %shard_map.111 = (bf16[8,80,384]{2,1,0:T(8,128)(2,1)S(1)}, bf16[80,384]{1,0:T(8,128)(2,1)S(1)}) custom-call(s32[3]{0:T(128)S(1)} %pad_add_fusion.place_ref, bf16[2,10,14,768]{3,2,1,0:T(8,128)(2,1)S(1)} %pad_maximum_fusion.fields_ref), custom_call_target="tpu_custom_call" | custom-call | flops 100000000 | bytes 983040 | tf_op jit(solution)/shard_map/pallas_call | solution.py:159
  3.4 0.8 %shard_map.112 = (bf16[2,80,384]{2,1,0:T(8,128)(2,1)S(1)}, bf16[2,80,384]{2,1,0:T(8,128)(2,1)S(1)}, bf16[2,80,384]{2,1,0:T(8,128)(2,1)S(1)}, bf16[2,80,384]{2,1,0:T(8,128)(2,1)S(1)}) custom-call(s32[3]{0:T(128)S(1)} %pad_add_fusion.place_ref, bf16[8,80,384]{2,1,0:T(8,128)(2,1)S(1)} %get-tuple-element.23.own_ref, ...), custom_call_target="tpu_custom_call" | custom-call | bytes 1413120 | tf_op jit(solution)/shard_map/pallas_call | solution.py:159
  4.2 5.1 %collective-permute-start.4 = (bf16[2,80,384]{2,1,0:T(8,128)(2,1)S(1)}, bf16[2,80,384]{2,1,0:T(8,128)(2,1)S(1)}, u32[]{:S(2)}, u32[]{:S(2)}) collective-permute-start(bf16[2,80,384]{2,1,0:T(8,128)(2,1)S(1)} %get-tuple-element.26), channel_id=1, source_target_pairs={{0,24},{2,30},{4,28},{6,26},{8,16},{10,22},{12,20},{14,18},{16,8},... | collective-permute-start | bytes 368648 | tf_op jit(solution)/shard_map/ppermute | solution.py:577
  9.3 0.6 %collective-permute-start.6 = (bf16[2,80,384]{2,1,0:T(8,128)(2,1)S(1)}, bf16[2,80,384]{2,1,0:T(8,128)(2,1)S(1)}, u32[]{:S(2)}, u32[]{:S(2)}) collective-permute-start(bf16[2,80,384]{2,1,0:T(8,128)(2,1)S(1)} %get-tuple-element.28), channel_id=1, source_target_pairs={{0,16},{2,22},{4,20},{6,18},{8,24},{10,30},{12,28},{14,26},{16,0},... | collective-permute-start | bytes 368648 | tf_op jit(solution)/shard_map/ppermute | solution.py:577
  9.9 1.7 %collective-permute-start.2 = (bf16[80,384]{1,0:T(8,128)(2,1)S(1)}, bf16[80,384]{1,0:T(8,128)(2,1)S(1)}, u32[]{:S(2)}, u32[]{:S(2)}) collective-permute-start(bf16[80,384]{1,0:T(8,128)(2,1)S(1)} %get-tuple-element.25), channel_id=1, source_target_pairs={{0,4},{2,6},{4,0},{6,2},{8,12},{10,14},{12,8},{14,10},{16,20},{18,... | collective-permute-start | bytes 184328 | tf_op jit(solution)/shard_map/ppermute | solution.py:577
  11.6 1.8 %collective-permute-done.4.refs_0_ = bf16[2,80,384]{2,1,0:T(8,128)(2,1)S(1)} collective-permute-done((bf16[2,80,384]{2,1,0:T(8,128)(2,1)S(1)}, bf16[2,80,384]{2,1,0:T(8,128)(2,1)S(1)}, u32[]{:S(2)}, u32[]{:S(2)}) %collective-permute-start.4) | collective-permute-done | bytes 122912 | tf_op jit(solution)/shard_map/ppermute | solution.py:577
  13.4 3.6 %collective-permute-done.5.refs_1_ = bf16[2,80,384]{2,1,0:T(8,128)(2,1)S(1)} collective-permute-done((bf16[2,80,384]{2,1,0:T(8,128)(2,1)S(1)}, bf16[2,80,384]{2,1,0:T(8,128)(2,1)S(1)}, u32[]{:S(2)}, u32[]{:S(2)}) %collective-permute-start.5) | collective-permute-done | bytes 122912 | tf_op jit(solution)/shard_map/ppermute | solution.py:577
  16.9 0.9 %collective-permute-start.8 = (bf16[2,80,384]{2,1,0:T(8,128)(2,1)S(1)}, bf16[2,80,384]{2,1,0:T(8,128)(2,1)S(1)}, u32[]{:S(2)}, u32[]{:S(2)}) collective-permute-start(bf16[2,80,384]{2,1,0:T(8,128)(2,1)S(1)} %collective-permute-done.5.refs_1_), channel_id=1, source_target_pairs={{0,2},{2,0},{4,6},{6,4},{8,10},{10,8},{12,14},{14,12},{16,18},{18,... | collective-permute-start | bytes 368648 | tf_op jit(solution)/shard_map/ppermute | solution.py:573
  17.8 3.0 %collective-permute-done.6.refs_2_ = bf16[2,80,384]{2,1,0:T(8,128)(2,1)S(1)} collective-permute-done((bf16[2,80,384]{2,1,0:T(8,128)(2,1)S(1)}, bf16[2,80,384]{2,1,0:T(8,128)(2,1)S(1)}, u32[]{:S(2)}, u32[]{:S(2)}) %collective-permute-start.6) | collective-permute-done | bytes 122912 | tf_op jit(solution)/shard_map/ppermute | solution.py:577
  20.7 0.5 collective-permute-start.3
  21.3 0.9 %collective-permute-done.3.other_side_ref = bf16[80,384]{1,0:T(8,128)(2,1)S(1)} collective-permute-done((bf16[80,384]{1,0:T(8,128)(2,1)S(1)}, bf16[80,384]{1,0:T(8,128)(2,1)S(1)}, u32[]{:S(2)}, u32[]{:S(2)}) %collective-permute-start.3) | collective-permute-done | bytes 61472 | tf_op jit(solution)/shard_map/ppermute | solution.py:573
  22.2 1.0 %shard_map.113.spec_ref = bf16[336,384]{1,0:T(8,128)(2,1)S(1)} custom-call(s32[3]{0:T(128)S(1)} %pad_add_fusion.place_ref, bf16[8,2,128,256]{3,2,1,0:T(8,128)(2,1)S(1)} %copy-done, bf16[2,80,384]{2,1,0:T(8,128)(2,1)S(1)} %get-tuple-element.24.own_ref, bf16[80,384]{1,0:T(8,128)(2,1)S(1)} %collective-permute-done.2.side_ref, ...), custom_call_target="tpu_custom_call" | custom-call | bytes 2289664 | tf_op jit(solution)/shard_map/pallas_call | solution.py:159
  23.3 1.6 %collective-permute-start.10 = (bf16[336,384]{1,0:T(8,128)(2,1)S(1)}, bf16[336,384]{1,0:T(8,128)(2,1)S(1)}, u32[]{:S(2)}, u32[]{:S(2)}) collective-permute-start(bf16[336,384]{1,0:T(8,128)(2,1)S(1)} %shard_map.113.spec_ref), channel_id=1, source_target_pairs={{0,1},{1,0},{2,3},{3,2},{4,5},{5,4},{6,7},{7,6},{8,9},{9,8},{10,11... | collective-permute-start | bytes 774152 | tf_op jit(solution)/shard_map/ppermute | solution.py:580
  24.8 1.3 %shard_map.114 = (f32[160,1536]{1,0:T(8,128)S(1)}, bf16[4,192,192]{2,1,0:T(8,128)(2,1)S(1)}, f32[8,192]{1,0:T(8,128)S(1)}) custom-call(s32[3]{0:T(128)S(1)} %pad_add_fusion.place_ref, bf16[640,80]{1,0:T(8,128)(2,1)S(1)} %copy-done.5, bf16[336,384]{1,0:T(8,128)(2,1)S(1)} %shard_map.113.spec_ref, f32[2,8,96,96]{3,2,1,0:T(8,128)S(1)} %copy-done.3, ...), custom_call_target="tpu_custom_call" | custom-call | flops 117964800 | bytes 2830336 | tf_op jit(solution)/shard_map/pallas_call | solution.py:159
  26.1 5.7 %collective-permute-done.10.refs_0_ = bf16[336,384]{1,0:T(8,128)(2,1)S(1)} collective-permute-done((bf16[336,384]{1,0:T(8,128)(2,1)S(1)}, bf16[336,384]{1,0:T(8,128)(2,1)S(1)}, u32[]{:S(2)}, u32[]{:S(2)}) %collective-permute-start.10) | collective-permute-done | bytes 258080 | tf_op jit(solution)/shard_map/ppermute | solution.py:580
  31.8 3.9 %shard_map.115.own_ref = f32[264,384]{1,0:T(8,128)S(1)} custom-call(s32[3]{0:T(128)S(1)} %pad_add_fusion.place_ref, bf16[640,80]{1,0:T(8,128)(2,1)S(1)} %copy-done.5, bf16[336,384]{1,0:T(8,128)(2,1)S(1)} %collective-permute-done.10.refs_0_, f32[160,1536]{1,0:T(8,128)S(1)} %get-tuple-element.29.refs_1_, bf16[4,192,192]{2,1,0:T(8,128)(2,1)S(1)} %get-tuple-element.30.refs_2_, ...), custom_call_target="tpu_custom_call" | custom-call | bytes 2050048 | tf_op jit(solution)/shard_map/pallas_call | solution.py:159
  35.7 0.1 collective-permute-start.11
  35.8 1.7 %collective-permute-done.11.other_ref = f32[264,384]{1,0:T(8,128)S(1)} collective-permute-done((f32[264,384]{1,0:T(8,128)S(1)}, f32[264,384]{1,0:T(8,128)S(1)}, u32[]{:S(2)}, u32[]{:S(2)}) %collective-permute-start.11) | collective-permute-done | bytes 405536 | tf_op jit(solution)/shard_map/ppermute | solution.py:573
  37.5 1.3 %shard_map.116 = (bf16[136,384]{1,0:T(8,128)(2,1)S(1)}, bf16[136,384]{1,0:T(8,128)(2,1)S(1)}, bf16[176,384]{1,0:T(8,128)(2,1)S(1)}, bf16[176,384]{1,0:T(8,128)(2,1)S(1)}, bf16[176,384]{1,0:T(8,128)(2,1)S(1)}) custom-call(s32[3]{0:T(128)S(1)} %pad_add_fusion.place_ref, bf16[8,2,128,256]{3,2,1,0:T(8,128)(2,1)S(1)} %copy-done.1, ...), custom_call_target="tpu_custom_call" | custom-call | bytes 2473984 | tf_op jit(solution)/shard_map/pallas_call | solution.py:159
  38.8 2.6 %collective-permute-start.13 = (bf16[176,384]{1,0:T(8,128)(2,1)S(1)}, bf16[176,384]{1,0:T(8,128)(2,1)S(1)}, u32[]{:S(2)}, u32[]{:S(2)}) collective-permute-start(bf16[176,384]{1,0:T(8,128)(2,1)S(1)} %get-tuple-element.34), channel_id=1, source_target_pairs={{0,24},{2,30},{4,28},{6,26},{8,16},{10,22},{12,20},{14,18},{16,8},... | collective-permute-start | bytes 405512 | tf_op jit(solution)/shard_map/ppermute | solution.py:577
  41.4 1.9 %collective-permute-start.15 = (bf16[176,384]{1,0:T(8,128)(2,1)S(1)}, bf16[176,384]{1,0:T(8,128)(2,1)S(1)}, u32[]{:S(2)}, u32[]{:S(2)}) collective-permute-start(bf16[176,384]{1,0:T(8,128)(2,1)S(1)} %get-tuple-element.38), channel_id=1, source_target_pairs={{0,16},{2,22},{4,20},{6,18},{8,24},{10,30},{12,28},{14,26},{16,0},... | collective-permute-start | bytes 405512 | tf_op jit(solution)/shard_map/ppermute | solution.py:577
  43.2 1.0 %collective-permute-start.12 = (bf16[136,384]{1,0:T(8,128)(2,1)S(1)}, bf16[136,384]{1,0:T(8,128)(2,1)S(1)}, u32[]{:S(2)}, u32[]{:S(2)}) collective-permute-start(bf16[136,384]{1,0:T(8,128)(2,1)S(1)} %get-tuple-element.33), channel_id=1, source_target_pairs={{0,4},{2,6},{4,0},{6,2},{8,12},{10,14},{12,8},{14,10},{16,20},{18,... | collective-permute-start | bytes 313352 | tf_op jit(solution)/shard_map/ppermute | solution.py:577
  44.3 6.4 %collective-permute-done.12.refs_1_ = bf16[136,384]{1,0:T(8,128)(2,1)S(1)} collective-permute-done((bf16[136,384]{1,0:T(8,128)(2,1)S(1)}, bf16[136,384]{1,0:T(8,128)(2,1)S(1)}, u32[]{:S(2)}, u32[]{:S(2)}) %collective-permute-start.12) | collective-permute-done | bytes 104480 | tf_op jit(solution)/shard_map/ppermute | solution.py:577
  50.7 1.9 %collective-permute-done.14.refs_3_ = bf16[176,384]{1,0:T(8,128)(2,1)S(1)} collective-permute-done((bf16[176,384]{1,0:T(8,128)(2,1)S(1)}, bf16[176,384]{1,0:T(8,128)(2,1)S(1)}, u32[]{:S(2)}, u32[]{:S(2)}) %collective-permute-start.14) | collective-permute-done | bytes 135200 | tf_op jit(solution)/shard_map/ppermute | solution.py:577
  52.5 0.4 collective-permute-start.17
  52.9 0.2 collective-permute-start.18
  53.0 1.2 %shard_map.117 = (f32[5,40,384]{2,1,0:T(8,128)S(1)}, f32[5,96,384]{2,1,0:T(8,128)S(1)}, f32[5,192]{1,0:T(8,128)S(1)}) custom-call(s32[3]{0:T(128)S(1)} %pad_add_fusion.place_ref, bf16[136,384]{1,0:T(8,128)(2,1)S(1)} %get-tuple-element.32.refs_0_, bf16[136,384]{1,0:T(8,128)(2,1)S(1)} %collective-permute-done.12.refs_1_, ...), custom_call_target="tpu_custom_call" | custom-call | bytes 1662720 | tf_op jit(solution)/shard_map/pallas_call | solution.py:159
  54.3 2.7 %shard_map.118 = (bf16[10,14,768]{2,1,0:T(8,128)(2,1)}, f32[2,8,96,96]{3,2,1,0:T(8,128)}, f32[2,8,96]{2,1,0:T(8,128)}, f32[2,8,96,96]{3,2,1,0:T(8,128)}) custom-call(s32[3]{0:T(128)S(1)} %pad_add_fusion.place_ref, f32[5,40,384]{2,1,0:T(8,128)S(1)} %get-tuple-element.39.columns_ref, f32[5,96,384]{2,1,0:T(8,128)S(1)} %get-tuple-element.40.weights_ref, ...), custom_call_target="tpu_custom_call" | custom-call | bytes 3069696 | tf_op jit(solution)/shard_map/pallas_call | solution.py:159
  (30 shorter events, 0.1 us)
Async XLA Ops:
  0.6 2.7 %collective-permute-start = (bf16[10,14,768]{2,1,0:T(8,128)(2,1)}, bf16[10,14,768]{2,1,0:T(8,128)(2,1)S(1)}, u32[]{:S(2)}, u32[]{:S(2)}) collective-permute-start(bf16[10,14,768]{2,1,0:T(8,128)(2,1)} %param.8), channel_id=1, source_target_pairs={{0,2},{2,0},{4,6},{6,4},{8,10},{10,8},{12,14},{14,12},{16,18},{18,... | collective-permute-start | bytes 645128 | tf_op jit(solution)/shard_map/ppermute | solution.py:573
  1.1 2.2 %collective-permute-start.1 = (bf16[10,14,768]{2,1,0:T(8,128)(2,1)}, bf16[10,14,768]{2,1,0:T(8,128)(2,1)S(1)}, u32[]{:S(2)}, u32[]{:S(2)}) collective-permute-start(bf16[10,14,768]{2,1,0:T(8,128)(2,1)} %cot_ref.1), channel_id=1, source_target_pairs={{0,2},{2,0},{4,6},{6,4},{8,10},{10,8},{12,14},{14,12},{16,18},{18,... | collective-permute-start | bytes 645128 | tf_op jit(solution)/shard_map/ppermute | solution.py:573
  1.3 20.9 %copy-start = (bf16[8,2,128,256]{3,2,1,0:T(8,128)(2,1)S(1)}, bf16[8,2,128,256]{3,2,1,0:T(8,128)(2,1)}, u32[]{:S(2)}) copy-start(bf16[8,2,128,256]{3,2,1,0:T(8,128)(2,1)} %constant.38.clone.table_ref) | copy-start | bytes 3145732
  4.2 9.2 %collective-permute-start.4 = (bf16[2,80,384]{2,1,0:T(8,128)(2,1)S(1)}, bf16[2,80,384]{2,1,0:T(8,128)(2,1)S(1)}, u32[]{:S(2)}, u32[]{:S(2)}) collective-permute-start(bf16[2,80,384]{2,1,0:T(8,128)(2,1)S(1)} %get-tuple-element.26), channel_id=1, source_target_pairs={{0,24},{2,30},{4,28},{6,26},{8,16},{10,22},{12,20},{14,18},{16,8},... | collective-permute-start | bytes 368648 | tf_op jit(solution)/shard_map/ppermute | solution.py:577
  9.3 7.6 %collective-permute-start.5 = (bf16[2,80,384]{2,1,0:T(8,128)(2,1)S(1)}, bf16[2,80,384]{2,1,0:T(8,128)(2,1)S(1)}, u32[]{:S(2)}, u32[]{:S(2)}) collective-permute-start(bf16[2,80,384]{2,1,0:T(8,128)(2,1)S(1)} %get-tuple-element.27), channel_id=1, source_target_pairs={{0,8},{2,14},{4,12},{6,10},{8,0},{10,6},{12,4},{14,2},{16,24},{18,... | collective-permute-start | bytes 368648 | tf_op jit(solution)/shard_map/ppermute | solution.py:577
  9.3 11.4 %collective-permute-start.6 = (bf16[2,80,384]{2,1,0:T(8,128)(2,1)S(1)}, bf16[2,80,384]{2,1,0:T(8,128)(2,1)S(1)}, u32[]{:S(2)}, u32[]{:S(2)}) collective-permute-start(bf16[2,80,384]{2,1,0:T(8,128)(2,1)S(1)} %get-tuple-element.28), channel_id=1, source_target_pairs={{0,16},{2,22},{4,20},{6,18},{8,24},{10,30},{12,28},{14,26},{16,0},... | collective-permute-start | bytes 368648 | tf_op jit(solution)/shard_map/ppermute | solution.py:577
  9.9 10.8 %collective-permute-start.2 = (bf16[80,384]{1,0:T(8,128)(2,1)S(1)}, bf16[80,384]{1,0:T(8,128)(2,1)S(1)}, u32[]{:S(2)}, u32[]{:S(2)}) collective-permute-start(bf16[80,384]{1,0:T(8,128)(2,1)S(1)} %get-tuple-element.25), channel_id=1, source_target_pairs={{0,4},{2,6},{4,0},{6,2},{8,12},{10,14},{12,8},{14,10},{16,20},{18,... | collective-permute-start | bytes 184328 | tf_op jit(solution)/shard_map/ppermute | solution.py:577
  13.4 8.8 %collective-permute-start.7 = (bf16[2,80,384]{2,1,0:T(8,128)(2,1)S(1)}, bf16[2,80,384]{2,1,0:T(8,128)(2,1)S(1)}, u32[]{:S(2)}, u32[]{:S(2)}) collective-permute-start(bf16[2,80,384]{2,1,0:T(8,128)(2,1)S(1)} %collective-permute-done.4.refs_0_), channel_id=1, source_target_pairs={{0,2},{2,0},{4,6},{6,4},{8,10},{10,8},{12,14},{14,12},{16,18},{18,... | collective-permute-start | bytes 368648 | tf_op jit(solution)/shard_map/ppermute | solution.py:573
  16.9 5.2 %collective-permute-start.8 = (bf16[2,80,384]{2,1,0:T(8,128)(2,1)S(1)}, bf16[2,80,384]{2,1,0:T(8,128)(2,1)S(1)}, u32[]{:S(2)}, u32[]{:S(2)}) collective-permute-start(bf16[2,80,384]{2,1,0:T(8,128)(2,1)S(1)} %collective-permute-done.5.refs_1_), channel_id=1, source_target_pairs={{0,2},{2,0},{4,6},{6,4},{8,10},{10,8},{12,14},{14,12},{16,18},{18,... | collective-permute-start | bytes 368648 | tf_op jit(solution)/shard_map/ppermute | solution.py:573
  20.7 1.4 %collective-permute-start.9 = (bf16[2,80,384]{2,1,0:T(8,128)(2,1)S(1)}, bf16[2,80,384]{2,1,0:T(8,128)(2,1)S(1)}, u32[]{:S(2)}, u32[]{:S(2)}) collective-permute-start(bf16[2,80,384]{2,1,0:T(8,128)(2,1)S(1)} %collective-permute-done.6.refs_2_), channel_id=1, source_target_pairs={{0,2},{2,0},{4,6},{6,4},{8,10},{10,8},{12,14},{14,12},{16,18},{18,... | collective-permute-start | bytes 368648 | tf_op jit(solution)/shard_map/ppermute | solution.py:573
  20.7 1.4 %collective-permute-start.3 = (bf16[80,384]{1,0:T(8,128)(2,1)S(1)}, bf16[80,384]{1,0:T(8,128)(2,1)S(1)}, u32[]{:S(2)}, u32[]{:S(2)}) collective-permute-start(bf16[80,384]{1,0:T(8,128)(2,1)S(1)} %collective-permute-done.2.side_ref), channel_id=1, source_target_pairs={{0,2},{2,0},{4,6},{6,4},{8,10},{10,8},{12,14},{14,12},{16,18},{18,... | collective-permute-start | bytes 184328 | tf_op jit(solution)/shard_map/ppermute | solution.py:573
  22.2 2.6 %copy-start.3 = (f32[2,8,96,96]{3,2,1,0:T(8,128)S(1)}, f32[2,8,96,96]{3,2,1,0:T(8,128)}, u32[]{:S(2)}) copy-start(f32[2,8,96,96]{3,2,1,0:T(8,128)} %win_ref.1) | copy-start | bytes 1769476
  22.2 2.6 %copy-start.4 = (f32[2,8,96,96]{3,2,1,0:T(8,128)S(1)}, f32[2,8,96,96]{3,2,1,0:T(8,128)}, u32[]{:S(2)}) copy-start(f32[2,8,96,96]{3,2,1,0:T(8,128)} %wout_ref.1) | copy-start | bytes 1769476
  22.2 2.6 %copy-start.5 = (bf16[640,80]{1,0:T(8,128)(2,1)S(1)}, bf16[640,80]{1,0:T(8,128)(2,1)}, u32[]{:S(2)}) copy-start(bf16[640,80]{1,0:T(8,128)(2,1)} %constant.39.clone.table_ref) | copy-start | bytes 307204
  22.2 2.6 %copy-start.6 = (f32[2,8,96]{2,1,0:T(8,128)S(1)}, f32[2,8,96]{2,1,0:T(8,128)}, u32[]{:S(2)}) copy-start(f32[2,8,96]{2,1,0:T(8,128)} %bin_ref.1) | copy-start | bytes 18436
  23.3 8.5 %collective-permute-start.10 = (bf16[336,384]{1,0:T(8,128)(2,1)S(1)}, bf16[336,384]{1,0:T(8,128)(2,1)S(1)}, u32[]{:S(2)}, u32[]{:S(2)}) collective-permute-start(bf16[336,384]{1,0:T(8,128)(2,1)S(1)} %shard_map.113.spec_ref), channel_id=1, source_target_pairs={{0,1},{1,0},{2,3},{3,2},{4,5},{5,4},{6,7},{7,6},{8,9},{9,8},{10,11... | collective-permute-start | bytes 774152 | tf_op jit(solution)/shard_map/ppermute | solution.py:580
  31.8 5.7 %copy-start.1 = (bf16[8,2,128,256]{3,2,1,0:T(8,128)(2,1)S(1)}, bf16[8,2,128,256]{3,2,1,0:T(8,128)(2,1)}, u32[]{:S(2)}) copy-start(bf16[8,2,128,256]{3,2,1,0:T(8,128)(2,1)} %constant.40.clone.table_ref) | copy-start | bytes 3145732
  35.7 1.8 %collective-permute-start.11 = (f32[264,384]{1,0:T(8,128)S(1)}, f32[264,384]{1,0:T(8,128)S(1)}, u32[]{:S(2)}, u32[]{:S(2)}) collective-permute-start(f32[264,384]{1,0:T(8,128)S(1)} %shard_map.115.own_ref), channel_id=1, source_target_pairs={{0,2},{2,0},{4,6},{6,4},{8,10},{10,8},{12,14},{14,12},{16,18},{18,... | collective-permute-start | bytes 1216520 | tf_op jit(solution)/shard_map/ppermute | solution.py:573
  38.8 11.9 %collective-permute-start.13 = (bf16[176,384]{1,0:T(8,128)(2,1)S(1)}, bf16[176,384]{1,0:T(8,128)(2,1)S(1)}, u32[]{:S(2)}, u32[]{:S(2)}) collective-permute-start(bf16[176,384]{1,0:T(8,128)(2,1)S(1)} %get-tuple-element.34), channel_id=1, source_target_pairs={{0,24},{2,30},{4,28},{6,26},{8,16},{10,22},{12,20},{14,18},{16,8},... | collective-permute-start | bytes 405512 | tf_op jit(solution)/shard_map/ppermute | solution.py:577
  41.4 11.1 %collective-permute-start.14 = (bf16[176,384]{1,0:T(8,128)(2,1)S(1)}, bf16[176,384]{1,0:T(8,128)(2,1)S(1)}, u32[]{:S(2)}, u32[]{:S(2)}) collective-permute-start(bf16[176,384]{1,0:T(8,128)(2,1)S(1)} %get-tuple-element.37), channel_id=1, source_target_pairs={{0,8},{2,14},{4,12},{6,10},{8,0},{10,6},{12,4},{14,2},{16,24},{18,... | collective-permute-start | bytes 405512 | tf_op jit(solution)/shard_map/ppermute | solution.py:577
  41.4 11.5 %collective-permute-start.15 = (bf16[176,384]{1,0:T(8,128)(2,1)S(1)}, bf16[176,384]{1,0:T(8,128)(2,1)S(1)}, u32[]{:S(2)}, u32[]{:S(2)}) collective-permute-start(bf16[176,384]{1,0:T(8,128)(2,1)S(1)} %get-tuple-element.38), channel_id=1, source_target_pairs={{0,16},{2,22},{4,20},{6,18},{8,24},{10,30},{12,28},{14,26},{16,0},... | collective-permute-start | bytes 405512 | tf_op jit(solution)/shard_map/ppermute | solution.py:577
  43.2 7.4 %collective-permute-start.12 = (bf16[136,384]{1,0:T(8,128)(2,1)S(1)}, bf16[136,384]{1,0:T(8,128)(2,1)S(1)}, u32[]{:S(2)}, u32[]{:S(2)}) collective-permute-start(bf16[136,384]{1,0:T(8,128)(2,1)S(1)} %get-tuple-element.33), channel_id=1, source_target_pairs={{0,4},{2,6},{4,0},{6,2},{8,12},{10,14},{12,8},{14,10},{16,20},{18,... | collective-permute-start | bytes 313352 | tf_op jit(solution)/shard_map/ppermute | solution.py:577
  50.6 3.6 %collective-permute-start.16 = (bf16[176,384]{1,0:T(8,128)(2,1)S(1)}, bf16[176,384]{1,0:T(8,128)(2,1)S(1)}, u32[]{:S(2)}, u32[]{:S(2)}) collective-permute-start(bf16[176,384]{1,0:T(8,128)(2,1)S(1)} %collective-permute-done.13.refs_2_), channel_id=1, source_target_pairs={{0,2},{2,0},{4,6},{6,4},{8,10},{10,8},{12,14},{14,12},{16,18},{18,... | collective-permute-start | bytes 405512 | tf_op jit(solution)/shard_map/ppermute | solution.py:573
  52.5 1.7 %collective-permute-start.17 = (bf16[176,384]{1,0:T(8,128)(2,1)S(1)}, bf16[176,384]{1,0:T(8,128)(2,1)S(1)}, u32[]{:S(2)}, u32[]{:S(2)}) collective-permute-start(bf16[176,384]{1,0:T(8,128)(2,1)S(1)} %collective-permute-done.14.refs_3_), channel_id=1, source_target_pairs={{0,2},{2,0},{4,6},{6,4},{8,10},{10,8},{12,14},{14,12},{16,18},{18,... | collective-permute-start | bytes 405512 | tf_op jit(solution)/shard_map/ppermute | solution.py:573
  52.9 1.4 %collective-permute-start.18 = (bf16[176,384]{1,0:T(8,128)(2,1)S(1)}, bf16[176,384]{1,0:T(8,128)(2,1)S(1)}, u32[]{:S(2)}, u32[]{:S(2)}) collective-permute-start(bf16[176,384]{1,0:T(8,128)(2,1)S(1)} %collective-permute-done.15.refs_4_), channel_id=1, source_target_pairs={{0,2},{2,0},{4,6},{6,4},{8,10},{10,8},{12,14},{14,12},{16,18},{18,... | collective-permute-start | bytes 405512 | tf_op jit(solution)/shard_map/ppermute | solution.py:573
  53.0 1.2 %copy-start.2 = (bf16[10,14,768]{2,1,0:T(8,128)(2,1)S(1)}, bf16[10,14,768]{2,1,0:T(8,128)(2,1)}, u32[]{:S(2)}) copy-start(bf16[10,14,768]{2,1,0:T(8,128)(2,1)} %cot_ref.1) | copy-start | bytes 645124

commit v8 on v7

--- a/solution.py
+++ b/solution.py
@@ -440,11 +440,15 @@
     count = len(refs) - 3
     columns_ref, weights_ref, bias_ref = refs[count:]
     for n in range(count):
-        columns_ref[n], weights_ref[n], bias_ref[n : n + 1, :] = arrived(refs[n], member, data_rows)
-
-
-def last_kernel(data_rows, place_ref, columns_ref, weights_ref, bias_ref, cot_ref, *refs):
+        columns_ref[n], weights, bias_ref[n : n + 1, :] = arrived(refs[n], member, data_rows)
+        width = weights_ref.shape[3]
+        for i in range(4):
+            weights_ref[n, i] = weights[:, i * width : (i + 1) * width]
+
+
+def last_kernel(data_rows, place_ref, *refs):
     place, member = place_ref[0], place_ref[1]
+    early, (cot_ref, *refs) = (refs[:3], refs[3:6]), refs[6:]
     lates = refs[: len(BASES)]
     out_ref, win_ref, bin_ref, wout_ref, held_ref = refs[len(BASES) :]
     rows, cols, _ = cot_ref.shape
@@ -456,15 +460,18 @@
         held_ref[source] = columns
         for i in range(4):
             target = (win_ref, wout_ref)[i // 2]
-            target[i % 2, source] = weights[:, i * width : (i + 1) * width]
+            target[i % 2, source] = weights[i]
         for k in range(2):
             bin_ref[k, pl.ds(source, 1), :] = bias[:, k * width : (k + 1) * width]
 
-    for n, base in enumerate((0, 1) + BASES):
-        source = place ^ (base + member) if n >= 2 else place ^ base
-        settle(source, columns_ref[n], weights_ref[n], bias_ref[n : n + 1, :])
+    sources = ([place, place ^ 1], [place ^ (base + member) for base in BASES])
+    for group, (columns_ref, weights_ref, bias_ref) in zip(sources, early):
+        for n, source in enumerate(group):
+            settle(source, columns_ref[n], weights_ref.at[n], bias_ref[n : n + 1, :])
     for ref, base in zip(lates, BASES):
-        settle(place ^ (base + 1 - member), *arrived(ref, member, data_rows))
+        columns, weights, bias = arrived(ref, member, data_rows)
+        parts = [weights[:, i * width : (i + 1) * width] for i in range(4)]
+        settle(place ^ (base + 1 - member), columns, parts, bias)
     for q in range(pairs):
         for h in range(2):
             parts = []
@@ -662,18 +669,23 @@
             scratch=(pltpu.VMEM((count, data_rows, wide), f32),),
         )
         sent = serve(slots)
-        side, sent[0] = lax.optimization_barrier((to_place(side, 1, 1), sent[0]))
-        firsts, late = [own, side, *sent], [to_member(x, 1) for x in sent]
-        held = call(
-            functools.partial(first_kernel, data_rows),
-            scalars,
-            firsts,
-            (
-                shape((len(firsts), data_rows, wide), f32),
-                shape((len(firsts), share, wide), f32),
-                shape((len(firsts), 2 * width), f32),
-            ),
-        )
+
+        def first(group):
+            n = len(group)
+            return call(
+                functools.partial(first_kernel, data_rows),
+                scalars,
+                group,
+                (
+                    shape((n, data_rows, wide), f32),
+                    shape((n, 4, share, width), f32),
+                    shape((n, 2 * width), f32),
+                ),
+            )
+
+        held, sent[0] = lax.optimization_barrier((first([own, to_place(side, 1, 1)]), sent[0]))
+        late = [to_member(x, 1) for x in sent]
+        held = [*held, *first(sent)]
         return call(
             functools.partial(last_kernel, data_rows),
             scalars,

time: 57.2 us -> 57 us (level)
  waiting for transfers between devices: 24.9 us -> 24 us
    ppermute x8, waiting for transfers between devices: 16.5 us -> 15.7 us  [to_place(): return lax.ppermute(values, 'lon', turn)]
    pallas_call x8 -> x9, Pallas kernels: 13.1 us -> 13.4 us  [call(): pl.pallas_call(kernel, grid_spec=pltpu.PrefetchScalarGridSpec(num_scalar_...]
  transfers between devices with their start and end apart: 19 -> 19, of which waited for: 8 -> 8; matrix products, arithmetic and copies ran while one was open for 2% -> 2% of each run, Pallas kernels for 6% -> 7%
where the time goes in v8:
time: 57 us; the launch traced here: 56.9 us
  waiting for transfers between devices  24 us (42%)
  starting transfers between devices  17.3 us (30%)
  Pallas kernels  13.4 us (24%)
  other arithmetic  1.29 us (2%)
  between operations  0.81 us (1%)
    ppermute x8, waiting for transfers between devices, to_place(): return lax.ppermute(values, 'lon', turn)  15.7 us
    pallas_call x9, Pallas kernels, call(): pl.pallas_call(kernel, grid_spec=pltpu.PrefetchScalarGridSpec(num_scalar_...  13.4 us
    ppermute x8, starting transfers between devices, to_place(): return lax.ppermute(values, 'lon', turn)  12.9 us
    ppermute x1, waiting for transfers between devices, to_lat(): lax.ppermute(values, 'lat', [(i, (i + step) % lat_count) for i in range(l...  5.69 us
    ppermute x10, starting transfers between devices, to_member(): return lax.ppermute(values, 'lon', turn)  2.89 us
    ppermute x10, waiting for transfers between devices, to_member(): return lax.ppermute(values, 'lon', turn)  2.66 us
    ppermute x1, starting transfers between devices, to_lat(): lax.ppermute(values, 'lat', [(i, (i + step) % lat_count) for i in range(l...  1.56 us
    another operation x1, other arithmetic, body(): jnp.stack([features, cotangent])  1.21 us
  transfers between devices with their start and end apart: 19, of which 8 were waited for; matrix products, arithmetic and copies ran while one was open for 2% of the time, Pallas kernels for 7%

profile of v8, /device:TPU:0, one launch (start us, length us, event | category | flops | bytes accessed | tf_op | source)
XLA Modules:
  0.0 56.9 jit_solution(5654494423326856056)
XLA Ops:
  0.6 0.5 collective-permute-start
  1.1 0.1 collective-permute-start.1
  1.3 1.2 %pad_maximum_fusion.fields_ref = bf16[2,10,14,768]{3,2,1,0:T(8,128)(2,1)S(1)} fusion(bf16[1,10,14,768]{3,2,1,0:T(8,128)(2,1)} %bitcast.5, bf16[1,10,14,768]{3,2,1,0:T(8,128)(2,1)} %bitcast.6), kind=kLoop, calls=%fused_computation | loop fusion | flops 215040 | bytes 860160 | tf_op jit(solution)/shard_map/stack | solution.py:604
  2.5 0.8 %shard_map.111 = (bf16[8,80,384]{2,1,0:T(8,128)(2,1)S(1)}, bf16[80,384]{1,0:T(8,128)(2,1)S(1)}) custom-call(s32[3]{0:T(128)S(1)} %pad_add_fusion.place_ref, bf16[2,10,14,768]{3,2,1,0:T(8,128)(2,1)S(1)} %pad_maximum_fusion.fields_ref), custom_call_target="tpu_custom_call" | custom-call | flops 100000000 | bytes 983040 | tf_op jit(solution)/shard_map/pallas_call | solution.py:159
  3.4 0.8 %shard_map.112 = (bf16[2,80,384]{2,1,0:T(8,128)(2,1)S(1)}, bf16[2,80,384]{2,1,0:T(8,128)(2,1)S(1)}, bf16[2,80,384]{2,1,0:T(8,128)(2,1)S(1)}, bf16[2,80,384]{2,1,0:T(8,128)(2,1)S(1)}) custom-call(s32[3]{0:T(128)S(1)} %pad_add_fusion.place_ref, bf16[8,80,384]{2,1,0:T(8,128)(2,1)S(1)} %get-tuple-element.28.own_ref, ...), custom_call_target="tpu_custom_call" | custom-call | bytes 1413120 | tf_op jit(solution)/shard_map/pallas_call | solution.py:159
  4.2 5.1 %collective-permute-start.4 = (bf16[2,80,384]{2,1,0:T(8,128)(2,1)S(1)}, bf16[2,80,384]{2,1,0:T(8,128)(2,1)S(1)}, u32[]{:S(2)}, u32[]{:S(2)}) collective-permute-start(bf16[2,80,384]{2,1,0:T(8,128)(2,1)S(1)} %get-tuple-element.31), channel_id=1, source_target_pairs={{0,24},{2,30},{4,28},{6,26},{8,16},{10,22},{12,20},{14,18},{16,8},... | collective-permute-start | bytes 368648 | tf_op jit(solution)/shard_map/ppermute | solution.py:584
  9.3 0.6 %collective-permute-start.6 = (bf16[2,80,384]{2,1,0:T(8,128)(2,1)S(1)}, bf16[2,80,384]{2,1,0:T(8,128)(2,1)S(1)}, u32[]{:S(2)}, u32[]{:S(2)}) collective-permute-start(bf16[2,80,384]{2,1,0:T(8,128)(2,1)S(1)} %get-tuple-element.33), channel_id=1, source_target_pairs={{0,16},{2,22},{4,20},{6,18},{8,24},{10,30},{12,28},{14,26},{16,0},... | collective-permute-start | bytes 368648 | tf_op jit(solution)/shard_map/ppermute | solution.py:584
  9.9 1.7 %collective-permute-start.2 = (bf16[80,384]{1,0:T(8,128)(2,1)S(1)}, bf16[80,384]{1,0:T(8,128)(2,1)S(1)}, u32[]{:S(2)}, u32[]{:S(2)}) collective-permute-start(bf16[80,384]{1,0:T(8,128)(2,1)S(1)} %get-tuple-element.30), channel_id=1, source_target_pairs={{0,4},{2,6},{4,0},{6,2},{8,12},{10,14},{12,8},{14,10},{16,20},{18,... | collective-permute-start | bytes 184328 | tf_op jit(solution)/shard_map/ppermute | solution.py:584
  11.6 1.8 %collective-permute-done.4.refs_0_ = bf16[2,80,384]{2,1,0:T(8,128)(2,1)S(1)} collective-permute-done((bf16[2,80,384]{2,1,0:T(8,128)(2,1)S(1)}, bf16[2,80,384]{2,1,0:T(8,128)(2,1)S(1)}, u32[]{:S(2)}, u32[]{:S(2)}) %collective-permute-start.4) | collective-permute-done | bytes 122912 | tf_op jit(solution)/shard_map/ppermute | solution.py:584
  13.4 3.6 %collective-permute-done.5.refs_1_ = bf16[2,80,384]{2,1,0:T(8,128)(2,1)S(1)} collective-permute-done((bf16[2,80,384]{2,1,0:T(8,128)(2,1)S(1)}, bf16[2,80,384]{2,1,0:T(8,128)(2,1)S(1)}, u32[]{:S(2)}, u32[]{:S(2)}) %collective-permute-start.5) | collective-permute-done | bytes 122912 | tf_op jit(solution)/shard_map/ppermute | solution.py:584
  16.9 0.9 %collective-permute-start.8 = (bf16[2,80,384]{2,1,0:T(8,128)(2,1)S(1)}, bf16[2,80,384]{2,1,0:T(8,128)(2,1)S(1)}, u32[]{:S(2)}, u32[]{:S(2)}) collective-permute-start(bf16[2,80,384]{2,1,0:T(8,128)(2,1)S(1)} %collective-permute-done.5.refs_1_), channel_id=1, source_target_pairs={{0,2},{2,0},{4,6},{6,4},{8,10},{10,8},{12,14},{14,12},{16,18},{18,... | collective-permute-start | bytes 368648 | tf_op jit(solution)/shard_map/ppermute | solution.py:580
  17.8 3.0 %collective-permute-done.6.refs_2_ = bf16[2,80,384]{2,1,0:T(8,128)(2,1)S(1)} collective-permute-done((bf16[2,80,384]{2,1,0:T(8,128)(2,1)S(1)}, bf16[2,80,384]{2,1,0:T(8,128)(2,1)S(1)}, u32[]{:S(2)}, u32[]{:S(2)}) %collective-permute-start.6) | collective-permute-done | bytes 122912 | tf_op jit(solution)/shard_map/ppermute | solution.py:584
  20.7 0.5 collective-permute-start.3
  21.3 0.9 %collective-permute-done.3.other_side_ref = bf16[80,384]{1,0:T(8,128)(2,1)S(1)} collective-permute-done((bf16[80,384]{1,0:T(8,128)(2,1)S(1)}, bf16[80,384]{1,0:T(8,128)(2,1)S(1)}, u32[]{:S(2)}, u32[]{:S(2)}) %collective-permute-start.3) | collective-permute-done | bytes 61472 | tf_op jit(solution)/shard_map/ppermute | solution.py:580
  22.2 1.0 %shard_map.113.spec_ref = bf16[336,384]{1,0:T(8,128)(2,1)S(1)} custom-call(s32[3]{0:T(128)S(1)} %pad_add_fusion.place_ref, bf16[8,2,128,256]{3,2,1,0:T(8,128)(2,1)S(1)} %copy-done, bf16[2,80,384]{2,1,0:T(8,128)(2,1)S(1)} %get-tuple-element.29.own_ref, bf16[80,384]{1,0:T(8,128)(2,1)S(1)} %collective-permute-done.2.side_ref, ...), custom_call_target="tpu_custom_call" | custom-call | bytes 2289664 | tf_op jit(solution)/shard_map/pallas_call | solution.py:159
  23.3 1.6 %collective-permute-start.10 = (bf16[336,384]{1,0:T(8,128)(2,1)S(1)}, bf16[336,384]{1,0:T(8,128)(2,1)S(1)}, u32[]{:S(2)}, u32[]{:S(2)}) collective-permute-start(bf16[336,384]{1,0:T(8,128)(2,1)S(1)} %shard_map.113.spec_ref), channel_id=1, source_target_pairs={{0,1},{1,0},{2,3},{3,2},{4,5},{5,4},{6,7},{7,6},{8,9},{9,8},{10,11... | collective-permute-start | bytes 774152 | tf_op jit(solution)/shard_map/ppermute | solution.py:587
  24.8 1.3 %shard_map.114 = (f32[160,1536]{1,0:T(8,128)S(1)}, bf16[4,192,192]{2,1,0:T(8,128)(2,1)S(1)}, f32[8,192]{1,0:T(8,128)S(1)}) custom-call(s32[3]{0:T(128)S(1)} %pad_add_fusion.place_ref, bf16[640,80]{1,0:T(8,128)(2,1)S(1)} %copy-done.5, bf16[336,384]{1,0:T(8,128)(2,1)S(1)} %shard_map.113.spec_ref, f32[2,8,96,96]{3,2,1,0:T(8,128)S(1)} %copy-done.3, ...), custom_call_target="tpu_custom_call" | custom-call | flops 117964800 | bytes 2830336 | tf_op jit(solution)/shard_map/pallas_call | solution.py:159
  26.1 5.7 %collective-permute-done.10.refs_0_ = bf16[336,384]{1,0:T(8,128)(2,1)S(1)} collective-permute-done((bf16[336,384]{1,0:T(8,128)(2,1)S(1)}, bf16[336,384]{1,0:T(8,128)(2,1)S(1)}, u32[]{:S(2)}, u32[]{:S(2)}) %collective-permute-start.10) | collective-permute-done | bytes 258080 | tf_op jit(solution)/shard_map/ppermute | solution.py:587
  31.8 3.9 %shard_map.115.own_ref = f32[264,384]{1,0:T(8,128)S(1)} custom-call(s32[3]{0:T(128)S(1)} %pad_add_fusion.place_ref, bf16[640,80]{1,0:T(8,128)(2,1)S(1)} %copy-done.5, bf16[336,384]{1,0:T(8,128)(2,1)S(1)} %collective-permute-done.10.refs_0_, f32[160,1536]{1,0:T(8,128)S(1)} %get-tuple-element.34.refs_1_, bf16[4,192,192]{2,1,0:T(8,128)(2,1)S(1)} %get-tuple-element.35.refs_2_, ...), custom_call_target="tpu_custom_call" | custom-call | bytes 2050048 | tf_op jit(solution)/shard_map/pallas_call | solution.py:159
  35.8 1.7 %collective-permute-done.11.other_ref = f32[264,384]{1,0:T(8,128)S(1)} collective-permute-done((f32[264,384]{1,0:T(8,128)S(1)}, f32[264,384]{1,0:T(8,128)S(1)}, u32[]{:S(2)}, u32[]{:S(2)}) %collective-permute-start.11) | collective-permute-done | bytes 405536 | tf_op jit(solution)/shard_map/ppermute | solution.py:580
  37.5 1.3 %shard_map.116 = (bf16[136,384]{1,0:T(8,128)(2,1)S(1)}, bf16[136,384]{1,0:T(8,128)(2,1)S(1)}, bf16[176,384]{1,0:T(8,128)(2,1)S(1)}, bf16[176,384]{1,0:T(8,128)(2,1)S(1)}, bf16[176,384]{1,0:T(8,128)(2,1)S(1)}) custom-call(s32[3]{0:T(128)S(1)} %pad_add_fusion.place_ref, bf16[8,2,128,256]{3,2,1,0:T(8,128)(2,1)S(1)} %copy-done.1, ...), custom_call_target="tpu_custom_call" | custom-call | bytes 2473984 | tf_op jit(solution)/shard_map/pallas_call | solution.py:159
  38.8 2.6 %collective-permute-start.13 = (bf16[176,384]{1,0:T(8,128)(2,1)S(1)}, bf16[176,384]{1,0:T(8,128)(2,1)S(1)}, u32[]{:S(2)}, u32[]{:S(2)}) collective-permute-start(bf16[176,384]{1,0:T(8,128)(2,1)S(1)} %get-tuple-element.42), channel_id=1, source_target_pairs={{0,24},{2,30},{4,28},{6,26},{8,16},{10,22},{12,20},{14,18},{16,8},... | collective-permute-start | bytes 405512 | tf_op jit(solution)/shard_map/ppermute | solution.py:584
  41.4 1.9 %collective-permute-start.15 = (bf16[176,384]{1,0:T(8,128)(2,1)S(1)}, bf16[176,384]{1,0:T(8,128)(2,1)S(1)}, u32[]{:S(2)}, u32[]{:S(2)}) collective-permute-start(bf16[176,384]{1,0:T(8,128)(2,1)S(1)} %get-tuple-element.48), channel_id=1, source_target_pairs={{0,16},{2,22},{4,20},{6,18},{8,24},{10,30},{12,28},{14,26},{16,0},... | collective-permute-start | bytes 405512 | tf_op jit(solution)/shard_map/ppermute | solution.py:584
  43.2 1.0 %collective-permute-start.12 = (bf16[136,384]{1,0:T(8,128)(2,1)S(1)}, bf16[136,384]{1,0:T(8,128)(2,1)S(1)}, u32[]{:S(2)}, u32[]{:S(2)}) collective-permute-start(bf16[136,384]{1,0:T(8,128)(2,1)S(1)} %get-tuple-element.38), channel_id=1, source_target_pairs={{0,4},{2,6},{4,0},{6,2},{8,12},{10,14},{12,8},{14,10},{16,20},{18,... | collective-permute-start | bytes 313352 | tf_op jit(solution)/shard_map/ppermute | solution.py:584
  44.3 6.4 %collective-permute-done.12.refs_1_ = bf16[136,384]{1,0:T(8,128)(2,1)S(1)} collective-permute-done((bf16[136,384]{1,0:T(8,128)(2,1)S(1)}, bf16[136,384]{1,0:T(8,128)(2,1)S(1)}, u32[]{:S(2)}, u32[]{:S(2)}) %collective-permute-start.12) | collective-permute-done | bytes 104480 | tf_op jit(solution)/shard_map/ppermute | solution.py:584
  50.6 0.9 %shard_map.117 = (f32[2,40,384]{2,1,0:T(8,128)S(1)}, f32[2,4,96,96]{3,2,1,0:T(8,128)S(1)}, f32[2,192]{1,0:T(2,128)S(1)}) custom-call(s32[3]{0:T(128)S(1)} %pad_add_fusion.place_ref, bf16[136,384]{1,0:T(8,128)(2,1)S(1)} %get-tuple-element.37.refs_0_, bf16[136,384]{1,0:T(8,128)(2,1)S(1)} %collective-permute-done.12.refs_1_), custom_call_target="tpu_custom_call" | custom-call | bytes 628224 | tf_op jit(solution)/shard_map/pallas_call | solution.py:159
  51.5 1.0 %collective-permute-done.14.refs_1_ = bf16[176,384]{1,0:T(8,128)(2,1)S(1)} collective-permute-done((bf16[176,384]{1,0:T(8,128)(2,1)S(1)}, bf16[176,384]{1,0:T(8,128)(2,1)S(1)}, u32[]{:S(2)}, u32[]{:S(2)}) %collective-permute-start.14) | collective-permute-done | bytes 135200 | tf_op jit(solution)/shard_map/ppermute | solution.py:584
  52.5 0.4 collective-permute-start.17
  52.9 0.2 collective-permute-start.18
  53.0 0.4 collective-permute-start.16
  53.4 1.0 %shard_map.118 = (f32[3,40,384]{2,1,0:T(8,128)S(1)}, f32[3,4,96,96]{3,2,1,0:T(8,128)S(1)}, f32[3,192]{1,0:T(4,128)S(1)}) custom-call(s32[3]{0:T(128)S(1)} %pad_add_fusion.place_ref, bf16[176,384]{1,0:T(8,128)(2,1)S(1)} %collective-permute-done.13.refs_0_, bf16[176,384]{1,0:T(8,128)(2,1)S(1)} %collective-permute-done.14.refs_1_, ...), custom_call_target="tpu_custom_call" | custom-call | bytes 1034496 | tf_op jit(solution)/shard_map/pallas_call | solution.py:159
  54.5 2.4 %shard_map.119 = (bf16[10,14,768]{2,1,0:T(8,128)(2,1)}, f32[2,8,96,96]{3,2,1,0:T(8,128)}, f32[2,8,96]{2,1,0:T(8,128)}, f32[2,8,96,96]{3,2,1,0:T(8,128)}) custom-call(s32[3]{0:T(128)S(1)} %pad_add_fusion.place_ref, f32[2,40,384]{2,1,0:T(8,128)S(1)} %get-tuple-element.43.refs_0_, f32[2,4,96,96]{3,2,1,0:T(8,128)S(1)} %get-tuple-element.44.refs_1_, ...), custom_call_target="tpu_custom_call" | custom-call | bytes 3069696 | tf_op jit(solution)/shard_map/pallas_call | solution.py:159
  (31 shorter events, 0.2 us)
Async XLA Ops:
  0.6 2.7 %collective-permute-start = (bf16[10,14,768]{2,1,0:T(8,128)(2,1)}, bf16[10,14,768]{2,1,0:T(8,128)(2,1)S(1)}, u32[]{:S(2)}, u32[]{:S(2)}) collective-permute-start(bf16[10,14,768]{2,1,0:T(8,128)(2,1)} %param.8), channel_id=1, source_target_pairs={{0,2},{2,0},{4,6},{6,4},{8,10},{10,8},{12,14},{14,12},{16,18},{18,... | collective-permute-start | bytes 645128 | tf_op jit(solution)/shard_map/ppermute | solution.py:580
  1.1 2.2 %collective-permute-start.1 = (bf16[10,14,768]{2,1,0:T(8,128)(2,1)}, bf16[10,14,768]{2,1,0:T(8,128)(2,1)S(1)}, u32[]{:S(2)}, u32[]{:S(2)}) collective-permute-start(bf16[10,14,768]{2,1,0:T(8,128)(2,1)} %refs_6_.1), channel_id=1, source_target_pairs={{0,2},{2,0},{4,6},{6,4},{8,10},{10,8},{12,14},{14,12},{16,18},{18,... | collective-permute-start | bytes 645128 | tf_op jit(solution)/shard_map/ppermute | solution.py:580
  1.3 20.9 %copy-start = (bf16[8,2,128,256]{3,2,1,0:T(8,128)(2,1)S(1)}, bf16[8,2,128,256]{3,2,1,0:T(8,128)(2,1)}, u32[]{:S(2)}) copy-start(bf16[8,2,128,256]{3,2,1,0:T(8,128)(2,1)} %constant.38.clone.table_ref) | copy-start | bytes 3145732
  4.2 9.2 %collective-permute-start.4 = (bf16[2,80,384]{2,1,0:T(8,128)(2,1)S(1)}, bf16[2,80,384]{2,1,0:T(8,128)(2,1)S(1)}, u32[]{:S(2)}, u32[]{:S(2)}) collective-permute-start(bf16[2,80,384]{2,1,0:T(8,128)(2,1)S(1)} %get-tuple-element.31), channel_id=1, source_target_pairs={{0,24},{2,30},{4,28},{6,26},{8,16},{10,22},{12,20},{14,18},{16,8},... | collective-permute-start | bytes 368648 | tf_op jit(solution)/shard_map/ppermute | solution.py:584
  9.3 7.6 %collective-permute-start.5 = (bf16[2,80,384]{2,1,0:T(8,128)(2,1)S(1)}, bf16[2,80,384]{2,1,0:T(8,128)(2,1)S(1)}, u32[]{:S(2)}, u32[]{:S(2)}) collective-permute-start(bf16[2,80,384]{2,1,0:T(8,128)(2,1)S(1)} %get-tuple-element.32), channel_id=1, source_target_pairs={{0,8},{2,14},{4,12},{6,10},{8,0},{10,6},{12,4},{14,2},{16,24},{18,... | collective-permute-start | bytes 368648 | tf_op jit(solution)/shard_map/ppermute | solution.py:584
  9.3 11.4 %collective-permute-start.6 = (bf16[2,80,384]{2,1,0:T(8,128)(2,1)S(1)}, bf16[2,80,384]{2,1,0:T(8,128)(2,1)S(1)}, u32[]{:S(2)}, u32[]{:S(2)}) collective-permute-start(bf16[2,80,384]{2,1,0:T(8,128)(2,1)S(1)} %get-tuple-element.33), channel_id=1, source_target_pairs={{0,16},{2,22},{4,20},{6,18},{8,24},{10,30},{12,28},{14,26},{16,0},... | collective-permute-start | bytes 368648 | tf_op jit(solution)/shard_map/ppermute | solution.py:584
  9.9 10.8 %collective-permute-start.2 = (bf16[80,384]{1,0:T(8,128)(2,1)S(1)}, bf16[80,384]{1,0:T(8,128)(2,1)S(1)}, u32[]{:S(2)}, u32[]{:S(2)}) collective-permute-start(bf16[80,384]{1,0:T(8,128)(2,1)S(1)} %get-tuple-element.30), channel_id=1, source_target_pairs={{0,4},{2,6},{4,0},{6,2},{8,12},{10,14},{12,8},{14,10},{16,20},{18,... | collective-permute-start | bytes 184328 | tf_op jit(solution)/shard_map/ppermute | solution.py:584
  13.4 8.8 %collective-permute-start.7 = (bf16[2,80,384]{2,1,0:T(8,128)(2,1)S(1)}, bf16[2,80,384]{2,1,0:T(8,128)(2,1)S(1)}, u32[]{:S(2)}, u32[]{:S(2)}) collective-permute-start(bf16[2,80,384]{2,1,0:T(8,128)(2,1)S(1)} %collective-permute-done.4.refs_0_), channel_id=1, source_target_pairs={{0,2},{2,0},{4,6},{6,4},{8,10},{10,8},{12,14},{14,12},{16,18},{18,... | collective-permute-start | bytes 368648 | tf_op jit(solution)/shard_map/ppermute | solution.py:580
  16.9 5.2 %collective-permute-start.8 = (bf16[2,80,384]{2,1,0:T(8,128)(2,1)S(1)}, bf16[2,80,384]{2,1,0:T(8,128)(2,1)S(1)}, u32[]{:S(2)}, u32[]{:S(2)}) collective-permute-start(bf16[2,80,384]{2,1,0:T(8,128)(2,1)S(1)} %collective-permute-done.5.refs_1_), channel_id=1, source_target_pairs={{0,2},{2,0},{4,6},{6,4},{8,10},{10,8},{12,14},{14,12},{16,18},{18,... | collective-permute-start | bytes 368648 | tf_op jit(solution)/shard_map/ppermute | solution.py:580
  20.7 1.4 %collective-permute-start.9 = (bf16[2,80,384]{2,1,0:T(8,128)(2,1)S(1)}, bf16[2,80,384]{2,1,0:T(8,128)(2,1)S(1)}, u32[]{:S(2)}, u32[]{:S(2)}) collective-permute-start(bf16[2,80,384]{2,1,0:T(8,128)(2,1)S(1)} %collective-permute-done.6.refs_2_), channel_id=1, source_target_pairs={{0,2},{2,0},{4,6},{6,4},{8,10},{10,8},{12,14},{14,12},{16,18},{18,... | collective-permute-start | bytes 368648 | tf_op jit(solution)/shard_map/ppermute | solution.py:580
  20.7 1.4 %collective-permute-start.3 = (bf16[80,384]{1,0:T(8,128)(2,1)S(1)}, bf16[80,384]{1,0:T(8,128)(2,1)S(1)}, u32[]{:S(2)}, u32[]{:S(2)}) collective-permute-start(bf16[80,384]{1,0:T(8,128)(2,1)S(1)} %collective-permute-done.2.side_ref), channel_id=1, source_target_pairs={{0,2},{2,0},{4,6},{6,4},{8,10},{10,8},{12,14},{14,12},{16,18},{18,... | collective-permute-start | bytes 184328 | tf_op jit(solution)/shard_map/ppermute | solution.py:580
  22.2 2.6 %copy-start.3 = (f32[2,8,96,96]{3,2,1,0:T(8,128)S(1)}, f32[2,8,96,96]{3,2,1,0:T(8,128)}, u32[]{:S(2)}) copy-start(f32[2,8,96,96]{3,2,1,0:T(8,128)} %win_ref.1) | copy-start | bytes 1769476
  22.2 2.6 %copy-start.4 = (f32[2,8,96,96]{3,2,1,0:T(8,128)S(1)}, f32[2,8,96,96]{3,2,1,0:T(8,128)}, u32[]{:S(2)}) copy-start(f32[2,8,96,96]{3,2,1,0:T(8,128)} %wout_ref.1) | copy-start | bytes 1769476
  22.2 2.6 %copy-start.5 = (bf16[640,80]{1,0:T(8,128)(2,1)S(1)}, bf16[640,80]{1,0:T(8,128)(2,1)}, u32[]{:S(2)}) copy-start(bf16[640,80]{1,0:T(8,128)(2,1)} %constant.39.clone.table_ref) | copy-start | bytes 307204
  22.2 2.6 %copy-start.6 = (f32[2,8,96]{2,1,0:T(8,128)S(1)}, f32[2,8,96]{2,1,0:T(8,128)}, u32[]{:S(2)}) copy-start(f32[2,8,96]{2,1,0:T(8,128)} %bin_ref.1) | copy-start | bytes 18436
  23.3 8.5 %collective-permute-start.10 = (bf16[336,384]{1,0:T(8,128)(2,1)S(1)}, bf16[336,384]{1,0:T(8,128)(2,1)S(1)}, u32[]{:S(2)}, u32[]{:S(2)}) collective-permute-start(bf16[336,384]{1,0:T(8,128)(2,1)S(1)} %shard_map.113.spec_ref), channel_id=1, source_target_pairs={{0,1},{1,0},{2,3},{3,2},{4,5},{5,4},{6,7},{7,6},{8,9},{9,8},{10,11... | collective-permute-start | bytes 774152 | tf_op jit(solution)/shard_map/ppermute | solution.py:587
  31.8 5.7 %copy-start.1 = (bf16[8,2,128,256]{3,2,1,0:T(8,128)(2,1)S(1)}, bf16[8,2,128,256]{3,2,1,0:T(8,128)(2,1)}, u32[]{:S(2)}) copy-start(bf16[8,2,128,256]{3,2,1,0:T(8,128)(2,1)} %constant.40.clone.table_ref) | copy-start | bytes 3145732
  35.7 1.8 %collective-permute-start.11 = (f32[264,384]{1,0:T(8,128)S(1)}, f32[264,384]{1,0:T(8,128)S(1)}, u32[]{:S(2)}, u32[]{:S(2)}) collective-permute-start(f32[264,384]{1,0:T(8,128)S(1)} %shard_map.115.own_ref), channel_id=1, source_target_pairs={{0,2},{2,0},{4,6},{6,4},{8,10},{10,8},{12,14},{14,12},{16,18},{18,... | collective-permute-start | bytes 1216520 | tf_op jit(solution)/shard_map/ppermute | solution.py:580
  38.8 12.7 %collective-permute-start.13 = (bf16[176,384]{1,0:T(8,128)(2,1)S(1)}, bf16[176,384]{1,0:T(8,128)(2,1)S(1)}, u32[]{:S(2)}, u32[]{:S(2)}) collective-permute-start(bf16[176,384]{1,0:T(8,128)(2,1)S(1)} %get-tuple-element.42), channel_id=1, source_target_pairs={{0,24},{2,30},{4,28},{6,26},{8,16},{10,22},{12,20},{14,18},{16,8},... | collective-permute-start | bytes 405512 | tf_op jit(solution)/shard_map/ppermute | solution.py:584
  41.4 11.1 %collective-permute-start.14 = (bf16[176,384]{1,0:T(8,128)(2,1)S(1)}, bf16[176,384]{1,0:T(8,128)(2,1)S(1)}, u32[]{:S(2)}, u32[]{:S(2)}) collective-permute-start(bf16[176,384]{1,0:T(8,128)(2,1)S(1)} %get-tuple-element.47), channel_id=1, source_target_pairs={{0,8},{2,14},{4,12},{6,10},{8,0},{10,6},{12,4},{14,2},{16,24},{18,... | collective-permute-start | bytes 405512 | tf_op jit(solution)/shard_map/ppermute | solution.py:584
  41.4 11.5 %collective-permute-start.15 = (bf16[176,384]{1,0:T(8,128)(2,1)S(1)}, bf16[176,384]{1,0:T(8,128)(2,1)S(1)}, u32[]{:S(2)}, u32[]{:S(2)}) collective-permute-start(bf16[176,384]{1,0:T(8,128)(2,1)S(1)} %get-tuple-element.48), channel_id=1, source_target_pairs={{0,16},{2,22},{4,20},{6,18},{8,24},{10,30},{12,28},{14,26},{16,0},... | collective-permute-start | bytes 405512 | tf_op jit(solution)/shard_map/ppermute | solution.py:584
  43.2 7.4 %collective-permute-start.12 = (bf16[136,384]{1,0:T(8,128)(2,1)S(1)}, bf16[136,384]{1,0:T(8,128)(2,1)S(1)}, u32[]{:S(2)}, u32[]{:S(2)}) collective-permute-start(bf16[136,384]{1,0:T(8,128)(2,1)S(1)} %get-tuple-element.38), channel_id=1, source_target_pairs={{0,4},{2,6},{4,0},{6,2},{8,12},{10,14},{12,8},{14,10},{16,20},{18,... | collective-permute-start | bytes 313352 | tf_op jit(solution)/shard_map/ppermute | solution.py:584
  51.5 2.9 %copy-start.2 = (bf16[10,14,768]{2,1,0:T(8,128)(2,1)S(1)}, bf16[10,14,768]{2,1,0:T(8,128)(2,1)}, u32[]{:S(2)}) copy-start(bf16[10,14,768]{2,1,0:T(8,128)(2,1)} %refs_6_.1) | copy-start | bytes 645124
  52.5 1.9 %collective-permute-start.17 = (bf16[176,384]{1,0:T(8,128)(2,1)S(1)}, bf16[176,384]{1,0:T(8,128)(2,1)S(1)}, u32[]{:S(2)}, u32[]{:S(2)}) collective-permute-start(bf16[176,384]{1,0:T(8,128)(2,1)S(1)} %collective-permute-done.14.refs_1_), channel_id=1, source_target_pairs={{0,2},{2,0},{4,6},{6,4},{8,10},{10,8},{12,14},{14,12},{16,18},{18,... | collective-permute-start | bytes 405512 | tf_op jit(solution)/shard_map/ppermute | solution.py:580
  52.9 1.6 %collective-permute-start.18 = (bf16[176,384]{1,0:T(8,128)(2,1)S(1)}, bf16[176,384]{1,0:T(8,128)(2,1)S(1)}, u32[]{:S(2)}, u32[]{:S(2)}) collective-permute-start(bf16[176,384]{1,0:T(8,128)(2,1)S(1)} %collective-permute-done.15.refs_2_), channel_id=1, source_target_pairs={{0,2},{2,0},{4,6},{6,4},{8,10},{10,8},{12,14},{14,12},{16,18},{18,... | collective-permute-start | bytes 405512 | tf_op jit(solution)/shard_map/ppermute | solution.py:580
  53.0 1.4 %collective-permute-start.16 = (bf16[176,384]{1,0:T(8,128)(2,1)S(1)}, bf16[176,384]{1,0:T(8,128)(2,1)S(1)}, u32[]{:S(2)}, u32[]{:S(2)}) collective-permute-start(bf16[176,384]{1,0:T(8,128)(2,1)S(1)} %collective-permute-done.13.refs_0_), channel_id=1, source_target_pairs={{0,2},{2,0},{4,6},{6,4},{8,10},{10,8},{12,14},{14,12},{16,18},{18,... | collective-permute-start | bytes 405512 | tf_op jit(solution)/shard_map/ppermute | solution.py:580

commit v9 on v8

--- a/solution.py
+++ b/solution.py
@@ -75,8 +75,9 @@
     whole = []
     for place in range(blocks):
         for member in range(2):
-            sources = [(0, 0), (0, 1), (1, member), (1, 1 - member)]
-            sources += [(base + m, n) for m in (member, 1 - member) for base in BASES for n in range(2)]
+            sources = [(0, 0), (0, 1), (1, member)]
+            sources += [(base + member, n) for base in BASES for n in range(2)] + [(1, 1 - member)]
+            sources += [(base + 1 - member, n) for base in BASES for n in range(2)]
             rows = np.stack([table[place ^ k, n, :, member] for k, n in sources])
             rows = rows.transpose(2, 0, 1).reshape(modes, -1)
             whole.append(np.concatenate(halves(rows)))
@@ -200,16 +201,24 @@
         ref[1 - member] = pack_ref[target]
 
 
-def paired_lon_kernel(place_ref, table_ref, own_ref, side_ref, other_side_ref, *refs):
-    pieces = [own_ref.at[0], own_ref.at[1], side_ref, other_side_ref]
-    pieces += [ref.at[n] for ref in refs[:-2] for n in range(2)]
-    coded_ref, spec_ref = refs[-2:]
+def early_lon_kernel(place_ref, table_ref, own_ref, side_ref, *refs):
+    sent, out_ref = refs[:-1], refs[-1]
+    pieces = [own_ref.at[0], own_ref.at[1], side_ref] + [ref.at[n] for ref in sent for n in range(2)]
+    table = table_ref[0, 0][:, : len(pieces) * PAD]
+    for q in range(out_ref.shape[0]):
+        data = [piece[q * PAD : (q + 1) * PAD, :] for piece in pieces]
+        out_ref[q] = dot(table, jnp.concatenate(data, axis=0))
+
+
+def late_lon_kernel(place_ref, table_ref, early_ref, side_ref, *refs):
+    late, (coded_ref, spec_ref) = refs[:-2], refs[-2:]
+    pieces = [side_ref] + [ref.at[n] for ref in late for n in range(2)]
     pairs, modes, lanes = spec_ref.shape
-    table = table_ref[0, 0]
+    table = table_ref[0, 0][:, table_ref.shape[3] - len(pieces) * PAD :]
     tops = []
     for q in range(pairs):
         data = [piece[q * PAD : (q + 1) * PAD, :] for piece in pieces]
-        total = dot(table, jnp.concatenate(data, axis=0))
+        total = early_ref[q] + dot(table, jnp.concatenate(data, axis=0))
         spec = total[:modes] + total[modes:]
         spec_ref[q] = spec
         tops.append(jnp.max(jnp.abs(spec), axis=0, keepdims=True))
@@ -311,6 +320,12 @@
     slopes = cdf + pre * jnp.exp(-0.5 * pre * pre) * density_norm
     grad_pre = dot3(g_parts, m_out, ((1,), (1,))) * slopes
     p_parts = split(grad_pre)
+    products = []
+    for left, right in ((x_parts, p_parts), (split(hidden), g_parts)):
+        total = dot3(left, right, ((0,), (0,)))
+        products.append(total[:width, :width] + total[width:, width:])
+        products.append(total[:width, width:] - total[width:, :width])
+    weights = jnp.concatenate(products, axis=1) * scaling
     grad_spec = dot3(p_parts, m_in, ((1,), (1,)))
     lanes = []
     for n in range(subs):
@@ -333,12 +348,6 @@
                 row = (q * subs // 2 + n) * tile
                 back_ref[row : row + tile, :] = jnp.concatenate([band[n], band[n + subs // 2]], axis=1)
 
-    pieces = []
-    for left, right in ((x_parts, p_parts), (split(hidden), g_parts)):
-        total = dot3(left, right, ((0,), (0,)))
-        pieces.append(total[:width, :width] + total[width:, width:])
-        pieces.append(total[:width, width:] - total[width:, :width])
-    weights = jnp.concatenate(pieces, axis=1) * scaling
     bias = jnp.sum(grad_pre, axis=0, keepdims=True) * scaling
     if shares == 1:
         start = pairs * subs // 2 * tile
@@ -615,11 +624,12 @@
         side = to_place(side, 1, 1)
         sent = [side, *serve(slots)]
         late = [to_member(x, 1) for x in sent]
-        sent, late = [side, late[0], *sent[1:]], late[1:]
         table = paired_table(blocks, cols)
-        (coded,) = call(
-            paired_lon_kernel, scalars, (table, own, *sent, *late), specs={0: by_place(table)}, **spectrum
+        specs = {0: by_place(table)}
+        (early,) = call(
+            early_lon_kernel, scalars, (table, own, *sent), (shape((pairs, 2 * modes, wide), f32),), specs=specs
         )
+        (coded,) = call(late_lon_kernel, scalars, (table, early, *late), specs=specs, **spectrum)
     else:
         (packed,) = call(
             functools.partial(pack_kernel, width),

time: 57 us -> 56.9 us (level)
  waiting for transfers between devices: 24 us -> 23.1 us
  Pallas kernels: 13.4 us -> 14.2 us
    ppermute x10, waiting for transfers between devices: 2.66 us -> 1.75 us  [to_member(): return lax.ppermute(values, 'lon', turn)]
    pallas_call x9 -> x10, Pallas kernels: 13.4 us -> 14.2 us  [call(): pl.pallas_call(kernel, grid_spec=pltpu.PrefetchScalarGridSpec(num_scalar_...]
  transfers between devices with their start and end apart: 19 -> 19, of which waited for: 8 -> 7; matrix products, arithmetic and copies ran while one was open for 2% -> 2% of each run, Pallas kernels for 7% -> 9%
where the time goes in v9:
time: 56.9 us; the launch traced here: 56.7 us
  waiting for transfers between devices  23.1 us (41%)
  starting transfers between devices  17.3 us (30%)
  Pallas kernels  14.2 us (25%)
  other arithmetic  1.29 us (2%)
  between operations  0.84 us (1%)
    ppermute x8, waiting for transfers between devices, to_place(): return lax.ppermute(values, 'lon', turn)  15.7 us
    pallas_call x10, Pallas kernels, call(): pl.pallas_call(kernel, grid_spec=pltpu.PrefetchScalarGridSpec(num_scalar_...  14.2 us
    ppermute x8, starting transfers between devices, to_place(): return lax.ppermute(values, 'lon', turn)  12.9 us
    ppermute x1, waiting for transfers between devices, to_lat(): lax.ppermute(values, 'lat', [(i, (i + step) % lat_count) for i in range(l...  5.64 us
    ppermute x10, starting transfers between devices, to_member(): return lax.ppermute(values, 'lon', turn)  2.86 us
    ppermute x10, waiting for transfers between devices, to_member(): return lax.ppermute(values, 'lon', turn)  1.75 us
    ppermute x1, starting transfers between devices, to_lat(): lax.ppermute(values, 'lat', [(i, (i + step) % lat_count) for i in range(l...  1.55 us
    another operation x1, other arithmetic, body(): jnp.stack([features, cotangent])  1.21 us
  transfers between devices with their start and end apart: 19, of which 7 were waited for; matrix products, arithmetic and copies ran while one was open for 2% of the time, Pallas kernels for 9%

profile of v9, /device:TPU:0, one launch (start us, length us, event | category | flops | bytes accessed | tf_op | source)
XLA Modules:
  0.0 56.7 jit_solution(13365720793554951763)
XLA Ops:
  0.6 0.5 collective-permute-start
  1.1 0.1 collective-permute-start.1
  1.3 1.2 %pad_maximum_fusion.fields_ref = bf16[2,10,14,768]{3,2,1,0:T(8,128)(2,1)S(1)} fusion(bf16[1,10,14,768]{3,2,1,0:T(8,128)(2,1)} %bitcast.5, bf16[1,10,14,768]{3,2,1,0:T(8,128)(2,1)} %bitcast.6), kind=kLoop, calls=%fused_computation | loop fusion | flops 215040 | bytes 860160 | tf_op jit(solution)/shard_map/stack | solution.py:613
  2.5 0.8 %shard_map.111 = (bf16[8,80,384]{2,1,0:T(8,128)(2,1)S(1)}, bf16[80,384]{1,0:T(8,128)(2,1)S(1)}) custom-call(s32[3]{0:T(128)S(1)} %pad_add_fusion.place_ref, bf16[2,10,14,768]{3,2,1,0:T(8,128)(2,1)S(1)} %pad_maximum_fusion.fields_ref), custom_call_target="tpu_custom_call" | custom-call | flops 100000000 | bytes 983040 | tf_op jit(solution)/shard_map/pallas_call | solution.py:160
  3.4 0.8 %shard_map.112 = (bf16[2,80,384]{2,1,0:T(8,128)(2,1)S(1)}, bf16[2,80,384]{2,1,0:T(8,128)(2,1)S(1)}, bf16[2,80,384]{2,1,0:T(8,128)(2,1)S(1)}, bf16[2,80,384]{2,1,0:T(8,128)(2,1)S(1)}) custom-call(s32[3]{0:T(128)S(1)} %pad_add_fusion.place_ref, bf16[8,80,384]{2,1,0:T(8,128)(2,1)S(1)} %get-tuple-element.28.own_ref, ...), custom_call_target="tpu_custom_call" | custom-call | bytes 1413120 | tf_op jit(solution)/shard_map/pallas_call | solution.py:160
  4.2 5.1 %collective-permute-start.3 = (bf16[2,80,384]{2,1,0:T(8,128)(2,1)S(1)}, bf16[2,80,384]{2,1,0:T(8,128)(2,1)S(1)}, u32[]{:S(2)}, u32[]{:S(2)}) collective-permute-start(bf16[2,80,384]{2,1,0:T(8,128)(2,1)S(1)} %get-tuple-element.31), channel_id=1, source_target_pairs={{0,24},{2,30},{4,28},{6,26},{8,16},{10,22},{12,20},{14,18},{16,8},... | collective-permute-start | bytes 368648 | tf_op jit(solution)/shard_map/ppermute | solution.py:593
  9.3 0.6 %collective-permute-start.5 = (bf16[2,80,384]{2,1,0:T(8,128)(2,1)S(1)}, bf16[2,80,384]{2,1,0:T(8,128)(2,1)S(1)}, u32[]{:S(2)}, u32[]{:S(2)}) collective-permute-start(bf16[2,80,384]{2,1,0:T(8,128)(2,1)S(1)} %get-tuple-element.33), channel_id=1, source_target_pairs={{0,16},{2,22},{4,20},{6,18},{8,24},{10,30},{12,28},{14,26},{16,0},... | collective-permute-start | bytes 368648 | tf_op jit(solution)/shard_map/ppermute | solution.py:593
  9.9 1.7 %collective-permute-start.2 = (bf16[80,384]{1,0:T(8,128)(2,1)S(1)}, bf16[80,384]{1,0:T(8,128)(2,1)S(1)}, u32[]{:S(2)}, u32[]{:S(2)}) collective-permute-start(bf16[80,384]{1,0:T(8,128)(2,1)S(1)} %get-tuple-element.30), channel_id=1, source_target_pairs={{0,4},{2,6},{4,0},{6,2},{8,12},{10,14},{12,8},{14,10},{16,20},{18,... | collective-permute-start | bytes 184328 | tf_op jit(solution)/shard_map/ppermute | solution.py:593
  11.6 1.8 %collective-permute-done.3.refs_0_ = bf16[2,80,384]{2,1,0:T(8,128)(2,1)S(1)} collective-permute-done((bf16[2,80,384]{2,1,0:T(8,128)(2,1)S(1)}, bf16[2,80,384]{2,1,0:T(8,128)(2,1)S(1)}, u32[]{:S(2)}, u32[]{:S(2)}) %collective-permute-start.3) | collective-permute-done | bytes 122912 | tf_op jit(solution)/shard_map/ppermute | solution.py:593
  13.4 3.6 %collective-permute-done.4.refs_1_ = bf16[2,80,384]{2,1,0:T(8,128)(2,1)S(1)} collective-permute-done((bf16[2,80,384]{2,1,0:T(8,128)(2,1)S(1)}, bf16[2,80,384]{2,1,0:T(8,128)(2,1)S(1)}, u32[]{:S(2)}, u32[]{:S(2)}) %collective-permute-start.4) | collective-permute-done | bytes 122912 | tf_op jit(solution)/shard_map/ppermute | solution.py:593
  16.9 0.9 %collective-permute-start.8 = (bf16[2,80,384]{2,1,0:T(8,128)(2,1)S(1)}, bf16[2,80,384]{2,1,0:T(8,128)(2,1)S(1)}, u32[]{:S(2)}, u32[]{:S(2)}) collective-permute-start(bf16[2,80,384]{2,1,0:T(8,128)(2,1)S(1)} %collective-permute-done.4.refs_1_), channel_id=1, source_target_pairs={{0,2},{2,0},{4,6},{6,4},{8,10},{10,8},{12,14},{14,12},{16,18},{18,... | collective-permute-start | bytes 368648 | tf_op jit(solution)/shard_map/ppermute | solution.py:589
  17.8 3.0 %collective-permute-done.5.refs_2_ = bf16[2,80,384]{2,1,0:T(8,128)(2,1)S(1)} collective-permute-done((bf16[2,80,384]{2,1,0:T(8,128)(2,1)S(1)}, bf16[2,80,384]{2,1,0:T(8,128)(2,1)S(1)}, u32[]{:S(2)}, u32[]{:S(2)}) %collective-permute-start.5) | collective-permute-done | bytes 122912 | tf_op jit(solution)/shard_map/ppermute | solution.py:593
  20.7 0.5 collective-permute-start.6
  21.3 0.9 %shard_map.113.early_ref = f32[5,128,384]{2,1,0:T(8,128)S(1)} custom-call(s32[3]{0:T(128)S(1)} %pad_add_fusion.place_ref, bf16[8,2,128,256]{3,2,1,0:T(8,128)(2,1)S(1)} %copy-done, bf16[2,80,384]{2,1,0:T(8,128)(2,1)S(1)} %get-tuple-element.29.own_ref, bf16[80,384]{1,0:T(8,128)(2,1)S(1)} %collective-permute-done.2.side_ref, ...), custom_call_target="tpu_custom_call" | custom-call | bytes 2584576 | tf_op jit(solution)/shard_map/pallas_call | solution.py:160
  22.2 1.0 %shard_map.114.spec_ref = bf16[336,384]{1,0:T(8,128)(2,1)S(1)} custom-call(s32[3]{0:T(128)S(1)} %pad_add_fusion.place_ref, bf16[8,2,128,256]{3,2,1,0:T(8,128)(2,1)S(1)} %copy-done, f32[5,128,384]{2,1,0:T(8,128)S(1)} %shard_map.113.early_ref, bf16[80,384]{1,0:T(8,128)(2,1)S(1)} %collective-permute-done.6.side_ref, ...), custom_call_target="tpu_custom_call" | custom-call | bytes 2719744 | tf_op jit(solution)/shard_map/pallas_call | solution.py:160
  23.3 1.6 %collective-permute-start.10 = (bf16[336,384]{1,0:T(8,128)(2,1)S(1)}, bf16[336,384]{1,0:T(8,128)(2,1)S(1)}, u32[]{:S(2)}, u32[]{:S(2)}) collective-permute-start(bf16[336,384]{1,0:T(8,128)(2,1)S(1)} %shard_map.114.spec_ref), channel_id=1, source_target_pairs={{0,1},{1,0},{2,3},{3,2},{4,5},{5,4},{6,7},{7,6},{8,9},{9,8},{10,11... | collective-permute-start | bytes 774152 | tf_op jit(solution)/shard_map/ppermute | solution.py:596
  24.8 1.3 %shard_map.115 = (f32[160,1536]{1,0:T(8,128)S(1)}, bf16[4,192,192]{2,1,0:T(8,128)(2,1)S(1)}, f32[8,192]{1,0:T(8,128)S(1)}) custom-call(s32[3]{0:T(128)S(1)} %pad_add_fusion.place_ref, bf16[640,80]{1,0:T(8,128)(2,1)S(1)} %copy-done.5, bf16[336,384]{1,0:T(8,128)(2,1)S(1)} %shard_map.114.spec_ref, f32[2,8,96,96]{3,2,1,0:T(8,128)S(1)} %copy-done.3, ...), custom_call_target="tpu_custom_call" | custom-call | flops 117964800 | bytes 2830336 | tf_op jit(solution)/shard_map/pallas_call | solution.py:160
  26.1 5.6 %collective-permute-done.10.refs_0_ = bf16[336,384]{1,0:T(8,128)(2,1)S(1)} collective-permute-done((bf16[336,384]{1,0:T(8,128)(2,1)S(1)}, bf16[336,384]{1,0:T(8,128)(2,1)S(1)}, u32[]{:S(2)}, u32[]{:S(2)}) %collective-permute-start.10) | collective-permute-done | bytes 258080 | tf_op jit(solution)/shard_map/ppermute | solution.py:596
  31.7 3.8 %shard_map.116.own_ref = f32[264,384]{1,0:T(8,128)S(1)} custom-call(s32[3]{0:T(128)S(1)} %pad_add_fusion.place_ref, bf16[640,80]{1,0:T(8,128)(2,1)S(1)} %copy-done.5, bf16[336,384]{1,0:T(8,128)(2,1)S(1)} %collective-permute-done.10.refs_0_, f32[160,1536]{1,0:T(8,128)S(1)} %get-tuple-element.34.refs_1_, bf16[4,192,192]{2,1,0:T(8,128)(2,1)S(1)} %get-tuple-element.35.refs_2_, ...), custom_call_target="tpu_custom_call" | custom-call | bytes 2050048 | tf_op jit(solution)/shard_map/pallas_call | solution.py:160
  35.6 1.7 %collective-permute-done.11.other_ref = f32[264,384]{1,0:T(8,128)S(1)} collective-permute-done((f32[264,384]{1,0:T(8,128)S(1)}, f32[264,384]{1,0:T(8,128)S(1)}, u32[]{:S(2)}, u32[]{:S(2)}) %collective-permute-start.11) | collective-permute-done | bytes 405536 | tf_op jit(solution)/shard_map/ppermute | solution.py:589
  37.4 1.3 %shard_map.117 = (bf16[136,384]{1,0:T(8,128)(2,1)S(1)}, bf16[136,384]{1,0:T(8,128)(2,1)S(1)}, bf16[176,384]{1,0:T(8,128)(2,1)S(1)}, bf16[176,384]{1,0:T(8,128)(2,1)S(1)}, bf16[176,384]{1,0:T(8,128)(2,1)S(1)}) custom-call(s32[3]{0:T(128)S(1)} %pad_add_fusion.place_ref, bf16[8,2,128,256]{3,2,1,0:T(8,128)(2,1)S(1)} %copy-done.1, ...), custom_call_target="tpu_custom_call" | custom-call | bytes 2473984 | tf_op jit(solution)/shard_map/pallas_call | solution.py:160
  38.6 2.6 %collective-permute-start.13 = (bf16[176,384]{1,0:T(8,128)(2,1)S(1)}, bf16[176,384]{1,0:T(8,128)(2,1)S(1)}, u32[]{:S(2)}, u32[]{:S(2)}) collective-permute-start(bf16[176,384]{1,0:T(8,128)(2,1)S(1)} %get-tuple-element.42), channel_id=1, source_target_pairs={{0,24},{2,30},{4,28},{6,26},{8,16},{10,22},{12,20},{14,18},{16,8},... | collective-permute-start | bytes 405512 | tf_op jit(solution)/shard_map/ppermute | solution.py:593
  41.2 1.9 %collective-permute-start.15 = (bf16[176,384]{1,0:T(8,128)(2,1)S(1)}, bf16[176,384]{1,0:T(8,128)(2,1)S(1)}, u32[]{:S(2)}, u32[]{:S(2)}) collective-permute-start(bf16[176,384]{1,0:T(8,128)(2,1)S(1)} %get-tuple-element.48), channel_id=1, source_target_pairs={{0,16},{2,22},{4,20},{6,18},{8,24},{10,30},{12,28},{14,26},{16,0},... | collective-permute-start | bytes 405512 | tf_op jit(solution)/shard_map/ppermute | solution.py:593
  43.1 1.0 %collective-permute-start.12 = (bf16[136,384]{1,0:T(8,128)(2,1)S(1)}, bf16[136,384]{1,0:T(8,128)(2,1)S(1)}, u32[]{:S(2)}, u32[]{:S(2)}) collective-permute-start(bf16[136,384]{1,0:T(8,128)(2,1)S(1)} %get-tuple-element.38), channel_id=1, source_target_pairs={{0,4},{2,6},{4,0},{6,2},{8,12},{10,14},{12,8},{14,10},{16,20},{18,... | collective-permute-start | bytes 313352 | tf_op jit(solution)/shard_map/ppermute | solution.py:593
  44.1 6.3 %collective-permute-done.12.refs_1_ = bf16[136,384]{1,0:T(8,128)(2,1)S(1)} collective-permute-done((bf16[136,384]{1,0:T(8,128)(2,1)S(1)}, bf16[136,384]{1,0:T(8,128)(2,1)S(1)}, u32[]{:S(2)}, u32[]{:S(2)}) %collective-permute-start.12) | collective-permute-done | bytes 104480 | tf_op jit(solution)/shard_map/ppermute | solution.py:593
  50.5 0.9 %shard_map.118 = (f32[2,40,384]{2,1,0:T(8,128)S(1)}, f32[2,4,96,96]{3,2,1,0:T(8,128)S(1)}, f32[2,192]{1,0:T(2,128)S(1)}) custom-call(s32[3]{0:T(128)S(1)} %pad_add_fusion.place_ref, bf16[136,384]{1,0:T(8,128)(2,1)S(1)} %get-tuple-element.37.refs_0_, bf16[136,384]{1,0:T(8,128)(2,1)S(1)} %collective-permute-done.12.refs_1_), custom_call_target="tpu_custom_call" | custom-call | bytes 628224 | tf_op jit(solution)/shard_map/pallas_call | solution.py:160
  51.4 1.0 %collective-permute-done.14.refs_1_ = bf16[176,384]{1,0:T(8,128)(2,1)S(1)} collective-permute-done((bf16[176,384]{1,0:T(8,128)(2,1)S(1)}, bf16[176,384]{1,0:T(8,128)(2,1)S(1)}, u32[]{:S(2)}, u32[]{:S(2)}) %collective-permute-start.14) | collective-permute-done | bytes 135200 | tf_op jit(solution)/shard_map/ppermute | solution.py:593
  52.4 0.3 collective-permute-start.17
  52.7 0.2 collective-permute-start.18
  52.9 0.3 collective-permute-start.16
  53.2 1.0 %shard_map.119 = (f32[3,40,384]{2,1,0:T(8,128)S(1)}, f32[3,4,96,96]{3,2,1,0:T(8,128)S(1)}, f32[3,192]{1,0:T(4,128)S(1)}) custom-call(s32[3]{0:T(128)S(1)} %pad_add_fusion.place_ref, bf16[176,384]{1,0:T(8,128)(2,1)S(1)} %collective-permute-done.13.refs_0_, bf16[176,384]{1,0:T(8,128)(2,1)S(1)} %collective-permute-done.14.refs_1_, ...), custom_call_target="tpu_custom_call" | custom-call | bytes 1034496 | tf_op jit(solution)/shard_map/pallas_call | solution.py:160
  54.3 2.4 %shard_map.120 = (bf16[10,14,768]{2,1,0:T(8,128)(2,1)}, f32[2,8,96,96]{3,2,1,0:T(8,128)}, f32[2,8,96]{2,1,0:T(8,128)}, f32[2,8,96,96]{3,2,1,0:T(8,128)}) custom-call(s32[3]{0:T(128)S(1)} %pad_add_fusion.place_ref, f32[2,40,384]{2,1,0:T(8,128)S(1)} %get-tuple-element.43.refs_0_, f32[2,4,96,96]{3,2,1,0:T(8,128)S(1)} %get-tuple-element.44.refs_1_, ...), custom_call_target="tpu_custom_call" | custom-call | bytes 3069696 | tf_op jit(solution)/shard_map/pallas_call | solution.py:160
  (32 shorter events, 0.2 us)
Async XLA Ops:
  0.6 2.7 %collective-permute-start = (bf16[10,14,768]{2,1,0:T(8,128)(2,1)}, bf16[10,14,768]{2,1,0:T(8,128)(2,1)S(1)}, u32[]{:S(2)}, u32[]{:S(2)}) collective-permute-start(bf16[10,14,768]{2,1,0:T(8,128)(2,1)} %param.8), channel_id=1, source_target_pairs={{0,2},{2,0},{4,6},{6,4},{8,10},{10,8},{12,14},{14,12},{16,18},{18,... | collective-permute-start | bytes 645128 | tf_op jit(solution)/shard_map/ppermute | solution.py:589
  1.1 2.2 %collective-permute-start.1 = (bf16[10,14,768]{2,1,0:T(8,128)(2,1)}, bf16[10,14,768]{2,1,0:T(8,128)(2,1)S(1)}, u32[]{:S(2)}, u32[]{:S(2)}) collective-permute-start(bf16[10,14,768]{2,1,0:T(8,128)(2,1)} %refs_6_.1), channel_id=1, source_target_pairs={{0,2},{2,0},{4,6},{6,4},{8,10},{10,8},{12,14},{14,12},{16,18},{18,... | collective-permute-start | bytes 645128 | tf_op jit(solution)/shard_map/ppermute | solution.py:589
  1.3 19.9 %copy-start = (bf16[8,2,128,256]{3,2,1,0:T(8,128)(2,1)S(1)}, bf16[8,2,128,256]{3,2,1,0:T(8,128)(2,1)}, u32[]{:S(2)}) copy-start(bf16[8,2,128,256]{3,2,1,0:T(8,128)(2,1)} %constant.38.clone.table_ref) | copy-start | bytes 3145732
  4.2 9.2 %collective-permute-start.3 = (bf16[2,80,384]{2,1,0:T(8,128)(2,1)S(1)}, bf16[2,80,384]{2,1,0:T(8,128)(2,1)S(1)}, u32[]{:S(2)}, u32[]{:S(2)}) collective-permute-start(bf16[2,80,384]{2,1,0:T(8,128)(2,1)S(1)} %get-tuple-element.31), channel_id=1, source_target_pairs={{0,24},{2,30},{4,28},{6,26},{8,16},{10,22},{12,20},{14,18},{16,8},... | collective-permute-start | bytes 368648 | tf_op jit(solution)/shard_map/ppermute | solution.py:593
  9.3 7.6 %collective-permute-start.4 = (bf16[2,80,384]{2,1,0:T(8,128)(2,1)S(1)}, bf16[2,80,384]{2,1,0:T(8,128)(2,1)S(1)}, u32[]{:S(2)}, u32[]{:S(2)}) collective-permute-start(bf16[2,80,384]{2,1,0:T(8,128)(2,1)S(1)} %get-tuple-element.32), channel_id=1, source_target_pairs={{0,8},{2,14},{4,12},{6,10},{8,0},{10,6},{12,4},{14,2},{16,24},{18,... | collective-permute-start | bytes 368648 | tf_op jit(solution)/shard_map/ppermute | solution.py:593
  9.3 11.4 %collective-permute-start.5 = (bf16[2,80,384]{2,1,0:T(8,128)(2,1)S(1)}, bf16[2,80,384]{2,1,0:T(8,128)(2,1)S(1)}, u32[]{:S(2)}, u32[]{:S(2)}) collective-permute-start(bf16[2,80,384]{2,1,0:T(8,128)(2,1)S(1)} %get-tuple-element.33), channel_id=1, source_target_pairs={{0,16},{2,22},{4,20},{6,18},{8,24},{10,30},{12,28},{14,26},{16,0},... | collective-permute-start | bytes 368648 | tf_op jit(solution)/shard_map/ppermute | solution.py:593
  9.9 10.8 %collective-permute-start.2 = (bf16[80,384]{1,0:T(8,128)(2,1)S(1)}, bf16[80,384]{1,0:T(8,128)(2,1)S(1)}, u32[]{:S(2)}, u32[]{:S(2)}) collective-permute-start(bf16[80,384]{1,0:T(8,128)(2,1)S(1)} %get-tuple-element.30), channel_id=1, source_target_pairs={{0,4},{2,6},{4,0},{6,2},{8,12},{10,14},{12,8},{14,10},{16,20},{18,... | collective-permute-start | bytes 184328 | tf_op jit(solution)/shard_map/ppermute | solution.py:593
  13.4 8.8 %collective-permute-start.7 = (bf16[2,80,384]{2,1,0:T(8,128)(2,1)S(1)}, bf16[2,80,384]{2,1,0:T(8,128)(2,1)S(1)}, u32[]{:S(2)}, u32[]{:S(2)}) collective-permute-start(bf16[2,80,384]{2,1,0:T(8,128)(2,1)S(1)} %collective-permute-done.3.refs_0_), channel_id=1, source_target_pairs={{0,2},{2,0},{4,6},{6,4},{8,10},{10,8},{12,14},{14,12},{16,18},{18,... | collective-permute-start | bytes 368648 | tf_op jit(solution)/shard_map/ppermute | solution.py:589
  16.9 5.3 %collective-permute-start.8 = (bf16[2,80,384]{2,1,0:T(8,128)(2,1)S(1)}, bf16[2,80,384]{2,1,0:T(8,128)(2,1)S(1)}, u32[]{:S(2)}, u32[]{:S(2)}) collective-permute-start(bf16[2,80,384]{2,1,0:T(8,128)(2,1)S(1)} %collective-permute-done.4.refs_1_), channel_id=1, source_target_pairs={{0,2},{2,0},{4,6},{6,4},{8,10},{10,8},{12,14},{14,12},{16,18},{18,... | collective-permute-start | bytes 368648 | tf_op jit(solution)/shard_map/ppermute | solution.py:589
  20.7 1.5 %collective-permute-start.9 = (bf16[2,80,384]{2,1,0:T(8,128)(2,1)S(1)}, bf16[2,80,384]{2,1,0:T(8,128)(2,1)S(1)}, u32[]{:S(2)}, u32[]{:S(2)}) collective-permute-start(bf16[2,80,384]{2,1,0:T(8,128)(2,1)S(1)} %collective-permute-done.5.refs_2_), channel_id=1, source_target_pairs={{0,2},{2,0},{4,6},{6,4},{8,10},{10,8},{12,14},{14,12},{16,18},{18,... | collective-permute-start | bytes 368648 | tf_op jit(solution)/shard_map/ppermute | solution.py:589
  20.7 1.4 %collective-permute-start.6 = (bf16[80,384]{1,0:T(8,128)(2,1)S(1)}, bf16[80,384]{1,0:T(8,128)(2,1)S(1)}, u32[]{:S(2)}, u32[]{:S(2)}) collective-permute-start(bf16[80,384]{1,0:T(8,128)(2,1)S(1)} %collective-permute-done.2.side_ref), channel_id=1, source_target_pairs={{0,2},{2,0},{4,6},{6,4},{8,10},{10,8},{12,14},{14,12},{16,18},{18,... | collective-permute-start | bytes 184328 | tf_op jit(solution)/shard_map/ppermute | solution.py:589
  22.1 2.7 %copy-start.3 = (f32[2,8,96,96]{3,2,1,0:T(8,128)S(1)}, f32[2,8,96,96]{3,2,1,0:T(8,128)}, u32[]{:S(2)}) copy-start(f32[2,8,96,96]{3,2,1,0:T(8,128)} %win_ref.1) | copy-start | bytes 1769476
  22.1 2.7 %copy-start.4 = (f32[2,8,96,96]{3,2,1,0:T(8,128)S(1)}, f32[2,8,96,96]{3,2,1,0:T(8,128)}, u32[]{:S(2)}) copy-start(f32[2,8,96,96]{3,2,1,0:T(8,128)} %wout_ref.1) | copy-start | bytes 1769476
  22.1 2.7 %copy-start.5 = (bf16[640,80]{1,0:T(8,128)(2,1)S(1)}, bf16[640,80]{1,0:T(8,128)(2,1)}, u32[]{:S(2)}) copy-start(bf16[640,80]{1,0:T(8,128)(2,1)} %constant.39.clone.table_ref) | copy-start | bytes 307204
  22.2 2.7 %copy-start.6 = (f32[2,8,96]{2,1,0:T(8,128)S(1)}, f32[2,8,96]{2,1,0:T(8,128)}, u32[]{:S(2)}) copy-start(f32[2,8,96]{2,1,0:T(8,128)} %bin_ref.1) | copy-start | bytes 18436
  23.3 8.5 %collective-permute-start.10 = (bf16[336,384]{1,0:T(8,128)(2,1)S(1)}, bf16[336,384]{1,0:T(8,128)(2,1)S(1)}, u32[]{:S(2)}, u32[]{:S(2)}) collective-permute-start(bf16[336,384]{1,0:T(8,128)(2,1)S(1)} %shard_map.114.spec_ref), channel_id=1, source_target_pairs={{0,1},{1,0},{2,3},{3,2},{4,5},{5,4},{6,7},{7,6},{8,9},{9,8},{10,11... | collective-permute-start | bytes 774152 | tf_op jit(solution)/shard_map/ppermute | solution.py:596
  31.7 5.6 %copy-start.1 = (bf16[8,2,128,256]{3,2,1,0:T(8,128)(2,1)S(1)}, bf16[8,2,128,256]{3,2,1,0:T(8,128)(2,1)}, u32[]{:S(2)}) copy-start(bf16[8,2,128,256]{3,2,1,0:T(8,128)(2,1)} %constant.40.clone.table_ref) | copy-start | bytes 3145732
  35.5 1.8 %collective-permute-start.11 = (f32[264,384]{1,0:T(8,128)S(1)}, f32[264,384]{1,0:T(8,128)S(1)}, u32[]{:S(2)}, u32[]{:S(2)}) collective-permute-start(f32[264,384]{1,0:T(8,128)S(1)} %shard_map.116.own_ref), channel_id=1, source_target_pairs={{0,2},{2,0},{4,6},{6,4},{8,10},{10,8},{12,14},{14,12},{16,18},{18,... | collective-permute-start | bytes 1216520 | tf_op jit(solution)/shard_map/ppermute | solution.py:589
  38.6 12.7 %collective-permute-start.13 = (bf16[176,384]{1,0:T(8,128)(2,1)S(1)}, bf16[176,384]{1,0:T(8,128)(2,1)S(1)}, u32[]{:S(2)}, u32[]{:S(2)}) collective-permute-start(bf16[176,384]{1,0:T(8,128)(2,1)S(1)} %get-tuple-element.42), channel_id=1, source_target_pairs={{0,24},{2,30},{4,28},{6,26},{8,16},{10,22},{12,20},{14,18},{16,8},... | collective-permute-start | bytes 405512 | tf_op jit(solution)/shard_map/ppermute | solution.py:593
  41.2 11.2 %collective-permute-start.14 = (bf16[176,384]{1,0:T(8,128)(2,1)S(1)}, bf16[176,384]{1,0:T(8,128)(2,1)S(1)}, u32[]{:S(2)}, u32[]{:S(2)}) collective-permute-start(bf16[176,384]{1,0:T(8,128)(2,1)S(1)} %get-tuple-element.47), channel_id=1, source_target_pairs={{0,8},{2,14},{4,12},{6,10},{8,0},{10,6},{12,4},{14,2},{16,24},{18,... | collective-permute-start | bytes 405512 | tf_op jit(solution)/shard_map/ppermute | solution.py:593
  41.2 11.5 %collective-permute-start.15 = (bf16[176,384]{1,0:T(8,128)(2,1)S(1)}, bf16[176,384]{1,0:T(8,128)(2,1)S(1)}, u32[]{:S(2)}, u32[]{:S(2)}) collective-permute-start(bf16[176,384]{1,0:T(8,128)(2,1)S(1)} %get-tuple-element.48), channel_id=1, source_target_pairs={{0,16},{2,22},{4,20},{6,18},{8,24},{10,30},{12,28},{14,26},{16,0},... | collective-permute-start | bytes 405512 | tf_op jit(solution)/shard_map/ppermute | solution.py:593
  43.1 7.4 %collective-permute-start.12 = (bf16[136,384]{1,0:T(8,128)(2,1)S(1)}, bf16[136,384]{1,0:T(8,128)(2,1)S(1)}, u32[]{:S(2)}, u32[]{:S(2)}) collective-permute-start(bf16[136,384]{1,0:T(8,128)(2,1)S(1)} %get-tuple-element.38), channel_id=1, source_target_pairs={{0,4},{2,6},{4,0},{6,2},{8,12},{10,14},{12,8},{14,10},{16,20},{18,... | collective-permute-start | bytes 313352 | tf_op jit(solution)/shard_map/ppermute | solution.py:593
  51.3 3.0 %copy-start.2 = (bf16[10,14,768]{2,1,0:T(8,128)(2,1)S(1)}, bf16[10,14,768]{2,1,0:T(8,128)(2,1)}, u32[]{:S(2)}) copy-start(bf16[10,14,768]{2,1,0:T(8,128)(2,1)} %refs_6_.1) | copy-start | bytes 645124
  52.4 1.9 %collective-permute-start.17 = (bf16[176,384]{1,0:T(8,128)(2,1)S(1)}, bf16[176,384]{1,0:T(8,128)(2,1)S(1)}, u32[]{:S(2)}, u32[]{:S(2)}) collective-permute-start(bf16[176,384]{1,0:T(8,128)(2,1)S(1)} %collective-permute-done.14.refs_1_), channel_id=1, source_target_pairs={{0,2},{2,0},{4,6},{6,4},{8,10},{10,8},{12,14},{14,12},{16,18},{18,... | collective-permute-start | bytes 405512 | tf_op jit(solution)/shard_map/ppermute | solution.py:589
  52.7 1.6 %collective-permute-start.18 = (bf16[176,384]{1,0:T(8,128)(2,1)S(1)}, bf16[176,384]{1,0:T(8,128)(2,1)S(1)}, u32[]{:S(2)}, u32[]{:S(2)}) collective-permute-start(bf16[176,384]{1,0:T(8,128)(2,1)S(1)} %collective-permute-done.15.refs_2_), channel_id=1, source_target_pairs={{0,2},{2,0},{4,6},{6,4},{8,10},{10,8},{12,14},{14,12},{16,18},{18,... | collective-permute-start | bytes 405512 | tf_op jit(solution)/shard_map/ppermute | solution.py:589
  52.9 1.4 %collective-permute-start.16 = (bf16[176,384]{1,0:T(8,128)(2,1)S(1)}, bf16[176,384]{1,0:T(8,128)(2,1)S(1)}, u32[]{:S(2)}, u32[]{:S(2)}) collective-permute-start(bf16[176,384]{1,0:T(8,128)(2,1)S(1)} %collective-permute-done.13.refs_0_), channel_id=1, source_target_pairs={{0,2},{2,0},{4,6},{6,4},{8,10},{10,8},{12,14},{14,12},{16,18},{18,... | collective-permute-start | bytes 405512 | tf_op jit(solution)/shard_map/ppermute | solution.py:589
